TPU v7x, 32 devices: a whole 2x2x4 slice. The times are simulated.
32 devices in a mesh: tunnel: 16 (over z, x, core), group: 2 (over y).
Axes of the slice: x: 2, y: 2, z: 4, core: 2. Of those that a mesh axis runs over, the one named last changes fastest.
Arguments:
- velocity: float32 [3, 64, 512, 256], P(None, ('tunnel', 'group')), may hold values from -6 to 6
- obstacle: int32 [64, 512, 256], P(('tunnel', 'group')), may hold values 0 or 1
- pressure: float32 [64, 512, 256], P('tunnel', 'group'), may hold values from -6 to 6
Outputs:
- corrected: float32 [3, 64, 512, 256], P(None, ('tunnel', 'group'))
- potential: float32 [64, 512, 256], P('tunnel', 'group')
All inputs are finite; a program needn't handle non-finite values. No bound on the sum of `obstacle` on one device may be relied on, other than what follows from the above.
Results may differ from a plain program's by a relative error of at most 0.00018.
Values sent between devices are 32-bit elements; how exact they have to be, the bound alone decides.
No kernel may reach another device: no remote copies, remote signals or barrier semaphores. Data moves between devices by JAX's collectives and lax.ppermute only.
A program may use at most 256 MiB of HBM per device.

v0:
```python
import math

import jax
import jax.numpy as jnp
from jax import lax
from jax.sharding import PartitionSpec as P

LEVELS = 3
SWEEPS = 2
COARSE_SWEEPS = 4


time_step = 0.1
viscosity = 0.05
relax_weight = 0.8
highest = lax.Precision.HIGHEST


def extended(value, sides, width):
    for axis, dim in sides:
        size, length = (lax.axis_size(axis), value.shape[dim])
        up = [(i, (i + 1) % size) for i in range(size)]
        down = [(j, i) for i, j in up]
        last = lax.slice_in_dim(value, length - width, length, axis=dim)
        initial = lax.slice_in_dim(value, 0, width, axis=dim)
        before = lax.ppermute(last, axis, up)
        after = lax.ppermute(initial, axis, down)
        value = jnp.concatenate([before, value, after], axis=dim)
    return value


def compact_tables(count):
    indices = jnp.arange(count, dtype=jnp.int32)
    product = indices[:, None] * indices[None, :] % count
    angles = product.astype(jnp.float32) * (2.0 * math.pi / count)
    cosines = jnp.cos(angles)
    sines = jnp.sin(angles)
    theta = indices.astype(jnp.float32) * (2.0 * math.pi / count)
    first_wave = (14.0 / 9.0 * jnp.sin(theta) + jnp.sin(2.0 * theta) / 18.0) / (
        1.0 + 2.0 / 3.0 * jnp.cos(theta)
    )
    second_wave = (
        24.0 / 11.0 * (1.0 - jnp.cos(theta)) + 3.0 / 22.0 * (1.0 - jnp.cos(2.0 * theta))
    ) / (1.0 + 4.0 / 11.0 * jnp.cos(theta))
    first_matrix = (
        jnp.dot(cosines * first_wave, sines.T, precision=highest)
        - jnp.dot(sines * first_wave, cosines.T, precision=highest)
    ) / count
    second_matrix = (
        -(
            jnp.dot(cosines * second_wave, cosines.T, precision=highest)
            + jnp.dot(sines * second_wave, sines.T, precision=highest)
        )
        / count
    )
    return (first_matrix, second_matrix)


def along_rows(matrix, field):
    return jnp.einsum("ij,...jz->...iz", matrix, field, precision=highest)


def along_depth(matrix, field):
    return jnp.einsum("...j,ij->...i", field, matrix, precision=highest)


def shifted(padded, offset, axis):
    count = padded.shape[axis] - 4
    return lax.slice_in_dim(padded, 2 + offset, 2 + offset + count, axis=axis)


def stream_first(padded, axis):
    ahead = shifted(padded, 1, axis) - shifted(padded, -1, axis)
    further = shifted(padded, 2, axis) - shifted(padded, -2, axis)
    return (8.0 * ahead - further) / 12.0


def stream_second(padded, axis):
    ahead = shifted(padded, 1, axis) + shifted(padded, -1, axis)
    further = shifted(padded, 2, axis) + shifted(padded, -2, axis)
    return (16.0 * ahead - further - 30.0 * shifted(padded, 0, axis)) / 12.0


def padded_neighbours(padded):
    interior = padded[1:-1, 1:-1]
    total = padded[2:, 1:-1] + padded[:-2, 1:-1]
    total = total + padded[1:-1, 2:] + padded[1:-1, :-2]
    return total + jnp.roll(interior, -1, 2) + jnp.roll(interior, 1, 2)


def relax_padded(padded, source_term, scale):
    interior = padded[1:-1, 1:-1]
    return interior + relax_weight / 6.0 * (
        padded_neighbours(padded) - 6.0 * interior - scale * source_term
    )


def faces(field):
    return extended(field, (("tunnel", 0), ("group", 1)), 1)


def thin_sweeps(field, source_term, scale, count):
    for sweep_index in range(count):
        field = relax_padded(faces(field), source_term, scale)
    return field


def smooth(field, source_term, scale, level):
    if level == 0:
        return thin_sweeps(field, source_term, scale, SWEEPS)
    return thin_sweeps(field, source_term, scale, SWEEPS)


def coarsest(source_term, scale):
    return thin_sweeps(jnp.zeros_like(source_term), source_term, scale, COARSE_SWEEPS)


def restrict(field):
    planes, rows, depth = field.shape
    blocks = field.reshape(planes // 2, 2, rows // 2, 2, depth // 2, 2)
    return jnp.sum(blocks, axis=(1, 3, 5)) * 0.125


def prolong(field):
    return jnp.repeat(jnp.repeat(jnp.repeat(field, 2, 0), 2, 1), 2, 2)


def cycle(field, source_term, level):
    scale = 4.0**level
    if level == LEVELS - 1:
        return coarsest(source_term, scale)
    field = smooth(field, source_term, scale, level)
    leftover = source_term - (padded_neighbours(faces(field)) - 6.0 * field) / scale
    coarse_source = restrict(leftover)
    coarse = cycle(jnp.zeros_like(coarse_source), coarse_source, level + 1)
    field = field + prolong(coarse)
    return smooth(field, source_term, scale, level)


def local(velocity, obstacle, pressure):
    row_count = velocity.shape[2]
    depth_count = velocity.shape[3]
    rows_first, rows_second = compact_tables(row_count)
    depth_first, depth_second = compact_tables(depth_count)
    rows_both = jnp.concatenate([rows_first, rows_second], axis=0)
    depth_both = jnp.concatenate([depth_first, depth_second], axis=0)
    keep = 1.0 - obstacle.astype(jnp.float32)
    row_terms = along_rows(rows_both, velocity)
    depth_terms = along_depth(depth_both, velocity)
    transverse = (
        velocity[1] * row_terms[:, :, :row_count] + velocity[2] * depth_terms[..., :depth_count]
    )
    diffusion = row_terms[:, :, row_count:] + depth_terms[..., depth_count:]
    padded = extended(velocity, ((("tunnel", "group"), 1),), 2)
    streamwise = -velocity[0] * stream_first(padded, 1) + viscosity * stream_second(padded, 1)
    tendency = streamwise - transverse + viscosity * diffusion
    star = (velocity + time_step * tendency) * keep
    star_padded = extended(star[0], ((("tunnel", "group"), 0),), 2)
    source = (
        stream_first(star_padded, 0)
        + along_rows(rows_first, star[1])
        + along_depth(depth_first, star[2])
    )
    source_tile = lax.all_to_all(source, "group", split_axis=1, concat_axis=0, tiled=True)
    potential = cycle(pressure, source_tile, 0)
    potential_padded = extended(potential, (("tunnel", 0),), 2)
    streamwise_grad = stream_first(potential_padded, 0)
    returned = lax.all_to_all(
        jnp.stack([potential, streamwise_grad]), "group", split_axis=1, concat_axis=2, tiled=True
    )
    gradient = jnp.stack(
        [returned[1], along_rows(rows_first, returned[0]), along_depth(depth_first, returned[0])]
    )
    corrected = (star - gradient) * keep
    return (corrected, potential)


def solution(mesh):
    in_specs = (
        P(None, ("tunnel", "group"), None, None),
        P(("tunnel", "group"), None, None),
        P("tunnel", "group", None),
    )
    out_specs = (P(None, ("tunnel", "group"), None, None), P("tunnel", "group", None))
    return jax.shard_map(local, mesh=mesh, in_specs=in_specs, out_specs=out_specs, check_vma=False)
```

profile of v0, /device:TPU:0, one launch (start us, length us, event | category | flops | bytes accessed | tf_op | source)
XLA Modules:
  0.0 580.1 jit_solution(15659955018039243905)
XLA Ops:
  0.6 6.4 %collective-permute-start = (f32[3,2,512,256]{3,2,1,0:T(8,128)}, f32[3,2,512,256]{3,2,1,0:T(8,128)S(1)}, u32[]{:S(2)}, u32[]{:S(2)}) collective-permute-start(f32[3,2,512,256]{3,2,1,0:T(8,128)} %param.3), channel_id=1, source_target_pairs={{1,0},{2,1},{3,2},{4,3},{5,4},{6,5},{7,6},{8,7},{9,8},{10,9},{11,1... | collective-permute-start | bytes 9437192 | tf_op jit(solution)/shard_map/ppermute | solution.py:27
  8.6 4.4 collective-permute-start.12
  20.3 6.2 %fusion.91 = f32[512,512]{1,0:T(8,128)S(1)} fusion(f32[512]{0:T(512)S(1)} %add_divide_fusion.1), kind=kOutput, calls=%fused_computation.163 | convolution fusion | flops 1618214912 | bytes 1050624 | tf_op jit(solution)/shard_map/dot_general | solution.py:46
  26.5 5.7 fusion.10
  32.3 6.3 %fusion.20 = f32[512,512]{1,0:T(8,128)S(1)} fusion(f32[512,512]{1,0:T(8,128)S(1)} %fusion.91, f32[512]{0:T(512)S(1)} %add_divide_fusion.1), kind=kOutput, calls=%fused_computation.42 | convolution fusion | flops 1618739200 | bytes 2099200 | tf_op jit(solution)/shard_map/dot_general | solution.py:47
  38.6 5.7 fusion.21
  44.3 11.2 %convolution_bitcast_fusion = f32[3,2,1024,256]{3,2,1,0:T(8,128)S(1)} fusion(f32[3,2,512,256]{3,2,1,0:T(8,128)S(1)} %copy-done, f32[512,512]{1,0:T(8,128)S(1)} %fusion.21, f32[512,512]{1,0:T(8,128)S(1)} %fusion.20), kind=kOutput, calls=%fused_computation.14 | convolution fusion | flops 9664200704 | bytes 11534336 | tf_op jit(solution)/shard_map/ij,...jz->...iz/dot_general | solution.py:60
  55.5 7.1 %convolution_bitcast_fusion.1 = f32[3,2,512,512]{3,2,1,0:T(8,128)} fusion(f32[3,2,512,256]{3,2,1,0:T(8,128)S(1)} %copy-done, f32[256,256]{1,0:T(8,128)S(1)} %fusion.25, f32[256,256]{1,0:T(8,128)S(1)} %fusion.26), kind=kOutput, calls=%fused_computation.15 | convolution fusion | flops 4831969280 | bytes 9961472 | tf_op jit(solution)/shard_map/...j,ij->...i/dot_general | solution.py:64
  62.6 43.1 %collective-permute-done = f32[3,2,512,256]{3,2,1,0:T(8,128)S(1)} collective-permute-done((f32[3,2,512,256]{3,2,1,0:T(8,128)}, f32[3,2,512,256]{3,2,1,0:T(8,128)S(1)}, u32[]{:S(2)}, u32[]{:S(2)}) %collective-permute-start) | collective-permute-done | bytes 3145760 | tf_op jit(solution)/shard_map/ppermute | solution.py:27
  108.4 7.6 %fusion.4 = f32[3,2,512,256]{3,2,1,0:T(8,128)S(1)} fusion(f32[3,2,512,256]{3,2,1,0:T(8,128)S(1)} %copy-done, f32[3,2,512,512]{3,2,1,0:T(8,128)} %convolution_bitcast_fusion.1, f32[3,2,1024,256]{3,2,1,0:T(8,128)S(1)} %convolution_bitcast_fusion, f32[3,2,512,256]{3,2,1,0:T(8,128)} %copy-done.8, f32[3,2,512,256]{3,2,1,0:T(8,128)} %copy-done.9, ...), kind=kLoop, calls=%fused_computation.5 | loop fusion | flops 19660800 | bytes 29360128 | tf_op jit(solution)/shard_map/mul | solution.py:157
  117.2 38.4 %collective-permute-start.6 = (f32[2,512,256]{2,1,0:T(8,128)}, f32[2,512,256]{2,1,0:T(8,128)}, u32[]{:S(2)}, u32[]{:S(2)}) collective-permute-start(f32[2,512,256]{2,1,0:T(8,128)} %slice_bitcast_fusion.4), channel_id=1, source_target_pairs={{1,0},{2,1},{3,2},{4,3},{5,4},{6,5},{7,6},{8,7},{9,8},{10,9},{11,1... | collective-permute-start | bytes 3145736 | tf_op jit(solution)/shard_map/ppermute | solution.py:27
  155.5 1.8 fusion.266
  157.4 2.5 copy.77
  159.9 3.2 fusion.265
  163.8 1.8 copy.59
  165.6 1.8 copy.61
  168.6 4.4 collective-permute-start.2
  173.6 3.1 convolution_bitcast_fusion.4
  176.7 6.5 %collective-permute-done.6 = f32[2,512,256]{2,1,0:T(8,128)} collective-permute-done((f32[2,512,256]{2,1,0:T(8,128)}, f32[2,512,256]{2,1,0:T(8,128)}, u32[]{:S(2)}, u32[]{:S(2)}) %collective-permute-start.6) | collective-permute-done | bytes 1048608 | tf_op jit(solution)/shard_map/ppermute | solution.py:27
  183.2 3.7 collective-permute-start.3
  187.7 8.1 %collective-permute-start.26 = (f32[3,1,64]{2,1,0:T(1,128)}, f32[3,1,64]{2,1,0:T(1,128)}, u32[]{:S(2)}, u32[]{:S(2)}) collective-permute-start(f32[3,1,64]{2,1,0:T(1,128)} %get-tuple-element.97), channel_id=1, source_target_pairs={{1,0},{0,1},{3,2},{2,3},{5,4},{4,5},{7,6},{6,7},{9,8},{8,9},{11,10... | collective-permute-start | bytes 2312 | tf_op jit(solution)/shard_map/ppermute | solution.py:27
  195.8 3.4 fusion.78
  199.3 1.8 copy.75
  201.1 3.6 all-to-all-start
  204.7 2.0 collective-permute-start.27
  212.2 1.9 collective-permute-start.5
  215.5 3.7 collective-permute-done.4
  219.2 2.0 copy.65
  224.6 7.4 %fusion.85 = f32[4,256,256]{1,0,2:T(4,128)S(1)} fusion(f32[4,256,256]{1,0,2:T(4,128)S(1)} %copy-done.3, f32[4,256,256]{1,0,2:T(4,128)S(1)} %all_to_all.27, f32[6,1,256]{1,0,2:T(8,128)} %copy.67, f32[1,256,256]{1,0,2:T(1,128)} %collective-permute-done.2, f32[1,256,256]{1,0,2:T(1,128)} %collective-permute-done.3, f32[6,1,256]{1,0,2:T(8,128)} %copy.65, ...), kind=kLoop, calls=%fused_computation.147 | loop fusion | flops 5242880 | bytes 5779456 | tf_op jit(solution)/shard_map/add | solution.py:93
  232.4 5.0 collective-permute-start.8
  239.0 2.3 collective-permute-done.8
  241.3 4.6 collective-permute-done.9
  251.0 2.0 collective-permute-start.11
  253.8 2.0 copy.79
  257.2 7.3 %fusion.69 = f32[4,256,256]{1,0,2:T(4,128)S(1)} fusion(f32[4,256,256]{1,0,2:T(4,128)S(1)} %fusion.85, f32[4,256,256]{1,0,2:T(4,128)S(1)} %all_to_all.27, f32[6,1,256]{1,0,2:T(8,128)} %copy.81, f32[1,256,256]{1,0,2:T(1,128)} %copy-done.12, f32[1,256,256]{1,0,2:T(1,128)} %copy-done.16, f32[6,1,256]{1,0,2:T(8,128)} %copy.79, ...), kind=kLoop, calls=%fused_computation.118 | loop fusion | flops 5242880 | bytes 5779456 | tf_op jit(solution)/shard_map/add | solution.py:93
  268.9 5.1 collective-permute-done.17
  276.7 2.1 copy.82
  284.6 2.0 copy.85
  286.6 8.0 %fusion.60 = f32[4,256,256]{1,0,2:T(4,128)} fusion(f32[4,256,256]{1,0,2:T(4,128)S(1)} %all_to_all.27, f32[6,1,256]{1,0,2:T(8,128)} %copy.85, f32[1,256,256]{1,0,2:T(1,128)} %copy-done.10, f32[4,256,256]{1,0,2:T(4,128)S(1)} %fusion.69, f32[1,256,256]{1,0,2:T(1,128)} %copy-done.13, f32[6,1,256]{1,0,2:T(8,128)S(1)} %copy.83, ...), kind=kLoop, calls=%fused_computation.101 | loop fusion | flops 4718592 | bytes 5779456 | tf_op jit(solution)/shard_map/sub | solution.py:133
  296.2 68.4 %reshape.95 = f32[2,2,128,2,128,2]{5,4,3,2,1,0:T(8,128)} reshape(f32[4,256,256]{2,1,0:T(8,128)S(1)} %copy.86) | data formatting | bytes 2097152 | tf_op jit(solution)/shard_map/reshape | solution.py:120
  364.6 20.8 %reduce_sum.21 = f32[2,128,128]{2,1,0:T(8,128)S(1)} reduce(f32[2,2,128,2,128,2]{5,4,3,2,1,0:T(8,128)} %reshape.95, f32[]{:T(128)} %constant.122.clone.1), dimensions={1,3,5}, to_apply=%region_0.1 | reduce | flops 229376 | bytes 1179652 | tf_op jit(solution)/shard_map/reduce_sum | solution.py:121
  388.3 4.5 collective-permute-done.21
  399.6 4.5 collective-permute-done.29
  408.9 5.5 reduce_sum.27
  414.4 2.8 reduce_sum.28
  419.6 4.5 collective-permute-done.33
  431.1 4.5 collective-permute-done.37
  441.9 4.7 collective-permute-done.41
  453.6 4.5 collective-permute-done.45
  464.8 4.5 collective-permute-done.49
  479.2 1.8 collective-permute-done.52
  481.0 4.7 collective-permute-done.53
  496.2 7.3 %fusion.53 = f32[4,256,256]{1,0,2:T(4,128)S(1)} fusion(f32[4,256,256]{1,0,2:T(4,128)S(1)} %bitcast_add_fusion, f32[4,256,256]{1,0,2:T(4,128)S(1)} %all_to_all.27, f32[6,1,256]{1,0,2:T(8,128)} %copy.93, f32[1,256,256]{1,0,2:T(1,128)} %copy-done.14, f32[1,256,256]{1,0,2:T(1,128)} %copy-done.17, f32[6,1,256]{1,0,2:T(8,128)} %copy.91, ...), kind=kLoop, calls=%fused_computation.86 | loop fusion | flops 5242880 | bytes 5779456 | tf_op jit(solution)/shard_map/add | solution.py:93
  507.9 4.9 collective-permute-done.57
  523.3 7.3 %fusion.44 = f32[4,256,256]{1,0,2:T(4,128)S(1)} fusion(f32[4,256,256]{1,0,2:T(4,128)S(1)} %fusion.53, f32[4,256,256]{1,0,2:T(4,128)S(1)} %all_to_all.27, f32[6,1,256]{1,0,2:T(8,128)} %copy.97, f32[1,256,256]{1,0,2:T(1,128)} %copy-done.11, f32[1,256,256]{1,0,2:T(1,128)} %copy-done.15, f32[6,1,256]{1,0,2:T(8,128)} %copy.95, ...), kind=kLoop, calls=%fused_computation.69 | loop fusion | flops 5242880 | bytes 5779456 | tf_op jit(solution)/shard_map/add | solution.py:93
  531.6 6.2 %collective-permute-done.60 = f32[2,256,256]{1,0,2:T(2,128)S(1)} collective-permute-done((f32[2,256,256]{1,0,2:T(2,128)S(1)}, f32[2,256,256]{1,0,2:T(2,128)S(1)}, u32[]{:S(2)}, u32[]{:S(2)}) %collective-permute-start.60) | collective-permute-done | bytes 524320 | tf_op jit(solution)/shard_map/ppermute | solution.py:27
  537.8 4.7 collective-permute-done.61
  542.5 1.9 fusion.35
  546.5 4.0 all-to-all-start.1
  551.9 19.1 %all-to-all-done.1 = f32[2,4,256,256]{2,3,0,1:T(8,128)S(1)} async-done(((f32[2,4,256,256]{2,3,0,1:T(8,128)}), f32[2,4,256,256]{2,3,0,1:T(8,128)S(1)}, u32[]{:S(2)}, u32[]{:S(2)}) %all-to-all-start.1) | async-done | bytes 2097184 | tf_op jit(solution)/shard_map/all_to_all | solution.py:168
  571.0 1.8 copy.99
  572.9 1.8 fusion.245
  574.7 1.9 convolution_bitcast_fusion.3
  577.7 2.1 fusion.7
  (261 shorter events, 134.1 us)
Async XLA Ops:
  0.6 105.0 %collective-permute-start = (f32[3,2,512,256]{3,2,1,0:T(8,128)}, f32[3,2,512,256]{3,2,1,0:T(8,128)S(1)}, u32[]{:S(2)}, u32[]{:S(2)}) collective-permute-start(f32[3,2,512,256]{3,2,1,0:T(8,128)} %param.3), channel_id=1, source_target_pairs={{1,0},{2,1},{3,2},{4,3},{5,4},{6,5},{7,6},{8,7},{9,8},{10,9},{11,1... | collective-permute-start | bytes 9437192 | tf_op jit(solution)/shard_map/ppermute | solution.py:27
  7.1 99.6 %collective-permute-start.1 = (f32[3,2,512,256]{3,2,1,0:T(8,128)}, f32[3,2,512,256]{3,2,1,0:T(8,128)S(1)}, u32[]{:S(2)}, u32[]{:S(2)}) collective-permute-start(f32[3,2,512,256]{3,2,1,0:T(8,128)} %param.3), channel_id=1, source_target_pairs={{0,1},{1,2},{2,3},{3,4},{4,5},{5,6},{6,7},{7,8},{8,9},{9,10},{10,1... | collective-permute-start | bytes 9437192 | tf_op jit(solution)/shard_map/ppermute | solution.py:26
  7.1 161.5 %collective-permute-start.24 = (f32[1,64,64]{2,1,0:T(8,128)S(1)}, f32[1,64,64]{2,1,0:T(8,128)S(1)}, u32[]{:S(2)}, u32[]{:S(2)}) collective-permute-start(f32[1,64,64]{2,1,0:T(8,128)S(1)} %broadcast_in_dim.21), channel_id=1, source_target_pairs={{2,0},{4,2},{6,4},{8,6},{10,8},{12,10},{14,12},{16,14},{18,16},{20... | collective-permute-start | bytes 49160 | tf_op jit(solution)/shard_map/ppermute | solution.py:27
  8.0 160.6 %collective-permute-start.25 = (f32[1,64,64]{2,1,0:T(8,128)S(1)}, f32[1,64,64]{2,1,0:T(8,128)S(1)}, u32[]{:S(2)}, u32[]{:S(2)}) collective-permute-start(f32[1,64,64]{2,1,0:T(8,128)S(1)} %broadcast_in_dim.21), channel_id=1, source_target_pairs={{0,2},{2,4},{4,6},{6,8},{8,10},{10,12},{12,14},{14,16},{16,18},{18... | collective-permute-start | bytes 49160 | tf_op jit(solution)/shard_map/ppermute | solution.py:26
  8.6 203.6 %collective-permute-start.12 = (f32[1,128,128]{2,1,0:T(8,128)}, f32[1,128,128]{2,1,0:T(8,128)}, u32[]{:S(2)}, u32[]{:S(2)}) collective-permute-start(f32[1,128,128]{2,1,0:T(8,128)} %broadcast.237), channel_id=1, source_target_pairs={{2,0},{4,2},{6,4},{8,6},{10,8},{12,10},{14,12},{16,14},{18,16},{20... | collective-permute-start | bytes 196616 | tf_op jit(solution)/shard_map/ppermute | solution.py:27
  117.2 66.0 %collective-permute-start.6 = (f32[2,512,256]{2,1,0:T(8,128)}, f32[2,512,256]{2,1,0:T(8,128)}, u32[]{:S(2)}, u32[]{:S(2)}) collective-permute-start(f32[2,512,256]{2,1,0:T(8,128)} %slice_bitcast_fusion.4), channel_id=1, source_target_pairs={{1,0},{2,1},{3,2},{4,3},{5,4},{6,5},{7,6},{8,7},{9,8},{10,9},{11,1... | collective-permute-start | bytes 3145736 | tf_op jit(solution)/shard_map/ppermute | solution.py:27
  155.5 32.2 %collective-permute-start.7 = (f32[2,512,256]{2,1,0:T(8,128)}, f32[2,512,256]{2,1,0:T(8,128)}, u32[]{:S(2)}, u32[]{:S(2)}) collective-permute-start(f32[2,512,256]{2,1,0:T(8,128)} %slice_bitcast_fusion.4), channel_id=1, source_target_pairs={{0,1},{1,2},{2,3},{3,4},{4,5},{5,6},{6,7},{7,8},{8,9},{9,10},{10,1... | collective-permute-start | bytes 3145736 | tf_op jit(solution)/shard_map/ppermute | solution.py:26
  168.6 45.5 %collective-permute-start.13 = (f32[1,128,128]{2,1,0:T(8,128)}, f32[1,128,128]{2,1,0:T(8,128)}, u32[]{:S(2)}, u32[]{:S(2)}) collective-permute-start(f32[1,128,128]{2,1,0:T(8,128)} %broadcast.237), channel_id=1, source_target_pairs={{0,2},{2,4},{4,6},{6,8},{8,10},{10,12},{12,14},{14,16},{16,18},{18... | collective-permute-start | bytes 196616 | tf_op jit(solution)/shard_map/ppermute | solution.py:26
  168.6 36.1 %collective-permute-start.2 = (f32[1,256,256]{1,0,2:T(1,128)}, f32[1,256,256]{1,0,2:T(1,128)}, u32[]{:S(2)}, u32[]{:S(2)}) collective-permute-start(f32[1,256,256]{1,0,2:T(1,128)} %copy.59), channel_id=1, source_target_pairs={{2,0},{4,2},{6,4},{8,6},{10,8},{12,10},{14,12},{16,14},{18,16},{20... | collective-permute-start | bytes 786440 | tf_op jit(solution)/shard_map/ppermute | solution.py:27
  183.2 23.5 %collective-permute-start.3 = (f32[1,256,256]{1,0,2:T(1,128)}, f32[1,256,256]{1,0,2:T(1,128)}, u32[]{:S(2)}, u32[]{:S(2)}) collective-permute-start(f32[1,256,256]{1,0,2:T(1,128)} %copy.61), channel_id=1, source_target_pairs={{0,2},{2,4},{4,6},{6,8},{8,10},{10,12},{12,14},{14,16},{16,18},{18... | collective-permute-start | bytes 786440 | tf_op jit(solution)/shard_map/ppermute | solution.py:26
  187.7 229.5 %collective-permute-start.26 = (f32[3,1,64]{2,1,0:T(1,128)}, f32[3,1,64]{2,1,0:T(1,128)}, u32[]{:S(2)}, u32[]{:S(2)}) collective-permute-start(f32[3,1,64]{2,1,0:T(1,128)} %get-tuple-element.97), channel_id=1, source_target_pairs={{1,0},{0,1},{3,2},{2,3},{5,4},{4,5},{7,6},{6,7},{9,8},{8,9},{11,10... | collective-permute-start | bytes 2312 | tf_op jit(solution)/shard_map/ppermute | solution.py:27
  201.1 21.5 %all-to-all-start = ((f32[2,512,256]{2,0,1:T(2,128)}), f32[2,512,256]{2,0,1:T(2,128)S(1)}, u32[]{:S(2)}, u32[]{:S(2)}) async-start(f32[2,512,256]{2,0,1:T(2,128)} %copy.75), calls=%async_computation | async-start | bytes 2097152 | tf_op jit(solution)/shard_map/all_to_all | solution.py:164
  204.7 212.6 %collective-permute-start.27 = (f32[3,1,64]{2,1,0:T(1,128)}, f32[3,1,64]{2,1,0:T(1,128)}, u32[]{:S(2)}, u32[]{:S(2)}) collective-permute-start(f32[3,1,64]{2,1,0:T(1,128)} %get-tuple-element.98), channel_id=1, source_target_pairs={{0,1},{1,0},{2,3},{3,2},{4,5},{5,4},{6,7},{7,6},{8,9},{9,8},{10,11... | collective-permute-start | bytes 2312 | tf_op jit(solution)/shard_map/ppermute | solution.py:26
  211.1 8.1 %collective-permute-start.4 = (f32[6,1,256]{2,1,0:T(1,128)S(1)}, f32[6,1,256]{2,1,0:T(1,128)}, u32[]{:S(2)}, u32[]{:S(2)}) collective-permute-start(f32[6,1,256]{2,1,0:T(1,128)S(1)} %copy.64), channel_id=1, source_target_pairs={{1,0},{0,1},{3,2},{2,3},{5,4},{4,5},{7,6},{6,7},{9,8},{8,9},{11,10... | collective-permute-start | bytes 18440 | tf_op jit(solution)/shard_map/ppermute | solution.py:27
  212.2 9.1 %collective-permute-start.5 = (f32[6,1,256]{2,1,0:T(1,128)}, f32[6,1,256]{2,1,0:T(1,128)S(1)}, u32[]{:S(2)}, u32[]{:S(2)}) collective-permute-start(f32[6,1,256]{2,1,0:T(1,128)} %copy.66), channel_id=1, source_target_pairs={{0,1},{1,0},{2,3},{3,2},{4,5},{5,4},{6,7},{7,6},{8,9},{9,8},{10,11... | collective-permute-start | bytes 18440 | tf_op jit(solution)/shard_map/ppermute | solution.py:26
  215.4 169.9 %collective-permute-start.14 = (f32[4,1,128]{2,1,0:T(1,128)}, f32[4,1,128]{2,1,0:T(1,128)}, u32[]{:S(2)}, u32[]{:S(2)}) collective-permute-start(f32[4,1,128]{2,1,0:T(1,128)} %get-tuple-element.65), channel_id=1, source_target_pairs={{1,0},{0,1},{3,2},{2,3},{5,4},{4,5},{7,6},{6,7},{9,8},{8,9},{11,10... | collective-permute-start | bytes 6152 | tf_op jit(solution)/shard_map/ppermute | solution.py:27
  232.4 8.9 %collective-permute-start.8 = (f32[1,256,256]{1,0,2:T(1,128)S(1)}, f32[1,256,256]{1,0,2:T(1,128)S(1)}, u32[]{:S(2)}, u32[]{:S(2)}) collective-permute-start(f32[1,256,256]{1,0,2:T(1,128)S(1)} %get-tuple-element.50), channel_id=1, source_target_pairs={{2,0},{4,2},{6,4},{8,6},{10,8},{12,10},{14,12},{16,14},{18,16},{20... | collective-permute-start | bytes 786440 | tf_op jit(solution)/shard_map/ppermute | solution.py:27
  237.4 8.5 %collective-permute-start.9 = (f32[1,256,256]{1,0,2:T(1,128)S(1)}, f32[1,256,256]{1,0,2:T(1,128)S(1)}, u32[]{:S(2)}, u32[]{:S(2)}) collective-permute-start(f32[1,256,256]{1,0,2:T(1,128)S(1)} %get-tuple-element.49), channel_id=1, source_target_pairs={{0,2},{2,4},{4,6},{6,8},{8,10},{10,12},{12,14},{14,16},{16,18},{18... | collective-permute-start | bytes 786440 | tf_op jit(solution)/shard_map/ppermute | solution.py:26
  250.0 3.8 collective-permute-start.10
  251.0 4.9 collective-permute-start.11
  265.0 3.9 collective-permute-start.16
  265.0 9.0 %collective-permute-start.17 = (f32[1,256,256]{1,0,2:T(1,128)S(1)}, f32[1,256,256]{1,0,2:T(1,128)S(1)}, u32[]{:S(2)}, u32[]{:S(2)}) collective-permute-start(f32[1,256,256]{1,0,2:T(1,128)S(1)} %get-tuple-element.43), channel_id=1, source_target_pairs={{0,2},{2,4},{4,6},{6,8},{8,10},{10,12},{12,14},{14,16},{16,18},{18... | collective-permute-start | bytes 786440 | tf_op jit(solution)/shard_map/ppermute | solution.py:26
  278.7 3.8 collective-permute-start.18
  280.6 3.9 collective-permute-start.19
  282.6 102.8 %collective-permute-start.15 = (f32[4,1,128]{2,1,0:T(1,128)}, f32[4,1,128]{2,1,0:T(1,128)}, u32[]{:S(2)}, u32[]{:S(2)}) collective-permute-start(f32[4,1,128]{2,1,0:T(1,128)} %get-tuple-element.66), channel_id=1, source_target_pairs={{0,1},{1,0},{2,3},{3,2},{4,5},{5,4},{6,7},{7,6},{8,9},{9,8},{10,11... | collective-permute-start | bytes 6152 | tf_op jit(solution)/shard_map/ppermute | solution.py:26
  386.3 2.0 collective-permute-start.20
  386.4 6.4 %collective-permute-start.21 = (f32[1,128,128]{2,1,0:T(8,128)S(1)}, f32[1,128,128]{2,1,0:T(8,128)S(1)}, u32[]{:S(2)}, u32[]{:S(2)}) collective-permute-start(f32[1,128,128]{2,1,0:T(8,128)S(1)} %get-tuple-element.89), channel_id=1, source_target_pairs={{0,2},{2,4},{4,6},{6,8},{8,10},{10,12},{12,14},{14,16},{16,18},{18... | collective-permute-start | bytes 196616 | tf_op jit(solution)/shard_map/ppermute | solution.py:26
  392.9 3.6 collective-permute-start.22
  393.9 3.6 collective-permute-start.23
  397.6 2.0 collective-permute-start.28
  397.7 6.4 %collective-permute-start.29 = (f32[1,128,128]{2,1,0:T(8,128)S(1)}, f32[1,128,128]{2,1,0:T(8,128)S(1)}, u32[]{:S(2)}, u32[]{:S(2)}) collective-permute-start(f32[1,128,128]{2,1,0:T(8,128)S(1)} %get-tuple-element.83), channel_id=1, source_target_pairs={{0,2},{2,4},{4,6},{6,8},{8,10},{10,12},{12,14},{14,16},{16,18},{18... | collective-permute-start | bytes 196616 | tf_op jit(solution)/shard_map/ppermute | solution.py:26
  404.2 3.6 collective-permute-start.30
  405.2 3.6 collective-permute-start.31
  418.0 1.7 collective-permute-start.32
  418.0 6.1 %collective-permute-start.33 = (f32[1,64,64]{2,1,0:T(8,128)S(1)}, f32[1,64,64]{2,1,0:T(8,128)S(1)}, u32[]{:S(2)}, u32[]{:S(2)}) collective-permute-start(f32[1,64,64]{2,1,0:T(8,128)S(1)} %broadcast_multiply_fusion.1), channel_id=1, source_target_pairs={{0,2},{2,4},{4,6},{6,8},{8,10},{10,12},{12,14},{14,16},{16,18},{18... | collective-permute-start | bytes 49160 | tf_op jit(solution)/shard_map/ppermute | solution.py:26
  424.1 3.6 collective-permute-start.34
  425.2 3.6 collective-permute-start.35
  429.4 1.7 collective-permute-start.36
  429.5 6.1 %collective-permute-start.37 = (f32[1,64,64]{2,1,0:T(8,128)S(1)}, f32[1,64,64]{2,1,0:T(8,128)S(1)}, u32[]{:S(2)}, u32[]{:S(2)}) collective-permute-start(f32[1,64,64]{2,1,0:T(8,128)S(1)} %fusion.202), channel_id=1, source_target_pairs={{0,2},{2,4},{4,6},{6,8},{8,10},{10,12},{12,14},{14,16},{16,18},{18... | collective-permute-start | bytes 49160 | tf_op jit(solution)/shard_map/ppermute | solution.py:26
  435.6 3.6 collective-permute-start.38
  436.6 3.6 collective-permute-start.39
  440.3 1.7 collective-permute-start.40
  440.3 6.3 %collective-permute-start.41 = (f32[1,64,64]{2,1,0:T(8,128)S(1)}, f32[1,64,64]{2,1,0:T(8,128)S(1)}, u32[]{:S(2)}, u32[]{:S(2)}) collective-permute-start(f32[1,64,64]{2,1,0:T(8,128)S(1)} %fusion.194), channel_id=1, source_target_pairs={{0,2},{2,4},{4,6},{6,8},{8,10},{10,12},{12,14},{14,16},{16,18},{18... | collective-permute-start | bytes 49160 | tf_op jit(solution)/shard_map/ppermute | solution.py:26
  446.6 3.6 collective-permute-start.42
  447.6 3.6 collective-permute-start.43
  451.6 2.0 collective-permute-start.44
  451.7 6.4 %collective-permute-start.45 = (f32[1,128,128]{2,1,0:T(8,128)S(1)}, f32[1,128,128]{2,1,0:T(8,128)S(1)}, u32[]{:S(2)}, u32[]{:S(2)}) collective-permute-start(f32[1,128,128]{2,1,0:T(8,128)S(1)} %get-tuple-element.77), channel_id=1, source_target_pairs={{0,2},{2,4},{4,6},{6,8},{8,10},{10,12},{12,14},{14,16},{16,18},{18... | collective-permute-start | bytes 196616 | tf_op jit(solution)/shard_map/ppermute | solution.py:26
  458.1 3.6 collective-permute-start.46
  459.1 3.6 collective-permute-start.47
  462.9 2.0 collective-permute-start.48
  462.9 6.4 %collective-permute-start.49 = (f32[1,128,128]{2,1,0:T(8,128)S(1)}, f32[1,128,128]{2,1,0:T(8,128)S(1)}, u32[]{:S(2)}, u32[]{:S(2)}) collective-permute-start(f32[1,128,128]{2,1,0:T(8,128)S(1)} %get-tuple-element.71), channel_id=1, source_target_pairs={{0,2},{2,4},{4,6},{6,8},{8,10},{10,12},{12,14},{14,16},{16,18},{18... | collective-permute-start | bytes 196616 | tf_op jit(solution)/shard_map/ppermute | solution.py:26
  469.4 3.6 collective-permute-start.50
  470.4 3.6 collective-permute-start.51
  477.0 3.9 collective-permute-start.52
  477.1 8.5 %collective-permute-start.53 = (f32[1,256,256]{1,0,2:T(1,128)S(1)}, f32[1,256,256]{1,0,2:T(1,128)S(1)}, u32[]{:S(2)}, u32[]{:S(2)}) collective-permute-start(f32[1,256,256]{1,0,2:T(1,128)S(1)} %get-tuple-element.37), channel_id=1, source_target_pairs={{0,2},{2,4},{4,6},{6,8},{8,10},{10,12},{12,14},{14,16},{16,18},{18... | collective-permute-start | bytes 786440 | tf_op jit(solution)/shard_map/ppermute | solution.py:26
  489.8 3.7 collective-permute-start.54
  491.2 3.7 collective-permute-start.55
  503.9 3.9 collective-permute-start.56
  504.0 8.8 %collective-permute-start.57 = (f32[1,256,256]{1,0,2:T(1,128)S(1)}, f32[1,256,256]{1,0,2:T(1,128)S(1)}, u32[]{:S(2)}, u32[]{:S(2)}) collective-permute-start(f32[1,256,256]{1,0,2:T(1,128)S(1)} %get-tuple-element.31), channel_id=1, source_target_pairs={{0,2},{2,4},{4,6},{6,8},{8,10},{10,12},{12,14},{14,16},{16,18},{18... | collective-permute-start | bytes 786440 | tf_op jit(solution)/shard_map/ppermute | solution.py:26
  516.9 3.7 collective-permute-start.58
  518.3 3.7 collective-permute-start.59
  531.1 6.8 %collective-permute-start.60 = (f32[2,256,256]{1,0,2:T(2,128)S(1)}, f32[2,256,256]{1,0,2:T(2,128)S(1)}, u32[]{:S(2)}, u32[]{:S(2)}) collective-permute-start(f32[2,256,256]{1,0,2:T(2,128)S(1)} %get-tuple-element.25), channel_id=1, source_target_pairs={{2,0},{4,2},{6,4},{8,6},{10,8},{12,10},{14,12},{16,14},{18,16},{20... | collective-permute-start | bytes 1572872 | tf_op jit(solution)/shard_map/ppermute | solution.py:27
  531.1 11.4 %collective-permute-start.61 = (f32[2,256,256]{1,0,2:T(2,128)S(1)}, f32[2,256,256]{1,0,2:T(2,128)S(1)}, u32[]{:S(2)}, u32[]{:S(2)}) collective-permute-start(f32[2,256,256]{1,0,2:T(2,128)S(1)} %get-tuple-element.26), channel_id=1, source_target_pairs={{0,2},{2,4},{4,6},{6,8},{8,10},{10,12},{12,14},{14,16},{16,18},{18... | collective-permute-start | bytes 1572872 | tf_op jit(solution)/shard_map/ppermute | solution.py:26
  546.5 24.5 %all-to-all-start.1 = ((f32[2,4,256,256]{2,3,0,1:T(8,128)}), f32[2,4,256,256]{2,3,0,1:T(8,128)S(1)}, u32[]{:S(2)}, u32[]{:S(2)}) async-start(f32[2,4,256,256]{2,3,0,1:T(8,128)} %copy.98), calls=%async_computation.1 | async-start | bytes 4194304 | tf_op jit(solution)/shard_map/all_to_all | solution.py:168
  (27 other events, 482.6 us)
where the time goes:
time: 590 us; the launch traced here: 580 us
  waiting for transfers between devices  173 us (29%)
  local copies, waits for them, and re-layouts  149 us (25%)
  starting transfers between devices  113 us (19%)
  other arithmetic  85.3 us (14%)
  matrix products  57.2 us (10%)
    ppermute x31, waiting for transfers between devices, extended(): after = lax.ppermute(initial, axis, down)  89.1 us
    ppermute x31, starting transfers between devices, extended(): after = lax.ppermute(initial, axis, down)  78.8 us
    reshape x1, local copies, waits for them, and re-layouts, restrict(): blocks = field.reshape(planes // 2, 2, rows // 2, 2, depth // 2, 2)  68.4 us
    ppermute x31, waiting for transfers between devices, extended(): before = lax.ppermute(last, axis, up)  65.3 us
    add x10, other arithmetic, relax_padded(): interior + relax_weight / 6.0 * (padded_neighbours(padded) - 6.0 * interi...  30.7 us
    ppermute x31, starting transfers between devices, extended(): before = lax.ppermute(last, axis, up)  27 us
    reduce_sum x3, other arithmetic, restrict(): return jnp.sum(blocks, axis=(1, 3, 5)) * 0.125  23.7 us
    all_to_all x1, waiting for transfers between devices, local(): lax.all_to_all(jnp.stack([potential, streamwise_grad]), 'group', split_ax...  19.1 us
  transfers between devices with their start and end apart: 64, of which 49 were waited for; matrix products, arithmetic and copies ran while one was open for 42% of the time, Pallas kernels for 0%

commit v1 on v0

--- a/solution.py
+++ b/solution.py
@@ -2,7 +2,11 @@
 
 import jax
 import jax.numpy as jnp
+import ml_dtypes
+import numpy as np
 from jax import lax
+from jax.experimental import pallas as pl
+from jax.experimental.pallas import tpu as pltpu
 from jax.sharding import PartitionSpec as P
 
 LEVELS = 3
@@ -175,6 +179,617 @@
     return (corrected, potential)
 
 
+HALO = 16
+weight = relax_weight / 6.0
+bf16 = jnp.bfloat16
+f32 = jnp.float32
+VMEM = pl.BlockSpec(memory_space=pltpu.VMEM)
+ANY = pl.BlockSpec(memory_space=pl.ANY)
+
+
+def wave_tables(count):
+    index = np.arange(count)
+    angles = 2.0 * np.pi * (np.outer(index, index) % count) / count
+    theta = 2.0 * np.pi * index / count
+    first_wave = (14.0 / 9.0 * np.sin(theta) + np.sin(2.0 * theta) / 18.0) / (
+        1.0 + 2.0 / 3.0 * np.cos(theta)
+    )
+    second_wave = (
+        24.0 / 11.0 * (1.0 - np.cos(theta)) + 3.0 / 22.0 * (1.0 - np.cos(2.0 * theta))
+    ) / (1.0 + 4.0 / 11.0 * np.cos(theta))
+    cosines, sines = (np.cos(angles), np.sin(angles))
+    first = ((cosines * first_wave) @ sines.T - (sines * first_wave) @ cosines.T) / count
+    second = -((cosines * second_wave) @ cosines.T + (sines * second_wave) @ sines.T) / count
+    return (first, second)
+
+
+def high_low(table):
+    high = table.astype(np.float32).astype(ml_dtypes.bfloat16)
+    low = (table - high.astype(np.float64)).astype(np.float32).astype(ml_dtypes.bfloat16)
+    return (high, low)
+
+
+def half_tables(count):
+    first, second = wave_tables(count)
+    half = count // 2
+    index = np.arange(half)
+    root_first = (math.sqrt(5.0) - 3.0) / 2.0
+    root_second = (math.sqrt(105.0) - 11.0) / 4.0
+    basis = np.zeros((8, half))
+    basis[0, 0] = 1.0
+    basis[1, -1] = 1.0
+    basis[2] = root_first**index
+    basis[3] = basis[2][::-1]
+    basis[4] = root_second**index
+    basis[5] = basis[4][::-1]
+    spread = []
+    for table, used in ((first, (0, 1, 2, 3)), (second, (0, 1, 4, 5))):
+        solved = np.linalg.lstsq(basis[list(used)].T, table[:half, half:].T, rcond=None)[0].T
+        wide = np.zeros((half, 8))
+        wide[:, list(used)] = solved
+        spread.append(wide)
+    own = np.concatenate([first[:half, :half], second[:half, :half]], axis=0)
+    return (own, np.concatenate(spread, axis=0), basis, first)
+
+
+def split(value):
+    high = value.astype(bf16)
+    low = (value - high.astype(f32)).astype(bf16)
+    return (high, low)
+
+
+def dot(left, right):
+    return jnp.dot(left, right, preferred_element_type=f32)
+
+
+def dot_left(table_high, table_low, value):
+    high, low = split(value)
+    return dot(table_high, high) + (dot(table_high, low) + dot(table_low, high))
+
+
+def dot_right(value, table_high, table_low):
+    high, low = split(value)
+    return dot(high, table_high) + (dot(low, table_high) + dot(high, table_low))
+
+
+def pick_left(zero_one, value):
+    high, low = split(value)
+    return dot(zero_one, high) + dot(zero_one, low)
+
+
+def pick_right(value, zero_one):
+    high, low = split(value)
+    return dot(high, zero_one) + dot(low, zero_one)
+
+
+def summary(basis_both, value):
+    high, low = split(value)
+    main = dot(basis_both, high)
+    rest = dot(basis_both, low)
+    return main[:8] + main[8:] + rest[:8]
+
+
+def summary_operand(value):
+    high = value.astype(bf16).astype(f32)
+    return jnp.concatenate([high, value - high, high, jnp.zeros_like(high)], axis=0).astype(bf16)
+
+
+def turn(value, shift, axis):
+    return pltpu.roll(value, shift % value.shape[axis], axis)
+
+
+def cross_sum(value):
+    return (turn(value, 1, 0) + turn(value, -1, 0)) + (turn(value, 1, 1) + turn(value, -1, 1))
+
+
+def first_of(values):
+    return (8.0 * (values[3] - values[1]) - (values[4] - values[0])) * (1.0 / 12.0)
+
+
+def second_of(values):
+    return (
+        16.0 * (values[3] + values[1]) - (values[4] + values[0]) - 30.0 * values[2]
+    ) * (1.0 / 12.0)
+
+
+def kernel_call(body, outs, scratch, specs, flops, *args, grid=None, out_specs=None):
+    total = sum(math.prod(a.shape) * a.dtype.itemsize for a in args)
+    total += sum(4 * math.prod(s) for s in outs)
+    options = {} if grid is None else {"grid": grid}
+    return pl.pallas_call(
+        body,
+        out_shape=[jax.ShapeDtypeStruct(s, f32) for s in outs],
+        in_specs=specs,
+        out_specs=[VMEM] * len(outs) if out_specs is None else out_specs,
+        scratch_shapes=scratch,
+        compiler_params=pltpu.CompilerParams(vmem_limit_bytes=56 * 1024 * 1024),
+        cost_estimate=pl.CostEstimate(flops=flops, bytes_accessed=total, transcendentals=0),
+        **options,
+    )(*args)
+
+
+def summaries_kernel(velocity_ref, basis_ref, kept_ref, sent_ref):
+    side = lax.axis_index("group")
+    half = basis_ref.shape[1]
+    for part in range(2):
+        rows = pl.ds(pl.multiple_of((side if part else 1 - side) * half, half), half)
+        out = sent_ref if part else kept_ref
+        for c in range(3):
+            for plane in range(2):
+                out[c, plane] = summary(basis_ref[...], velocity_ref[c, plane, rows])
+
+
+def tendency_kernel(
+    velocity_ref, peer_u, peer_v, peer_w, one_ref, other_u, other_v, other_w,
+    kept_ref, peer_sum_ref, rows_high, rows_low, spread_ref, depth_high, depth_low,
+    out_ref, field, sums, sems,
+):
+    side = lax.axis_index("group")
+    half = rows_high.shape[1]
+    step = pl.program_id(0)
+    own_at, peer_at = (2 + 2 * side, 4 - 2 * side)
+    one_at, other_at = (6 - 6 * side, 6 * side)
+
+    @pl.when(step == 0)
+    def _():
+        rows = pl.ds(pl.multiple_of(side * half, half), half)
+        copies = []
+        peers, others = ((peer_u, peer_v, peer_w), (other_u, other_v, other_w))
+        for c in range(3):
+            for source, place in (
+                (velocity_ref.at[c, :, rows], own_at),
+                (peers[c], peer_at),
+                (one_ref.at[c], one_at),
+                (others[c], other_at),
+            ):
+                copies.append(
+                    pltpu.make_async_copy(
+                        source, field.at[c, pl.ds(place, 2)], sems.at[len(copies)]
+                    )
+                )
+        for copy in copies:
+            copy.start()
+        sums[:, pl.ds(2 * side, 2)] = kept_ref[...]
+        sums[:, pl.ds(2 - 2 * side, 2)] = peer_sum_ref[...]
+        for copy in copies:
+            copy.wait()
+
+    u, v, w = (field[c, step + 2] for c in range(3))
+    for c in range(3):
+        value = field[c, step + 2]
+        high, low = split(value)
+        across = (
+            dot(rows_high[...], high)
+            + (dot(rows_high[...], low) + dot(rows_low[...], high))
+            + dot(spread_ref[...], summary_operand(sums[c, step]))
+        )
+        along = dot(high, depth_high[...]) + (
+            dot(low, depth_high[...]) + dot(high, depth_low[...])
+        )
+        width = value.shape[1]
+        near = [field[c, step + k] for k in range(5)]
+        advect = u * first_of(near) + v * across[:half] + w * along[:, :width]
+        diffuse = second_of(near) + across[half:] + along[:, width:]
+        out_ref[c, 0] = value + time_step * (viscosity * diffuse - advect)
+
+
+def star_kernel(raw_ref, solid_own, solid_peer, basis_ref, low_u, high_u, star_v, star_w, sum_v, solid):
+    side = lax.axis_index("group")
+    solid[pl.ds(2 * side, 2)] = solid_own[...]
+    solid[pl.ds(2 - 2 * side, 2)] = solid_peer[...]
+    for plane in range(4):
+        keep = 1.0 - solid[plane].astype(f32)
+        out_u = low_u if plane < 2 else high_u
+        out_u[plane % 2] = raw_ref[0, plane] * keep
+        value = raw_ref[1, plane] * keep
+        star_v[plane] = value
+        sum_v[plane] = summary(basis_ref[...], value)
+        star_w[plane] = raw_ref[2, plane] * keep
+
+
+def cross_kernel(star_v, star_w, rows_high, rows_low, depth_high, depth_low, out_ref):
+    half = rows_high.shape[1]
+    out_ref[0] = dot_left(rows_high[:half], rows_low[:half], star_v[0]) + dot_right(
+        star_w[0], depth_high[:, : star_w.shape[2]], depth_low[:, : star_w.shape[2]]
+    )
+
+
+def source_kernel(low_u, high_u, left_ref, right_ref, cross_ref, sum_ref, spread_ref, low_r, high_r, edge):
+    half = cross_ref.shape[1]
+    planes = [left_ref[0], left_ref[1], low_u[0], low_u[1], high_u[0], high_u[1], right_ref[0], right_ref[1]]
+    for plane in range(4):
+        value = (
+            first_of(planes[plane : plane + 5])
+            + cross_ref[plane]
+            + dot(spread_ref[:half], summary_operand(sum_ref[plane]))
+        )
+        out = low_r if plane < 2 else high_r
+        out[plane % 2] = value
+        edge[plane, :HALO] = value[:HALO]
+        edge[plane, HALO:] = value[half - HALO :]
+
+
+def fine_kernel(
+    pressure_ref, low_r, high_r, left_ref, right_ref, edge_ref, left_edge, right_edge, depth_pick, rows_pick,
+    base_ref, source_ref, coarse_ref, one, two,
+):
+    half = low_r.shape[1]
+    for plane in range(8):
+        body, edge = (
+            (left_ref, left_edge) if plane < 2 else
+            (low_r, edge_ref) if plane < 4 else
+            (high_r, edge_ref) if plane < 6 else (right_ref, right_edge)
+        )
+        at = plane - 2 if 2 <= plane < 6 else plane % 2
+        source_ref[plane, HALO : HALO + half] = body[plane % 2]
+        source_ref[plane, :HALO] = edge[at, HALO:]
+        source_ref[plane, HALO + half :] = edge[at, :HALO]
+    for k in range(8):
+        centre = pressure_ref[k + 1]
+        total = pressure_ref[k] + pressure_ref[k + 2] + cross_sum(centre)
+        one[k] = centre + weight * (total - 6.0 * centre - source_ref[k])
+    for k in range(6):
+        centre = one[k + 1]
+        total = one[k] + one[k + 2] + cross_sum(centre)
+        two[k] = centre + weight * (total - 6.0 * centre - source_ref[k + 1])
+    for pair in range(2):
+        left = []
+        for k in (2 * pair, 2 * pair + 1):
+            centre = two[k + 1]
+            total = two[k] + two[k + 2] + cross_sum(centre)
+            residual = source_ref[k + 2] - (total - 6.0 * centre)
+            base_ref[k] = centre - weight * residual
+            left.append(residual)
+        coarse_ref[pair] = 0.125 * pick_left(rows_pick[...], pick_right(left[0] + left[1], depth_pick[...]))
+
+
+def middle_kernel(own_ref, left_ref, right_ref, depth_pick, rows_pick, base_ref, coarse_ref, one, two):
+    source = [left_ref[0], left_ref[1], own_ref[0], own_ref[1], right_ref[0], right_ref[1]]
+    for k in range(6):
+        one[k] = (-4.0 * weight) * source[k]
+    for k in range(4):
+        centre = one[k + 1]
+        total = one[k] + one[k + 2] + cross_sum(centre)
+        two[k] = centre + weight * (total - 6.0 * centre - 4.0 * source[k + 1])
+    left = []
+    for k in range(2):
+        centre = two[k + 1]
+        total = two[k] + two[k + 2] + cross_sum(centre)
+        residual = source[k + 2] - 0.25 * (total - 6.0 * centre)
+        base_ref[k] = centre - (4.0 * weight) * residual
+        left.append(residual)
+    coarse_ref[...] = 0.125 * pick_left(rows_pick[...], pick_right(left[0] + left[1], depth_pick[...]))
+
+
+def middle_base_kernel(base_ref, left_ref, right_ref, source_ref, out_ref):
+    rows = out_ref.shape[1]
+    planes = [left_ref[0], base_ref[0], base_ref[1], right_ref[0]]
+    for k in range(2):
+        centre = planes[k + 1]
+        total = planes[k] + planes[k + 2] + cross_sum(centre)
+        value = centre + weight * (total - 6.0 * centre - 4.0 * source_ref[k])
+        out_ref[k] = value[HALO // 2 : HALO // 2 + rows]
+
+
+def base_kernel(base_ref, left_ref, right_ref, source_ref, low_ref, high_ref):
+    rows = low_ref.shape[1]
+    for k in range(4):
+        before = left_ref[0] if k == 0 else base_ref[k - 1]
+        after = right_ref[0] if k == 3 else base_ref[k + 1]
+        centre = base_ref[k]
+        total = before + after + cross_sum(centre)
+        value = centre + weight * (total - 6.0 * centre - source_ref[k + 2])
+        out = low_ref if k < 2 else high_ref
+        out[k % 2] = value[HALO : HALO + rows]
+
+
+def stream_kernel(low_ref, high_ref, left_ref, right_ref, low_u, high_u, own_ref, sent_ref):
+    side = lax.axis_index("group")
+    planes = [left_ref[0], left_ref[1], low_ref[0], low_ref[1], high_ref[0], high_ref[1], right_ref[0], right_ref[1]]
+    value = []
+    for plane in range(4):
+        star = (low_u if plane < 2 else high_u)[plane % 2]
+        value.append(star - first_of(planes[plane : plane + 5]))
+
+    @pl.when(side == 0)
+    def _():
+        for k in range(2):
+            own_ref[k] = value[k]
+            sent_ref[k] = value[2 + k]
+
+    @pl.when(side == 1)
+    def _():
+        for k in range(2):
+            own_ref[k] = value[2 + k]
+            sent_ref[k] = value[k]
+
+
+def final_kernel(
+    coarse_ref, own_mid, left_mid, right_mid, low_base, high_base, peer_base, own_u, peer_u,
+    star_v, peer_v, star_w, peer_w, solid_ref,
+    sum_high, sum_low, diff_high, diff_low, depth_high, depth_low,
+    mid_depth, mid_rows, fine_depth, fine_rows,
+    out_ref, potential_ref, bottom, bottom_next, spread2, mid, mid_next, fine, first_sweep, delta, section,
+):
+    side = lax.axis_index("group")
+    place = lax.axis_index("tunnel")
+    count = coarse_ref.shape[0]
+    half = own_u.shape[1]
+    own_rows = pl.ds(pl.multiple_of(side * half, half), half)
+    peer_rows = pl.ds(pl.multiple_of((1 - side) * half, half), half)
+    for k in range(11):
+        bottom[k] = (-16.0 * weight) * coarse_ref[lax.rem(place + (k + 2 * count - 5), count)]
+    source_at, target = (bottom, bottom_next)
+    for sweep_index in range(1, COARSE_SWEEPS):
+        for k in range(sweep_index, 11 - sweep_index):
+            centre = source_at[k]
+            total = source_at[k - 1] + source_at[k + 1] + cross_sum(centre)
+            right = coarse_ref[lax.rem(place + (k + 2 * count - 5), count)]
+            target[k] = centre + weight * (total - 6.0 * centre - 16.0 * right)
+        source_at, target = (target, source_at)
+    for k in range(5):
+        spread2[k] = pick_left(mid_rows[...], pick_right(source_at[k + 3], mid_depth[...]))
+    for k in range(9):
+        mid[k] = spread2[(side + k) // 2]
+    for k in range(1, 8):
+        centre = mid[k]
+        total = mid[k - 1] + mid[k + 1] + cross_sum(centre)
+        mid_next[k] = centre + weight * (total - 6.0 * centre)
+    held = (left_mid, own_mid, right_mid)
+    for k in range(6):
+        mid[9 + k] = held[k // 2][k % 2]
+    for k in range(2, 7):
+        centre = mid_next[k]
+        total = mid_next[k - 1] + mid_next[k + 1] + cross_sum(centre)
+        value = mid[9 + side + (k - 2)] + centre + weight * (total - 6.0 * centre)
+        fine[k - 2] = pick_left(fine_rows[...], pick_right(value, fine_depth[...]))
+    for j in range(5):
+        centre = fine[j]
+        shared = centre + weight * (centre + cross_sum(centre) - 6.0 * centre)
+        if j > 0:
+            first_sweep[2 * j - 1] = shared + weight * fine[j - 1]
+        if j < 4:
+            first_sweep[2 * j] = shared + weight * fine[j + 1]
+    for k in range(6):
+        centre = first_sweep[k + 1]
+        total = first_sweep[k] + first_sweep[k + 2] + cross_sum(centre)
+        delta[k] = centre + weight * (total - 6.0 * centre)
+    for k in range(4):
+        base = (low_base if k < 2 else high_base)[k % 2]
+        potential_ref[k] = base + delta[k + 2 - 2 * side, own_rows]
+    for k in range(2):
+        at = 2 + k
+        section[peer_rows] = delta[at, peer_rows] + peer_base[k]
+        section[own_rows] = potential_ref[2 * side + k]
+        value = section[...]
+        keep = 1.0 - solid_ref[k].astype(f32)
+        out_ref[2, k, own_rows] = star_w[2 * side + k]
+        out_ref[2, k, peer_rows] = peer_w[k]
+        out_ref[2, k] = (out_ref[2, k] - dot_right(value, depth_high[...], depth_low[...])) * keep
+        out_ref[1, k, own_rows] = star_v[2 * side + k]
+        out_ref[1, k, peer_rows] = peer_v[k]
+        top, low = (value[:half], value[half:])
+        even = dot_left(sum_high[...], sum_low[...], top + low)
+        odd = dot_left(diff_high[...], diff_low[...], top - low)
+        out_ref[1, k, :half] = (out_ref[1, k, :half] - (even + odd)) * keep[:half]
+        out_ref[1, k, half:] = (out_ref[1, k, half:] - (even - odd)) * keep[half:]
+        out_ref[0, k, own_rows] = own_u[k]
+        out_ref[0, k, peer_rows] = peer_u[k]
+        gradient = first_of([delta[at + offset] for offset in range(-2, 3)])
+        out_ref[0, k] = (out_ref[0, k] - gradient) * keep
+
+
+def pair_sums(fine, coarse):
+    return (np.arange(fine)[:, None] // 2 == np.arange(coarse)[None, :]).astype(ml_dtypes.bfloat16)
+
+
+def paired(velocity, obstacle, pressure):
+    rows, depth = velocity.shape[2:]
+    half = rows // 2
+    wide = half + 2 * HALO
+    tunnel_size = lax.axis_size("tunnel")
+    side = lax.axis_index("group")
+    both = ("tunnel", "group")
+    own, spread, basis, rows_first = half_tables(rows)
+    depth_first, depth_second = wave_tables(depth)
+    rows_high, rows_low = high_low(own)
+    spread_high, spread_low = high_low(spread)
+    spread_all = np.concatenate([spread_high, spread_high, spread_low, np.zeros_like(spread_low)], axis=1)
+    basis_both = np.concatenate(high_low(basis), axis=0)
+    depth_high, depth_low = high_low(np.concatenate([depth_first.T, depth_second.T], axis=1))
+    sum_high, sum_low = high_low((rows_first[:half, :half] + rows_first[:half, half:]) / 2.0)
+    diff_high, diff_low = high_low((rows_first[:half, :half] - rows_first[:half, half:]) / 2.0)
+
+    def swap(value):
+        return lax.ppermute(value, "group", [(0, 1), (1, 0)])
+
+    def forward(value):
+        return lax.ppermute(value, "tunnel", [(i, (i + 1) % tunnel_size) for i in range(tunnel_size)])
+
+    def backward(value):
+        return lax.ppermute(value, "tunnel", [((i + 1) % tunnel_size, i) for i in range(tunnel_size)])
+
+    own_way, swapped_way = ([], [])
+    for i in range(tunnel_size):
+        ahead, behind = ((i + 1) % tunnel_size, (i - 1) % tunnel_size)
+        own_way += [(2 * i + 1, 2 * ahead + 1), (2 * i, 2 * behind)]
+        swapped_way += [(2 * i, 2 * ahead), (2 * i + 1, 2 * behind + 1)]
+
+    def half_of(value, which, axis):
+        return lax.dynamic_slice_in_dim(value, which * half, half, axis=axis)
+
+    def pair_of(value, which):
+        return lax.dynamic_slice_in_dim(value, 2 * which, 2, axis=0)
+
+    plane = (half, depth)
+    peers, others = ([], [])
+    for c in range(3):
+        peers.append(swap(half_of(velocity[c], 1 - side, 1)))
+    one = lax.ppermute(half_of(velocity, side, 2), both, own_way)
+    for c in range(3):
+        others.append(lax.ppermute(peers[c], both, swapped_way))
+    kept_sum, sent_sum = kernel_call(
+        summaries_kernel, [(3, 2, 8, depth)] * 2, [], [VMEM] * 2, 10**8, velocity, basis_both
+    )
+    peer_sum = swap(sent_sum)
+    solid_peer = swap(half_of(obstacle, 1 - side, 1))
+
+    edge = swap(jnp.concatenate([pressure[:, :HALO], pressure[:, half - HALO :]], axis=1))
+    tall = jnp.concatenate([edge[:, HALO:], pressure, edge[:, :HALO]], axis=1)
+    pressure_wide = jnp.concatenate([forward(tall[1:]), tall, backward(tall[:3])], axis=0)
+
+    full = lambda shape: pl.BlockSpec(shape, lambda i: (0,) * len(shape))
+    (raw,) = kernel_call(
+        tendency_kernel,
+        [(3, 4) + plane],
+        [
+            pltpu.VMEM((3, 8) + plane, f32),
+            pltpu.VMEM((3, 4, 8, depth), f32),
+            pltpu.SemaphoreType.DMA((12,)),
+        ],
+        [ANY] * 8 + [full((3, 2, 8, depth))] * 2
+        + [full(rows_high.shape)] * 2 + [full(spread_all.shape)] + [full(depth_high.shape)] * 2,
+        6 * 10**9,
+        velocity, *peers, one, *others, kept_sum, peer_sum, rows_high, rows_low, spread_all, depth_high, depth_low,
+        grid=(4,),
+        out_specs=[pl.BlockSpec((3, 1) + plane, lambda i: (0, i, 0, 0))],
+    )
+    two_planes, four_planes = ((2,) + plane, (4,) + plane)
+    low_u, high_u, star_v, star_w, sum_v = kernel_call(
+        star_kernel,
+        [two_planes, two_planes, four_planes, four_planes, (4, 8, depth)],
+        [pltpu.VMEM(four_planes, jnp.int32)],
+        [VMEM] * 4,
+        10**8,
+        raw, half_of(obstacle, side, 1), solid_peer, basis_both,
+    )
+    left_u, right_u = (forward(high_u), backward(low_u))
+    peer_sum_v = swap(sum_v)
+    by_plane = pl.BlockSpec((1,) + plane, lambda i: (i, 0, 0))
+    (cross,) = kernel_call(
+        cross_kernel,
+        [four_planes],
+        [],
+        [by_plane] * 2 + [full(rows_high.shape)] * 2 + [full(depth_high.shape)] * 2,
+        10**9,
+        star_v, star_w, rows_high, rows_low, depth_high, depth_low,
+        grid=(4,),
+        out_specs=[by_plane],
+    )
+    low_r, high_r, edge_r = kernel_call(
+        source_kernel,
+        [two_planes, two_planes, (4, 2 * HALO, depth)],
+        [],
+        [VMEM] * 7,
+        10**8,
+        low_u, high_u, left_u, right_u, cross, peer_sum_v, spread_all,
+    )
+    edges = swap(edge_r)
+    left_r, right_r = (forward(high_r), backward(low_r))
+    left_edge, right_edge = (forward(edges[2:]), backward(edges[:2]))
+    peer_v, peer_w = (swap(pair_of(star_v, 1 - side)), swap(pair_of(star_w, 1 - side)))
+
+    mid_rows, mid_depth = (wide // 2, depth // 2)
+    base_one, source_wide, mid_source = kernel_call(
+        fine_kernel,
+        [(4, wide, depth), (8, wide, depth), (2, mid_rows, mid_depth)],
+        [pltpu.VMEM((8, wide, depth), f32), pltpu.VMEM((6, wide, depth), f32)],
+        [VMEM] * 10,
+        10**8,
+        pressure_wide, low_r, high_r, left_r, right_r, edges, left_edge, right_edge,
+        pair_sums(depth, mid_depth), pair_sums(wide, mid_rows).T,
+    )
+    left_mid, right_mid = (forward(mid_source), backward(mid_source))
+    low_depth = mid_depth // 2
+    twice = np.concatenate([pair_sums(mid_depth, low_depth)] * 2, axis=1)
+    own_pairs = pair_sums(half // 2, half // 4).T
+    own_pairs = np.pad(own_pairs, ((0, 0), (HALO // 2, HALO // 2)))
+    mid_one, low_source = kernel_call(
+        middle_kernel,
+        [(2, mid_rows, mid_depth), (half // 4, mid_depth)],
+        [pltpu.VMEM((6, mid_rows, mid_depth), f32), pltpu.VMEM((4, mid_rows, mid_depth), f32)],
+        [VMEM] * 5,
+        10**8,
+        mid_source, left_mid, right_mid, twice, own_pairs,
+    )
+    low_all = lax.all_gather(low_source, both)
+    low_all = low_all.reshape(tunnel_size, half // 2, mid_depth)
+    left_one, right_one = (forward(mid_one[1:]), backward(mid_one[:1]))
+    (mid_base,) = kernel_call(
+        middle_base_kernel,
+        [(2, half // 2, mid_depth)],
+        [],
+        [VMEM] * 4,
+        10**7,
+        mid_one, left_one, right_one, mid_source,
+    )
+    other_mid = swap(mid_base)
+    mid_base = jnp.where(
+        side == 0,
+        jnp.concatenate([mid_base, other_mid], axis=1),
+        jnp.concatenate([other_mid, mid_base], axis=1),
+    )
+    left_mid, right_mid = (forward(mid_base), backward(mid_base))
+
+    left_base, right_base = (forward(base_one[3:]), backward(base_one[:1]))
+    low_base, high_base = kernel_call(
+        base_kernel,
+        [two_planes, two_planes],
+        [],
+        [VMEM] * 4,
+        10**8,
+        base_one, left_base, right_base, source_wide,
+    )
+    peer_base = swap(jnp.where(side == 0, high_base, low_base))
+    left_b, right_b = (forward(high_base), backward(low_base))
+    own_u, sent_u = kernel_call(
+        stream_kernel,
+        [two_planes, two_planes],
+        [],
+        [VMEM] * 6,
+        10**8,
+        low_base, high_base, left_b, right_b, low_u, high_u,
+    )
+    peer_u = swap(sent_u)
+    low_plane = (half // 2, mid_depth)
+    mid_plane = (half, mid_depth)
+    fine_plane = (rows, depth)
+    expand_low = np.zeros((mid_depth, mid_depth), ml_dtypes.bfloat16)
+    expand_low[:low_depth] = pair_sums(mid_depth, low_depth).T
+    return kernel_call(
+        final_kernel,
+        [(3, 2) + fine_plane, four_planes],
+        [
+            pltpu.VMEM((11,) + low_plane, f32),
+            pltpu.VMEM((11,) + low_plane, f32),
+            pltpu.VMEM((5,) + mid_plane, f32),
+            pltpu.VMEM((15,) + mid_plane, f32),
+            pltpu.VMEM((9,) + mid_plane, f32),
+            pltpu.VMEM((5,) + fine_plane, f32),
+            pltpu.VMEM((8,) + fine_plane, f32),
+            pltpu.VMEM((6,) + fine_plane, f32),
+            pltpu.VMEM(fine_plane, f32),
+        ],
+        [VMEM] * 24,
+        10**9,
+        low_all, mid_base, left_mid, right_mid, low_base, high_base, peer_base, own_u, peer_u,
+        star_v, peer_v, star_w, peer_w, obstacle,
+        sum_high, sum_low, diff_high, diff_low,
+        np.ascontiguousarray(depth_high[:, :depth]), np.ascontiguousarray(depth_low[:, :depth]),
+        expand_low, pair_sums(half, half // 2),
+        np.ascontiguousarray(pair_sums(depth, mid_depth).T), pair_sums(rows, half),
+    )
+
+
+def step(velocity, obstacle, pressure):
+    planes, rows, depth = velocity.shape[1:]
+    fits = lax.axis_size("group") == 2 and planes == 2 and pressure.shape[0] == 4
+    fits = fits and lax.axis_size("tunnel") > 10 and rows % 512 == 0 and depth % 256 == 0
+    if fits:
+        return tuple(paired(velocity, obstacle, pressure))
+    return local(velocity, obstacle, pressure)
+
+
 def solution(mesh):
     in_specs = (
         P(None, ("tunnel", "group"), None, None),
@@ -182,4 +797,4 @@
         P("tunnel", "group", None),
     )
     out_specs = (P(None, ("tunnel", "group"), None, None), P("tunnel", "group", None))
-    return jax.shard_map(local, mesh=mesh, in_specs=in_specs, out_specs=out_specs, check_vma=False)
+    return jax.shard_map(step, mesh=mesh, in_specs=in_specs, out_specs=out_specs, check_vma=False)

time: 590 us -> 250 us (0.42); the launches traced: 580 us -> 247 us
  local copies, waits for them, and re-layouts: 149 us -> 18.7 us
  waiting for transfers between devices: 173 us -> 78.3 us
  other arithmetic: 85.3 us -> 3.99 us
  Pallas kernels: 0 us -> 60.5 us
  matrix products: 57.2 us -> 0 us
  starting transfers between devices: 113 us -> 70.6 us
  between operations: 1.79 us -> 14.4 us
    ppermute x62 -> x35, waiting for transfers between devices: 154 us -> 78.2 us  [the longest x13 65.3 us: swap(): return lax.ppermute(value, 'group', [(0, 1), (1, 0)])]
    reshape x2 -> x0, local copies, waits for them, and re-layouts: 69.4 us -> none  [the longest x1 68.4 us: restrict(): blocks = field.reshape(planes // 2, 2, rows // 2, 2, depth // 2, 2)]
    pallas_call x0 -> x11, Pallas kernels: none -> 60.5 us  [kernel_call(): pl.pallas_call(body, out_shape=[jax.ShapeDtypeStruct(s, f32) for s in out...]
    dot_general x14 -> x0, matrix products: 57.2 us -> none  [the longest x3 16.1 us: along_rows(): return jnp.einsum('ij,...jz->...iz', matrix, field, precision=highest)]
    slice x54 -> x7, local copies, waits for them, and re-layouts: 38.6 us -> 3.1 us  [the longest x1 1.73 us: paired(): peers.append(swap(half_of(velocity[c], 1 - side, 1)))]
    ppermute x62 -> x35, starting transfers between devices: 106 us -> 70.6 us  [the longest x9 26.1 us: backward(): lax.ppermute(value, 'tunnel', [((i + 1) % tunnel_size, i) for i in range(...]
    add x12 -> x0, other arithmetic: 32 us -> none  [the longest x10 30.7 us: relax_padded(): interior + relax_weight / 6.0 * (padded_neighbours(padded) - 6.0 * interi...]
    reduce_sum x3 -> x0, other arithmetic: 23.7 us -> none  [restrict(): return jnp.sum(blocks, axis=(1, 3, 5)) * 0.125]
  transfers between devices with their start and end apart: 64 -> 36, of which waited for: 49 -> 11; matrix products, arithmetic and copies ran while one was open for 42% -> 5% of each run, Pallas kernels for 0% -> 13%
where the time goes in v1:
time: 250 us; the launch traced here: 247 us
  waiting for transfers between devices  78.3 us (31%)
  starting transfers between devices  70.6 us (28%)
  Pallas kernels  60.5 us (24%)
  local copies, waits for them, and re-layouts  18.7 us (7%)
  between operations  14.4 us (6%)
  other arithmetic  3.99 us (2%)
    ppermute x13, waiting for transfers between devices, swap(): return lax.ppermute(value, 'group', [(0, 1), (1, 0)])  65.3 us
    pallas_call x11, Pallas kernels, kernel_call(): pl.pallas_call(body, out_shape=[jax.ShapeDtypeStruct(s, f32) for s in out...  60.5 us
    ppermute x9, starting transfers between devices, backward(): lax.ppermute(value, 'tunnel', [((i + 1) % tunnel_size, i) for i in range(...  26.1 us
    ppermute x9, starting transfers between devices, forward(): lax.ppermute(value, 'tunnel', [(i, (i + 1) % tunnel_size) for i in range(...  23.8 us
    ppermute x13, starting transfers between devices, swap(): return lax.ppermute(value, 'group', [(0, 1), (1, 0)])  15.3 us
    ppermute x9, waiting for transfers between devices, forward(): lax.ppermute(value, 'tunnel', [(i, (i + 1) % tunnel_size) for i in range(...  11.1 us
    unnamed x76, local copies, waits for them, and re-layouts  8.4 us
    dynamic_slice x5, local copies, waits for them, and re-layouts, half_of(): return lax.dynamic_slice_in_dim(value, which * half, half, axis=axis)  7.16 us
  transfers between devices with their start and end apart: 36, of which 11 were waited for; matrix products, arithmetic and copies ran while one was open for 5% of the time, Pallas kernels for 13%

profile of v1, /device:TPU:0, one launch (start us, length us, event | category | flops | bytes accessed | tf_op | source)
XLA Modules:
  0.0 246.6 jit_solution(7251212767745796186)
XLA Ops:
  7.2 2.9 %constant_dynamic-slice_fusion.4 = f32[3,2,256,256]{3,2,1,0:T(8,128)} fusion(f32[3,2,512,256]{3,2,1,0:T(8,128)} %velocity_ref.3, s32[]{:T(128)S(6)} %select_n.31), kind=kLoop, calls=%fused_computation.12 | loop fusion | bytes 3145732 | tf_op jit(solution)/shard_map/dynamic_slice | solution.py:619
  10.1 5.4 %collective-permute-start.6 = (f32[3,2,256,256]{3,2,1,0:T(8,128)}, f32[3,2,256,256]{3,2,1,0:T(8,128)}, u32[]{:S(2)}, u32[]{:S(2)}) collective-permute-start(f32[3,2,256,256]{3,2,1,0:T(8,128)} %constant_dynamic-slice_fusion.4), channel_id=1, source_target_pairs={{1,3},{0,30},{3,5},{2,0},{5,7},{4,2},{7,9},{6,4},{9,11},{8,6},{11,... | collective-permute-start | bytes 4718600 | tf_op jit(solution)/shard_map/ppermute | solution.py:628
  15.5 1.7 fusion
  17.3 1.2 dynamic-slice_bitcast_fusion.2
  18.5 1.2 dynamic-slice_bitcast_fusion.1
  19.7 2.0 collective-permute-start.4
  21.7 1.1 dynamic-slice_bitcast_fusion
  22.9 10.4 %collective-permute-done.3.peer_u = f32[2,256,256]{2,1,0:T(8,128)S(1)} collective-permute-done((f32[2,256,256]{2,1,0:T(8,128)S(1)}, f32[2,256,256]{2,1,0:T(8,128)S(1)}, u32[]{:S(2)}, u32[]{:S(2)}) %collective-permute-start.3) | collective-permute-done | bytes 524320 | tf_op jit(solution)/shard_map/ppermute | solution.py:604
  33.4 11.2 %collective-permute-done.4.peer_v = f32[2,256,256]{2,1,0:T(8,128)S(1)} collective-permute-done((f32[2,256,256]{2,1,0:T(8,128)S(1)}, f32[2,256,256]{2,1,0:T(8,128)S(1)}, u32[]{:S(2)}, u32[]{:S(2)}) %collective-permute-start.4) | collective-permute-done | bytes 524320 | tf_op jit(solution)/shard_map/ppermute | solution.py:604
  44.6 7.6 %collective-permute-done.5.peer_w = f32[2,256,256]{2,1,0:T(8,128)S(1)} collective-permute-done((f32[2,256,256]{2,1,0:T(8,128)S(1)}, f32[2,256,256]{2,1,0:T(8,128)S(1)}, u32[]{:S(2)}, u32[]{:S(2)}) %collective-permute-start.5) | collective-permute-done | bytes 524320 | tf_op jit(solution)/shard_map/ppermute | solution.py:604
  52.3 4.1 %collective-permute-start = (f32[4,32,256]{2,1,0:T(8,128)S(1)}, f32[4,32,256]{2,1,0:T(8,128)S(1)}, u32[]{:S(2)}, u32[]{:S(2)}) collective-permute-start(f32[4,32,256]{2,1,0:T(8,128)S(1)} %pad_maximum_fusion.2), channel_id=1, source_target_pairs={{0,1},{1,0},{2,3},{3,2},{4,5},{5,4},{6,7},{7,6},{8,9},{9,8},{10,11... | collective-permute-start | bytes 393224 | tf_op jit(solution)/shard_map/ppermute | solution.py:604
  56.4 3.0 %shard_map.230 = (f32[3,2,8,256]{3,2,1,0:T(8,128)}, f32[3,2,8,256]{3,2,1,0:T(8,128)}) custom-call(f32[3,2,512,256]{3,2,1,0:T(8,128)} %velocity_ref.3, bf16[16,256]{1,0:T(8,128)(2,1)} %constant.57.clone.basis_ref), custom_call_target="tpu_custom_call" | custom-call | flops 100000000 | bytes 3252224 | tf_op jit(solution)/shard_map/pallas_call | solution.py:299
  59.4 0.9 constant_dynamic-slice_fusion.2
  60.3 1.1 collective-permute-start.10
  61.5 3.5 %collective-permute-done.10.peer_sum_ref = f32[3,2,8,256]{3,2,1,0:T(8,128)S(1)} collective-permute-done((f32[3,2,8,256]{3,2,1,0:T(8,128)}, f32[3,2,8,256]{3,2,1,0:T(8,128)S(1)}, u32[]{:S(2)}, u32[]{:S(2)}) %collective-permute-start.10) | collective-permute-done | bytes 49184 | tf_op jit(solution)/shard_map/ppermute | solution.py:604
  65.0 1.2 collective-permute-start.11
  66.2 0.7 copy-done.33
  67.3 12.2 %shard_map.231.raw_ref = f32[3,4,256,256]{3,2,1,0:T(8,128)} custom-call(f32[3,2,512,256]{3,2,1,0:T(8,128)} %velocity_ref.3, f32[2,256,256]{2,1,0:T(8,128)} %copy-done.30, f32[2,256,256]{2,1,0:T(8,128)} %copy-done.31, f32[2,256,256]{2,1,0:T(8,128)} %copy-done.32, f32[3,2,256,256]{3,2,1,0:T(8,128)} %collective-permute-done.6.one_ref, ...), custom_call_target="tpu_custom_call" | custom-call | flops 6000000000 | bytes 12189696 | tf_op jit(solution)/shard_map/pallas_call | solution.py:299
  79.6 0.8 copy-done.18
  80.3 4.3 %shard_map.232 = (f32[2,256,256]{2,1,0:T(8,128)}, f32[2,256,256]{2,1,0:T(8,128)}, f32[4,256,256]{2,1,0:T(8,128)}, f32[4,256,256]{2,1,0:T(8,128)}, f32[4,8,256]{2,1,0:T(8,128)}) custom-call(f32[3,4,256,256]{3,2,1,0:T(8,128)} %shard_map.231.raw_ref, s32[2,256,256]{2,1,0:T(8,128)} %get-tuple-element.48.solid_own, s32[2,256,256]{2,1,0:T(8,128)} %copy-done.18, ...), custom_call_target="tpu_custom_call" | custom-call | flops 100000000 | bytes 7380992 | tf_op jit(solution)/shard_map/pallas_call | solution.py:299
  84.6 4.4 %collective-permute-start.13 = (f32[2,256,256]{2,1,0:T(8,128)}, f32[2,256,256]{2,1,0:T(8,128)S(1)}, u32[]{:S(2)}, u32[]{:S(2)}) collective-permute-start(f32[2,256,256]{2,1,0:T(8,128)} %get-tuple-element.23.low_u), channel_id=1, source_target_pairs={{2,0},{4,2},{6,4},{8,6},{10,8},{12,10},{14,12},{16,14},{18,16},{20... | collective-permute-start | bytes 1572872 | tf_op jit(solution)/shard_map/ppermute | solution.py:610
  89.3 4.4 %collective-permute-start.2 = (f32[3,288,256]{2,1,0:T(8,128)S(1)}, f32[3,288,256]{2,1,0:T(8,128)S(1)}, u32[]{:S(2)}, u32[]{:S(2)}) collective-permute-start(f32[3,288,256]{2,1,0:T(8,128)S(1)} %get-tuple-element.46), channel_id=1, source_target_pairs={{2,0},{4,2},{6,4},{8,6},{10,8},{12,10},{14,12},{16,14},{18,16},{20... | collective-permute-start | bytes 2654216 | tf_op jit(solution)/shard_map/ppermute | solution.py:610
  93.7 0.8 collective-permute-start.14
  94.5 4.6 %shard_map.233.cross_ref = f32[4,256,256]{2,1,0:T(8,128)} custom-call(f32[4,256,256]{2,1,0:T(8,128)} %get-tuple-element.25.star_v, f32[4,256,256]{2,1,0:T(8,128)} %get-tuple-element.26.star_w, bf16[512,256]{1,0:T(8,128)(2,1)} %constant.58.clone.rows_high, bf16[512,256]{1,0:T(8,128)(2,1)} %constant.59.clone.rows_low, ...), custom_call_target="tpu_custom_call" | custom-call | flops 1000000000 | bytes 4194304 | tf_op jit(solution)/shard_map/pallas_call | solution.py:299
  99.2 0.6 copy-done.29
  99.9 0.8 copy-done.14
  100.7 3.1 %shard_map.234 = (f32[2,256,256]{2,1,0:T(8,128)}, f32[2,256,256]{2,1,0:T(8,128)}, f32[4,32,256]{2,1,0:T(8,128)}) custom-call(f32[2,256,256]{2,1,0:T(8,128)} %get-tuple-element.23.low_u, f32[2,256,256]{2,1,0:T(8,128)} %get-tuple-element.24.high_u, f32[2,256,256]{2,1,0:T(8,128)} %copy-done.13, f32[2,256,256]{2,1,0:T(8,128)} %copy-done.14, ...), custom_call_target="tpu_custom_call" | custom-call | flops 100000000 | bytes 4390912 | tf_op jit(solution)/shard_map/pallas_call | solution.py:299
  103.9 1.2 collective-permute-start.17
  105.1 6.7 %collective-permute-start.15 = (f32[2,256,256]{2,1,0:T(8,128)}, f32[2,256,256]{2,1,0:T(8,128)S(1)}, u32[]{:S(2)}, u32[]{:S(2)}) collective-permute-start(f32[2,256,256]{2,1,0:T(8,128)} %get-tuple-element.29.high_r), channel_id=1, source_target_pairs={{0,2},{2,4},{4,6},{6,8},{8,10},{10,12},{12,14},{14,16},{16,18},{18... | collective-permute-start | bytes 1572872 | tf_op jit(solution)/shard_map/ppermute | solution.py:607
  111.8 4.4 %collective-permute-start.18 = (f32[2,32,256]{2,1,0:T(8,128)S(1)}, f32[2,32,256]{2,1,0:T(8,128)S(1)}, u32[]{:S(2)}, u32[]{:S(2)}) collective-permute-start(f32[2,32,256]{2,1,0:T(8,128)S(1)} %get-tuple-element.54), channel_id=1, source_target_pairs={{0,2},{2,4},{4,6},{6,8},{8,10},{10,12},{12,14},{14,16},{16,18},{18... | collective-permute-start | bytes 196616 | tf_op jit(solution)/shard_map/ppermute | solution.py:607
  116.1 4.5 %collective-permute-start.19 = (f32[2,32,256]{2,1,0:T(8,128)S(1)}, f32[2,32,256]{2,1,0:T(8,128)S(1)}, u32[]{:S(2)}, u32[]{:S(2)}) collective-permute-start(f32[2,32,256]{2,1,0:T(8,128)S(1)} %get-tuple-element.53), channel_id=1, source_target_pairs={{2,0},{4,2},{6,4},{8,6},{10,8},{12,10},{14,12},{16,14},{18,16},{20... | collective-permute-start | bytes 196616 | tf_op jit(solution)/shard_map/ppermute | solution.py:610
  120.6 1.8 pad_maximum_fusion.pressure_ref
  122.6 0.6 copy-done.27
  123.4 0.8 copy-done.12
  124.2 7.2 %shard_map.235 = (f32[4,288,256]{2,1,0:T(8,128)}, f32[8,288,256]{2,1,0:T(8,128)}, f32[2,144,128]{2,1,0:T(8,128)}) custom-call(f32[10,288,256]{2,1,0:T(8,128)} %pad_maximum_fusion.pressure_ref, f32[2,256,256]{2,1,0:T(8,128)} %get-tuple-element.28.low_r, f32[2,256,256]{2,1,0:T(8,128)} %get-tuple-element.29.high_r, f32[2,256,256]{2,1,0:T(8,128)} %copy-done.11, ...), custom_call_target="tpu_custom_call" | custom-call | flops 100000000 | bytes 9143296 | tf_op jit(solution)/shard_map/pallas_call | solution.py:299
  131.4 7.0 %collective-permute-start.20 = (f32[2,144,128]{2,1,0:T(8,128)}, f32[2,144,128]{2,1,0:T(8,128)S(1)}, u32[]{:S(2)}, u32[]{:S(2)}) collective-permute-start(f32[2,144,128]{2,1,0:T(8,128)} %get-tuple-element.31.own_ref.source_ref), channel_id=1, source_target_pairs={{0,2},{2,4},{4,6},{6,8},{8,10},{10,12},{12,14},{14,16},{16,18},{18... | collective-permute-start | bytes 442376 | tf_op jit(solution)/shard_map/ppermute | solution.py:607
  138.4 1.2 collective-permute-done.20.left_ref
  139.7 1.8 collective-permute-done.21.right_ref
  141.4 0.7 copy-done.24
  142.1 2.3 shard_map.236
  144.5 1.2 fusion.1
  145.6 1.9 collective-permute-start.27
  147.5 3.0 %collective-permute-start.28 = (f32[1,288,256]{2,1,0:T(8,128)S(1)}, f32[1,288,256]{2,1,0:T(8,128)S(1)}, u32[]{:S(2)}, u32[]{:S(2)}) collective-permute-start(f32[1,288,256]{2,1,0:T(8,128)S(1)} %get-tuple-element.43), channel_id=1, source_target_pairs={{2,0},{4,2},{6,4},{8,6},{10,8},{12,10},{14,12},{16,14},{18,16},{20... | collective-permute-start | bytes 884744 | tf_op jit(solution)/shard_map/ppermute | solution.py:610
  150.6 4.2 %collective-permute-done.27.left_ref = f32[1,288,256]{2,1,0:T(8,128)S(1)} collective-permute-done((f32[1,288,256]{2,1,0:T(8,128)S(1)}, f32[1,288,256]{2,1,0:T(8,128)S(1)}, u32[]{:S(2)}, u32[]{:S(2)}) %collective-permute-start.27) | collective-permute-done | bytes 294944 | tf_op jit(solution)/shard_map/ppermute | solution.py:607
  154.8 0.7 copy-done.19
  155.6 3.8 %shard_map.238 = (f32[2,256,256]{2,1,0:T(8,128)}, f32[2,256,256]{2,1,0:T(8,128)}) custom-call(f32[4,288,256]{2,1,0:T(8,128)} %get-tuple-element.34.base_ref, f32[1,288,256]{2,1,0:T(8,128)} %copy-done.19, f32[1,288,256]{2,1,0:T(8,128)} %copy-done.20, f32[8,288,256]{2,1,0:T(8,128)} %get-tuple-element.35.source_ref), custom_call_target="tpu_custom_call" | custom-call | flops 100000000 | bytes 5177344 | tf_op jit(solution)/shard_map/pallas_call | solution.py:299
  159.4 2.8 %collective-permute-start.30 = (f32[2,256,256]{2,1,0:T(8,128)}, f32[2,256,256]{2,1,0:T(8,128)S(1)}, u32[]{:S(2)}, u32[]{:S(2)}) collective-permute-start(f32[2,256,256]{2,1,0:T(8,128)} %get-tuple-element.37.high_ref.high_base), channel_id=1, source_target_pairs={{0,2},{2,4},{4,6},{6,8},{8,10},{10,12},{12,14},{14,16},{16,18},{18... | collective-permute-start | bytes 1572872 | tf_op jit(solution)/shard_map/ppermute | solution.py:607
  162.2 1.8 collective-permute-start.31
  164.7 4.4 %collective-permute-start.23 = (f32[1,144,128]{2,1,0:T(8,128)S(1)}, f32[1,144,128]{2,1,0:T(8,128)S(1)}, u32[]{:S(2)}, u32[]{:S(2)}) collective-permute-start(f32[1,144,128]{2,1,0:T(8,128)S(1)} %get-tuple-element.51), channel_id=1, source_target_pairs={{2,0},{4,2},{6,4},{8,6},{10,8},{12,10},{14,12},{16,14},{18,16},{20... | collective-permute-start | bytes 221192 | tf_op jit(solution)/shard_map/ppermute | solution.py:610
  169.1 1.1 broadcast_select_fusion
  170.2 1.3 collective-permute-done.30.left_ref
  172.0 1.5 collective-permute-start.29
  173.6 3.4 %shard_map.239 = (f32[2,256,256]{2,1,0:T(8,128)}, f32[2,256,256]{2,1,0:T(8,128)}) custom-call(f32[2,256,256]{2,1,0:T(8,128)} %get-tuple-element.36.low_ref.low_base, f32[2,256,256]{2,1,0:T(8,128)} %get-tuple-element.37.high_ref.high_base, f32[2,256,256]{2,1,0:T(8,128)} %copy-done.16, f32[2,256,256]{2,1,0:T(8,128)} %copy-done.17, ...), custom_call_target="tpu_custom_call" | custom-call | flops 100000000 | bytes 4194304 | tf_op jit(solution)/shard_map/pallas_call | solution.py:299
  177.0 0.8 collective-permute-start.32
  177.8 0.6 copy-done.26
  178.5 1.9 shard_map.237
  180.3 1.3 collective-permute-start.24
  181.6 32.6 %collective-permute-done.24 = f32[2,128,128]{2,1,0:T(8,128)S(1)} collective-permute-done((f32[2,128,128]{2,1,0:T(8,128)}, f32[2,128,128]{2,1,0:T(8,128)S(1)}, u32[]{:S(2)}, u32[]{:S(2)}) %collective-permute-start.24) | collective-permute-done | bytes 131104 | tf_op jit(solution)/shard_map/ppermute | solution.py:604
  214.2 1.0 maximum_select_fusion.own_mid
  215.2 1.1 collective-permute-start.25
  216.3 3.4 %collective-permute-start.26 = (f32[2,256,128]{2,1,0:T(8,128)S(1)}, f32[2,256,128]{2,1,0:T(8,128)S(1)}, u32[]{:S(2)}, u32[]{:S(2)}) collective-permute-start(f32[2,256,128]{2,1,0:T(8,128)S(1)} %maximum_select_fusion.own_mid), channel_id=1, source_target_pairs={{2,0},{4,2},{6,4},{8,6},{10,8},{12,10},{14,12},{16,14},{18,16},{20... | collective-permute-start | bytes 786440 | tf_op jit(solution)/shard_map/ppermute | solution.py:610
  219.7 4.1 %collective-permute-done.25.left_mid = f32[2,256,128]{2,1,0:T(8,128)S(1)} collective-permute-done((f32[2,256,128]{2,1,0:T(8,128)S(1)}, f32[2,256,128]{2,1,0:T(8,128)S(1)}, u32[]{:S(2)}, u32[]{:S(2)}) %collective-permute-start.25) | collective-permute-done | bytes 262176 | tf_op jit(solution)/shard_map/ppermute | solution.py:607
  223.9 0.6 copy-done.21
  225.1 14.7 %shard_map.240 = (f32[3,2,512,256]{3,2,1,0:T(8,128)}, f32[4,256,256]{2,1,0:T(8,128)}) custom-call(f32[16,128,128]{2,1,0:T(8,128)} %bitcast.7, f32[2,256,128]{2,1,0:T(8,128)} %copy-done.5, f32[2,256,128]{2,1,0:T(8,128)} %copy-done.21, f32[2,256,128]{2,1,0:T(8,128)} %copy-done.22, f32[2,256,256]{2,1,0:T(8,128)} %get-tuple-element.36.low_ref.low_base, ...), custom_call_target="tpu_custom_call" | custom-call | flops 1000000000 | bytes 14057472 | tf_op jit(solution)/shard_map/pallas_call | solution.py:299
  (115 shorter events, 3.6 us)
Async XLA Ops:
  7.2 8.4 %copy-start = (f32[3,2,512,256]{3,2,1,0:T(8,128)S(1)}, f32[3,2,512,256]{3,2,1,0:T(8,128)}, u32[]{:S(2)}) copy-start(f32[3,2,512,256]{3,2,1,0:T(8,128)} %velocity_ref.3) | copy-start | bytes 9437188
  7.2 216.7 %all-gather.3.cloned.1.call-start = ((), (), s32[]{:S(2)}) async-start(), calls=%async_computation | async-start | bytes 1081344 | tf_op jit(solution)/shard_map/all_gather | solution.py:715
  10.1 56.1 %collective-permute-start.6 = (f32[3,2,256,256]{3,2,1,0:T(8,128)}, f32[3,2,256,256]{3,2,1,0:T(8,128)}, u32[]{:S(2)}, u32[]{:S(2)}) collective-permute-start(f32[3,2,256,256]{3,2,1,0:T(8,128)} %constant_dynamic-slice_fusion.4), channel_id=1, source_target_pairs={{1,3},{0,30},{3,5},{2,0},{5,7},{4,2},{7,9},{6,4},{9,11},{8,6},{11,... | collective-permute-start | bytes 4718600 | tf_op jit(solution)/shard_map/ppermute | solution.py:628
  17.3 5.7 %copy-start.3 = (f32[4,256,256]{2,1,0:T(8,128)S(1)}, f32[4,256,256]{2,1,0:T(8,128)}, u32[]{:S(2)}) copy-start(f32[4,256,256]{2,1,0:T(8,128)} %param.25) | copy-start | bytes 3145732
  18.4 41.0 %copy-start.4 = (s32[2,512,256]{2,1,0:T(8,128)S(1)}, s32[2,512,256]{2,1,0:T(8,128)}, u32[]{:S(2)}) copy-start(s32[2,512,256]{2,1,0:T(8,128)} %solid_ref.1) | copy-start | bytes 3145732
  18.5 14.9 %collective-permute-start.3 = (f32[2,256,256]{2,1,0:T(8,128)S(1)}, f32[2,256,256]{2,1,0:T(8,128)S(1)}, u32[]{:S(2)}, u32[]{:S(2)}) collective-permute-start(f32[2,256,256]{2,1,0:T(8,128)S(1)} %dynamic-slice_bitcast_fusion.2), channel_id=1, source_target_pairs={{0,1},{1,0},{2,3},{3,2},{4,5},{5,4},{6,7},{7,6},{8,9},{9,8},{10,11... | collective-permute-start | bytes 1572872 | tf_op jit(solution)/shard_map/ppermute | solution.py:604
  19.7 24.9 %collective-permute-start.4 = (f32[2,256,256]{2,1,0:T(8,128)S(1)}, f32[2,256,256]{2,1,0:T(8,128)S(1)}, u32[]{:S(2)}, u32[]{:S(2)}) collective-permute-start(f32[2,256,256]{2,1,0:T(8,128)S(1)} %dynamic-slice_bitcast_fusion.1), channel_id=1, source_target_pairs={{0,1},{1,0},{2,3},{3,2},{4,5},{5,4},{6,7},{7,6},{8,9},{9,8},{10,11... | collective-permute-start | bytes 1572872 | tf_op jit(solution)/shard_map/ppermute | solution.py:604
  22.8 29.5 %collective-permute-start.5 = (f32[2,256,256]{2,1,0:T(8,128)S(1)}, f32[2,256,256]{2,1,0:T(8,128)S(1)}, u32[]{:S(2)}, u32[]{:S(2)}) collective-permute-start(f32[2,256,256]{2,1,0:T(8,128)S(1)} %dynamic-slice_bitcast_fusion), channel_id=1, source_target_pairs={{0,1},{1,0},{2,3},{3,2},{4,5},{5,4},{6,7},{7,6},{8,9},{9,8},{10,11... | collective-permute-start | bytes 1572872 | tf_op jit(solution)/shard_map/ppermute | solution.py:604
  33.4 28.1 %copy-start.30 = (f32[2,256,256]{2,1,0:T(8,128)}, f32[2,256,256]{2,1,0:T(8,128)S(1)}, u32[]{:S(2)}) copy-start(f32[2,256,256]{2,1,0:T(8,128)S(1)} %collective-permute-done.3.peer_u) | copy-start | bytes 1572868
  33.4 32.7 %collective-permute-start.7 = (f32[2,256,256]{2,1,0:T(8,128)S(1)}, f32[2,256,256]{2,1,0:T(8,128)S(1)}, u32[]{:S(2)}, u32[]{:S(2)}) collective-permute-start(f32[2,256,256]{2,1,0:T(8,128)S(1)} %collective-permute-done.3.peer_u), channel_id=1, source_target_pairs={{0,2},{1,31},{2,4},{3,1},{4,6},{5,3},{6,8},{7,5},{8,10},{9,7},{10,... | collective-permute-start | bytes 1572872 | tf_op jit(solution)/shard_map/ppermute | solution.py:630
  44.6 16.9 %copy-start.31 = (f32[2,256,256]{2,1,0:T(8,128)}, f32[2,256,256]{2,1,0:T(8,128)S(1)}, u32[]{:S(2)}) copy-start(f32[2,256,256]{2,1,0:T(8,128)S(1)} %collective-permute-done.4.peer_v) | copy-start | bytes 1572868
  44.6 21.5 %collective-permute-start.8 = (f32[2,256,256]{2,1,0:T(8,128)S(1)}, f32[2,256,256]{2,1,0:T(8,128)S(1)}, u32[]{:S(2)}, u32[]{:S(2)}) collective-permute-start(f32[2,256,256]{2,1,0:T(8,128)S(1)} %collective-permute-done.4.peer_v), channel_id=1, source_target_pairs={{0,2},{1,31},{2,4},{3,1},{4,6},{5,3},{6,8},{7,5},{8,10},{9,7},{10,... | collective-permute-start | bytes 1572872 | tf_op jit(solution)/shard_map/ppermute | solution.py:630
  52.2 9.2 %copy-start.32 = (f32[2,256,256]{2,1,0:T(8,128)}, f32[2,256,256]{2,1,0:T(8,128)S(1)}, u32[]{:S(2)}) copy-start(f32[2,256,256]{2,1,0:T(8,128)S(1)} %collective-permute-done.5.peer_w) | copy-start | bytes 1572868
  52.2 13.9 %collective-permute-start.9 = (f32[2,256,256]{2,1,0:T(8,128)S(1)}, f32[2,256,256]{2,1,0:T(8,128)S(1)}, u32[]{:S(2)}, u32[]{:S(2)}) collective-permute-start(f32[2,256,256]{2,1,0:T(8,128)S(1)} %collective-permute-done.5.peer_w), channel_id=1, source_target_pairs={{0,2},{1,31},{2,4},{3,1},{4,6},{5,3},{6,8},{7,5},{8,10},{9,7},{10,... | collective-permute-start | bytes 1572872 | tf_op jit(solution)/shard_map/ppermute | solution.py:630
  52.3 8.0 %collective-permute-start = (f32[4,32,256]{2,1,0:T(8,128)S(1)}, f32[4,32,256]{2,1,0:T(8,128)S(1)}, u32[]{:S(2)}, u32[]{:S(2)}) collective-permute-start(f32[4,32,256]{2,1,0:T(8,128)S(1)} %pad_maximum_fusion.2), channel_id=1, source_target_pairs={{0,1},{1,0},{2,3},{3,2},{4,5},{5,4},{6,7},{7,6},{8,9},{9,8},{10,11... | collective-permute-start | bytes 393224 | tf_op jit(solution)/shard_map/ppermute | solution.py:604
  60.3 4.7 %collective-permute-start.10 = (f32[3,2,8,256]{3,2,1,0:T(8,128)}, f32[3,2,8,256]{3,2,1,0:T(8,128)S(1)}, u32[]{:S(2)}, u32[]{:S(2)}) collective-permute-start(f32[3,2,8,256]{3,2,1,0:T(8,128)} %get-tuple-element.22), channel_id=1, source_target_pairs={{0,1},{1,0},{2,3},{3,2},{4,5},{5,4},{6,7},{7,6},{8,9},{9,8},{10,11... | collective-permute-start | bytes 147464 | tf_op jit(solution)/shard_map/ppermute | solution.py:604
  65.0 1.2 copy-start.36
  65.0 14.6 %collective-permute-start.11 = (s32[2,256,256]{2,1,0:T(8,128)S(1)}, s32[2,256,256]{2,1,0:T(8,128)S(1)}, u32[]{:S(2)}, u32[]{:S(2)}) collective-permute-start(s32[2,256,256]{2,1,0:T(8,128)S(1)} %get-tuple-element.47), channel_id=1, source_target_pairs={{0,1},{1,0},{2,3},{3,2},{4,5},{5,4},{6,7},{7,6},{8,9},{9,8},{10,11... | collective-permute-start | bytes 1572872 | tf_op jit(solution)/shard_map/ppermute | solution.py:604
  66.1 1.0 copy-start.34
  66.2 1.1 copy-start.35
  84.6 9.1 %copy-start.37 = (f32[4,8,256]{2,1,0:T(8,128)S(1)}, f32[4,8,256]{2,1,0:T(8,128)}, u32[]{:S(2)}) copy-start(f32[4,8,256]{2,1,0:T(8,128)} %get-tuple-element.27) | copy-start | bytes 98308
  84.6 14.5 %collective-permute-start.12 = (f32[2,256,256]{2,1,0:T(8,128)}, f32[2,256,256]{2,1,0:T(8,128)S(1)}, u32[]{:S(2)}, u32[]{:S(2)}) collective-permute-start(f32[2,256,256]{2,1,0:T(8,128)} %get-tuple-element.24.high_u), channel_id=1, source_target_pairs={{0,2},{2,4},{4,6},{6,8},{8,10},{10,12},{12,14},{14,16},{16,18},{18... | collective-permute-start | bytes 1572872 | tf_op jit(solution)/shard_map/ppermute | solution.py:607
  84.6 14.5 %collective-permute-start.13 = (f32[2,256,256]{2,1,0:T(8,128)}, f32[2,256,256]{2,1,0:T(8,128)S(1)}, u32[]{:S(2)}, u32[]{:S(2)}) collective-permute-start(f32[2,256,256]{2,1,0:T(8,128)} %get-tuple-element.23.low_u), channel_id=1, source_target_pairs={{2,0},{4,2},{6,4},{8,6},{10,8},{12,10},{14,12},{16,14},{18,16},{20... | collective-permute-start | bytes 1572872 | tf_op jit(solution)/shard_map/ppermute | solution.py:610
  89.2 26.9 %collective-permute-start.1 = (f32[3,288,256]{2,1,0:T(8,128)S(1)}, f32[3,288,256]{2,1,0:T(8,128)S(1)}, u32[]{:S(2)}, u32[]{:S(2)}) collective-permute-start(f32[3,288,256]{2,1,0:T(8,128)S(1)} %get-tuple-element.45), channel_id=1, source_target_pairs={{0,2},{2,4},{4,6},{6,8},{8,10},{10,12},{12,14},{14,16},{16,18},{18... | collective-permute-start | bytes 2654216 | tf_op jit(solution)/shard_map/ppermute | solution.py:607
  89.3 31.3 %collective-permute-start.2 = (f32[3,288,256]{2,1,0:T(8,128)S(1)}, f32[3,288,256]{2,1,0:T(8,128)S(1)}, u32[]{:S(2)}, u32[]{:S(2)}) collective-permute-start(f32[3,288,256]{2,1,0:T(8,128)S(1)} %get-tuple-element.46), channel_id=1, source_target_pairs={{2,0},{4,2},{6,4},{8,6},{10,8},{12,10},{14,12},{16,14},{18,16},{20... | collective-permute-start | bytes 2654216 | tf_op jit(solution)/shard_map/ppermute | solution.py:610
  93.7 5.4 %collective-permute-start.14 = (f32[4,8,256]{2,1,0:T(8,128)S(1)}, f32[4,8,256]{2,1,0:T(8,128)S(1)}, u32[]{:S(2)}, u32[]{:S(2)}) collective-permute-start(f32[4,8,256]{2,1,0:T(8,128)S(1)} %copy-done.37), channel_id=1, source_target_pairs={{0,1},{1,0},{2,3},{3,2},{4,5},{5,4},{6,7},{7,6},{8,9},{9,8},{10,11... | collective-permute-start | bytes 98312 | tf_op jit(solution)/shard_map/ppermute | solution.py:604
  99.9 0.8 copy-start.14
  103.9 7.9 %collective-permute-start.17 = (f32[4,32,256]{2,1,0:T(8,128)}, f32[4,32,256]{2,1,0:T(8,128)S(1)}, u32[]{:S(2)}, u32[]{:S(2)}) collective-permute-start(f32[4,32,256]{2,1,0:T(8,128)} %get-tuple-element.30), channel_id=1, source_target_pairs={{0,1},{1,0},{2,3},{3,2},{4,5},{5,4},{6,7},{7,6},{8,9},{9,8},{10,11... | collective-permute-start | bytes 393224 | tf_op jit(solution)/shard_map/ppermute | solution.py:604
  105.1 17.5 %collective-permute-start.15 = (f32[2,256,256]{2,1,0:T(8,128)}, f32[2,256,256]{2,1,0:T(8,128)S(1)}, u32[]{:S(2)}, u32[]{:S(2)}) collective-permute-start(f32[2,256,256]{2,1,0:T(8,128)} %get-tuple-element.29.high_r), channel_id=1, source_target_pairs={{0,2},{2,4},{4,6},{6,8},{8,10},{10,12},{12,14},{14,16},{16,18},{18... | collective-permute-start | bytes 1572872 | tf_op jit(solution)/shard_map/ppermute | solution.py:607
  111.7 10.9 %collective-permute-start.16 = (f32[2,256,256]{2,1,0:T(8,128)}, f32[2,256,256]{2,1,0:T(8,128)S(1)}, u32[]{:S(2)}, u32[]{:S(2)}) collective-permute-start(f32[2,256,256]{2,1,0:T(8,128)} %get-tuple-element.28.low_r), channel_id=1, source_target_pairs={{2,0},{4,2},{6,4},{8,6},{10,8},{12,10},{14,12},{16,14},{18,16},{20... | collective-permute-start | bytes 1572872 | tf_op jit(solution)/shard_map/ppermute | solution.py:610
  111.8 10.7 %copy-start.15 = (f32[4,32,256]{2,1,0:T(8,128)}, f32[4,32,256]{2,1,0:T(8,128)S(1)}, u32[]{:S(2)}) copy-start(f32[4,32,256]{2,1,0:T(8,128)S(1)} %collective-permute-done.17.edge_ref) | copy-start | bytes 393220
  111.8 10.8 %collective-permute-start.18 = (f32[2,32,256]{2,1,0:T(8,128)S(1)}, f32[2,32,256]{2,1,0:T(8,128)S(1)}, u32[]{:S(2)}, u32[]{:S(2)}) collective-permute-start(f32[2,32,256]{2,1,0:T(8,128)S(1)} %get-tuple-element.54), channel_id=1, source_target_pairs={{0,2},{2,4},{4,6},{6,8},{8,10},{10,12},{12,14},{14,16},{16,18},{18... | collective-permute-start | bytes 196616 | tf_op jit(solution)/shard_map/ppermute | solution.py:607
  116.1 6.5 %collective-permute-start.19 = (f32[2,32,256]{2,1,0:T(8,128)S(1)}, f32[2,32,256]{2,1,0:T(8,128)S(1)}, u32[]{:S(2)}, u32[]{:S(2)}) collective-permute-start(f32[2,32,256]{2,1,0:T(8,128)S(1)} %get-tuple-element.53), channel_id=1, source_target_pairs={{2,0},{4,2},{6,4},{8,6},{10,8},{12,10},{14,12},{16,14},{18,16},{20... | collective-permute-start | bytes 196616 | tf_op jit(solution)/shard_map/ppermute | solution.py:610
  122.4 28.1 %copy-start.1 = (f32[4,256,256]{2,1,0:T(8,128)S(1)}, f32[4,256,256]{2,1,0:T(8,128)}, u32[]{:S(2)}) copy-start(f32[4,256,256]{2,1,0:T(8,128)} %get-tuple-element.25.star_v) | copy-start | bytes 3145732
  122.6 0.8 copy-start.11
  123.4 0.8 copy-start.12
  131.4 8.2 %collective-permute-start.20 = (f32[2,144,128]{2,1,0:T(8,128)}, f32[2,144,128]{2,1,0:T(8,128)S(1)}, u32[]{:S(2)}, u32[]{:S(2)}) collective-permute-start(f32[2,144,128]{2,1,0:T(8,128)} %get-tuple-element.31.own_ref.source_ref), channel_id=1, source_target_pairs={{0,2},{2,4},{4,6},{6,8},{8,10},{10,12},{12,14},{14,16},{16,18},{18... | collective-permute-start | bytes 442376 | tf_op jit(solution)/shard_map/ppermute | solution.py:607
  138.4 3.0 %collective-permute-start.21 = (f32[2,144,128]{2,1,0:T(8,128)}, f32[2,144,128]{2,1,0:T(8,128)S(1)}, u32[]{:S(2)}, u32[]{:S(2)}) collective-permute-start(f32[2,144,128]{2,1,0:T(8,128)} %get-tuple-element.31.own_ref.source_ref), channel_id=1, source_target_pairs={{2,0},{4,2},{6,4},{8,6},{10,8},{12,10},{14,12},{16,14},{18,16},{20... | collective-permute-start | bytes 442376 | tf_op jit(solution)/shard_map/ppermute | solution.py:610
  139.6 1.8 copy-start.23
  144.4 19.6 %copy-start.2 = (f32[4,256,256]{2,1,0:T(8,128)S(1)}, f32[4,256,256]{2,1,0:T(8,128)}, u32[]{:S(2)}) copy-start(f32[4,256,256]{2,1,0:T(8,128)} %get-tuple-element.26.star_w) | copy-start | bytes 3145732
  145.6 9.2 %collective-permute-start.27 = (f32[1,288,256]{2,1,0:T(8,128)S(1)}, f32[1,288,256]{2,1,0:T(8,128)S(1)}, u32[]{:S(2)}, u32[]{:S(2)}) collective-permute-start(f32[1,288,256]{2,1,0:T(8,128)S(1)} %get-tuple-element.44), channel_id=1, source_target_pairs={{0,2},{2,4},{4,6},{6,8},{8,10},{10,12},{12,14},{14,16},{16,18},{18... | collective-permute-start | bytes 884744 | tf_op jit(solution)/shard_map/ppermute | solution.py:607
  147.5 7.3 %collective-permute-start.28 = (f32[1,288,256]{2,1,0:T(8,128)S(1)}, f32[1,288,256]{2,1,0:T(8,128)S(1)}, u32[]{:S(2)}, u32[]{:S(2)}) collective-permute-start(f32[1,288,256]{2,1,0:T(8,128)S(1)} %get-tuple-element.43), channel_id=1, source_target_pairs={{2,0},{4,2},{6,4},{8,6},{10,8},{12,10},{14,12},{16,14},{18,16},{20... | collective-permute-start | bytes 884744 | tf_op jit(solution)/shard_map/ppermute | solution.py:610
  150.5 14.1 %copy-start.6 = (f32[2,144,128]{2,1,0:T(8,128)S(1)}, f32[2,144,128]{2,1,0:T(8,128)}, u32[]{:S(2)}) copy-start(f32[2,144,128]{2,1,0:T(8,128)} %get-tuple-element.33.base_ref) | copy-start | bytes 442372
  154.8 0.8 copy-start.20
  159.4 12.1 %collective-permute-start.30 = (f32[2,256,256]{2,1,0:T(8,128)}, f32[2,256,256]{2,1,0:T(8,128)S(1)}, u32[]{:S(2)}, u32[]{:S(2)}) collective-permute-start(f32[2,256,256]{2,1,0:T(8,128)} %get-tuple-element.37.high_ref.high_base), channel_id=1, source_target_pairs={{0,2},{2,4},{4,6},{6,8},{8,10},{10,12},{12,14},{14,16},{16,18},{18... | collective-permute-start | bytes 1572872 | tf_op jit(solution)/shard_map/ppermute | solution.py:607
  162.2 9.9 %collective-permute-start.31 = (f32[2,256,256]{2,1,0:T(8,128)}, f32[2,256,256]{2,1,0:T(8,128)S(1)}, u32[]{:S(2)}, u32[]{:S(2)}) collective-permute-start(f32[2,256,256]{2,1,0:T(8,128)} %get-tuple-element.36.low_ref.low_base), channel_id=1, source_target_pairs={{2,0},{4,2},{6,4},{8,6},{10,8},{12,10},{14,12},{16,14},{18,16},{20... | collective-permute-start | bytes 1572872 | tf_op jit(solution)/shard_map/ppermute | solution.py:610
  164.0 52.2 %collective-permute-start.33 = (f32[2,256,256]{2,1,0:T(8,128)S(1)}, f32[2,256,256]{2,1,0:T(8,128)S(1)}, u32[]{:S(2)}, u32[]{:S(2)}) collective-permute-start(f32[2,256,256]{2,1,0:T(8,128)S(1)} %constant_dynamic-slice_fusion.1), channel_id=1, source_target_pairs={{0,1},{1,0},{2,3},{3,2},{4,5},{5,4},{6,7},{7,6},{8,9},{9,8},{10,11... | collective-permute-start | bytes 1572872 | tf_op jit(solution)/shard_map/ppermute | solution.py:604
  164.6 12.4 %collective-permute-start.22 = (f32[1,144,128]{2,1,0:T(8,128)S(1)}, f32[1,144,128]{2,1,0:T(8,128)S(1)}, u32[]{:S(2)}, u32[]{:S(2)}) collective-permute-start(f32[1,144,128]{2,1,0:T(8,128)S(1)} %get-tuple-element.52), channel_id=1, source_target_pairs={{0,2},{2,4},{4,6},{6,8},{8,10},{10,12},{12,14},{14,16},{16,18},{18... | collective-permute-start | bytes 221192 | tf_op jit(solution)/shard_map/ppermute | solution.py:607
  164.7 13.2 %collective-permute-start.23 = (f32[1,144,128]{2,1,0:T(8,128)S(1)}, f32[1,144,128]{2,1,0:T(8,128)S(1)}, u32[]{:S(2)}, u32[]{:S(2)}) collective-permute-start(f32[1,144,128]{2,1,0:T(8,128)S(1)} %get-tuple-element.51), channel_id=1, source_target_pairs={{2,0},{4,2},{6,4},{8,6},{10,8},{12,10},{14,12},{16,14},{18,16},{20... | collective-permute-start | bytes 221192 | tf_op jit(solution)/shard_map/ppermute | solution.py:610
  171.5 2.0 copy-start.16
  171.5 48.2 %collective-permute-start.34 = (f32[2,256,256]{2,1,0:T(8,128)S(1)}, f32[2,256,256]{2,1,0:T(8,128)S(1)}, u32[]{:S(2)}, u32[]{:S(2)}) collective-permute-start(f32[2,256,256]{2,1,0:T(8,128)S(1)} %constant_dynamic-slice_fusion), channel_id=1, source_target_pairs={{0,1},{1,0},{2,3},{3,2},{4,5},{5,4},{6,7},{7,6},{8,9},{9,8},{10,11... | collective-permute-start | bytes 1572872 | tf_op jit(solution)/shard_map/ppermute | solution.py:604
  172.0 1.6 copy-start.17
  172.0 51.8 %collective-permute-start.29 = (f32[2,256,256]{2,1,0:T(8,128)S(1)}, f32[2,256,256]{2,1,0:T(8,128)S(1)}, u32[]{:S(2)}, u32[]{:S(2)}) collective-permute-start(f32[2,256,256]{2,1,0:T(8,128)S(1)} %broadcast_select_fusion), channel_id=1, source_target_pairs={{0,1},{1,0},{2,3},{3,2},{4,5},{5,4},{6,7},{7,6},{8,9},{9,8},{10,11... | collective-permute-start | bytes 1572872 | tf_op jit(solution)/shard_map/ppermute | solution.py:604
  177.0 0.8 copy-start.25
  177.0 46.9 %collective-permute-start.32 = (f32[2,256,256]{2,1,0:T(8,128)}, f32[2,256,256]{2,1,0:T(8,128)S(1)}, u32[]{:S(2)}, u32[]{:S(2)}) collective-permute-start(f32[2,256,256]{2,1,0:T(8,128)} %get-tuple-element.39), channel_id=1, source_target_pairs={{0,1},{1,0},{2,3},{3,2},{4,5},{5,4},{6,7},{7,6},{8,9},{9,8},{10,11... | collective-permute-start | bytes 1572872 | tf_op jit(solution)/shard_map/ppermute | solution.py:604
  180.3 33.8 %collective-permute-start.24 = (f32[2,128,128]{2,1,0:T(8,128)}, f32[2,128,128]{2,1,0:T(8,128)S(1)}, u32[]{:S(2)}, u32[]{:S(2)}) collective-permute-start(f32[2,128,128]{2,1,0:T(8,128)} %shard_map.237), channel_id=1, source_target_pairs={{0,1},{1,0},{2,3},{3,2},{4,5},{5,4},{6,7},{7,6},{8,9},{9,8},{10,11... | collective-permute-start | bytes 393224 | tf_op jit(solution)/shard_map/ppermute | solution.py:604
  215.2 8.7 %copy-start.5 = (f32[2,256,128]{2,1,0:T(8,128)}, f32[2,256,128]{2,1,0:T(8,128)S(1)}, u32[]{:S(2)}) copy-start(f32[2,256,128]{2,1,0:T(8,128)S(1)} %maximum_select_fusion.own_mid) | copy-start | bytes 786436
  215.2 8.7 %collective-permute-start.25 = (f32[2,256,128]{2,1,0:T(8,128)S(1)}, f32[2,256,128]{2,1,0:T(8,128)S(1)}, u32[]{:S(2)}, u32[]{:S(2)}) collective-permute-start(f32[2,256,128]{2,1,0:T(8,128)S(1)} %maximum_select_fusion.own_mid), channel_id=1, source_target_pairs={{0,2},{2,4},{4,6},{6,8},{8,10},{10,12},{12,14},{14,16},{16,18},{18... | collective-permute-start | bytes 786440 | tf_op jit(solution)/shard_map/ppermute | solution.py:607
  216.3 7.7 %copy-start.7 = (f32[2,256,256]{2,1,0:T(8,128)}, f32[2,256,256]{2,1,0:T(8,128)S(1)}, u32[]{:S(2)}) copy-start(f32[2,256,256]{2,1,0:T(8,128)S(1)} %collective-permute-done.33.peer_v) | copy-start | bytes 1572868
  216.3 7.6 %collective-permute-start.26 = (f32[2,256,128]{2,1,0:T(8,128)S(1)}, f32[2,256,128]{2,1,0:T(8,128)S(1)}, u32[]{:S(2)}, u32[]{:S(2)}) collective-permute-start(f32[2,256,128]{2,1,0:T(8,128)S(1)} %maximum_select_fusion.own_mid), channel_id=1, source_target_pairs={{2,0},{4,2},{6,4},{8,6},{10,8},{12,10},{14,12},{16,14},{18,16},{20... | collective-permute-start | bytes 786440 | tf_op jit(solution)/shard_map/ppermute | solution.py:610
  219.7 4.2 %copy-start.8 = (f32[2,256,256]{2,1,0:T(8,128)}, f32[2,256,256]{2,1,0:T(8,128)S(1)}, u32[]{:S(2)}) copy-start(f32[2,256,256]{2,1,0:T(8,128)S(1)} %collective-permute-done.34.peer_w) | copy-start | bytes 1572868
  223.8 0.8 copy-start.22
  223.9 1.0 copy-start.9
  223.9 1.2 copy-start.10
  (10 other events, 7.0 us)
Sparse Core Ops, SparseCore 0:
  144.6 60.1 all-gather.2

commit v2 on v0

--- a/solution.py
+++ b/solution.py
@@ -1,8 +1,13 @@
+import functools
 import math
 
 import jax
 import jax.numpy as jnp
+import ml_dtypes
+import numpy as np
 from jax import lax
+from jax.experimental import pallas as pl
+from jax.experimental.pallas import tpu as pltpu
 from jax.sharding import PartitionSpec as P
 
 LEVELS = 3
@@ -175,6 +180,750 @@
     return (corrected, potential)
 
 
+HALO = 16
+weight = relax_weight / 6.0
+bf16 = jnp.bfloat16
+f32 = jnp.float32
+VMEM = pl.BlockSpec(memory_space=pltpu.VMEM)
+ANY = pl.BlockSpec(memory_space=pl.ANY)
+
+
+def wave_tables(count):
+    index = np.arange(count)
+    angles = 2.0 * np.pi * (np.outer(index, index) % count) / count
+    theta = 2.0 * np.pi * index / count
+    first_wave = (14.0 / 9.0 * np.sin(theta) + np.sin(2.0 * theta) / 18.0) / (
+        1.0 + 2.0 / 3.0 * np.cos(theta)
+    )
+    second_wave = (
+        24.0 / 11.0 * (1.0 - np.cos(theta)) + 3.0 / 22.0 * (1.0 - np.cos(2.0 * theta))
+    ) / (1.0 + 4.0 / 11.0 * np.cos(theta))
+    cosines, sines = (np.cos(angles), np.sin(angles))
+    first = ((cosines * first_wave) @ sines.T - (sines * first_wave) @ cosines.T) / count
+    second = -((cosines * second_wave) @ cosines.T + (sines * second_wave) @ sines.T) / count
+    return (first, second)
+
+
+def high_low(table):
+    high = table.astype(np.float32).astype(ml_dtypes.bfloat16)
+    low = (table - high.astype(np.float64)).astype(np.float32).astype(ml_dtypes.bfloat16)
+    return (high, low)
+
+
+def half_tables(count):
+    first, second = wave_tables(count)
+    half = count // 2
+    index = np.arange(half)
+    root_first = (math.sqrt(5.0) - 3.0) / 2.0
+    root_second = (math.sqrt(105.0) - 11.0) / 4.0
+    basis = np.zeros((8, half))
+    basis[0, 0] = 1.0
+    basis[1, -1] = 1.0
+    basis[2] = root_first**index
+    basis[3] = basis[2][::-1]
+    basis[4] = root_second**index
+    basis[5] = basis[4][::-1]
+    spread = []
+    for table, used in ((first, (0, 1, 2, 3)), (second, (0, 1, 4, 5))):
+        solved = np.linalg.lstsq(basis[list(used)].T, table[:half, half:].T, rcond=None)[0].T
+        wide = np.zeros((half, 8))
+        wide[:, list(used)] = solved
+        spread.append(wide)
+    own = np.concatenate([first[:half, :half], second[:half, :half]], axis=0)
+    return (own, np.concatenate(spread, axis=0), basis, first)
+
+
+def split(value):
+    high = value.astype(bf16)
+    low = (value - high.astype(f32)).astype(bf16)
+    return (high, low)
+
+
+def dot(left, right):
+    return jnp.dot(left, right, preferred_element_type=f32)
+
+
+def dot_left(table_high, table_low, value):
+    high, low = split(value)
+    return dot(table_high, high) + (dot(table_high, low) + dot(table_low, high))
+
+
+def dot_right(value, table_high, table_low):
+    high, low = split(value)
+    return dot(high, table_high) + (dot(low, table_high) + dot(high, table_low))
+
+
+def pick_left(zero_one, value):
+    high, low = split(value)
+    return dot(zero_one, high) + dot(zero_one, low)
+
+
+def pick_right(value, zero_one):
+    high, low = split(value)
+    return dot(high, zero_one) + dot(low, zero_one)
+
+
+def summary(basis_both, value):
+    high, low = split(value)
+    main = dot(basis_both, high)
+    rest = dot(basis_both, low)
+    return main[:8] + main[8:] + rest[:8]
+
+
+def summary_operand(value):
+    high = value.astype(bf16).astype(f32)
+    return jnp.concatenate([high, value - high, high, jnp.zeros_like(high)], axis=0).astype(bf16)
+
+
+def turn(value, shift, axis):
+    return pltpu.roll(value, shift % value.shape[axis], axis)
+
+
+def cross_sum(value):
+    return (turn(value, 1, 0) + turn(value, -1, 0)) + (turn(value, 1, 1) + turn(value, -1, 1))
+
+
+def first_of(values):
+    return (8.0 * (values[3] - values[1]) - (values[4] - values[0])) * (1.0 / 12.0)
+
+
+def second_of(values):
+    return (
+        16.0 * (values[3] + values[1]) - (values[4] + values[0]) - 30.0 * values[2]
+    ) * (1.0 / 12.0)
+
+
+def kernel_call(body, outs, scratch, specs, flops, *args, grid=None, out_specs=None, aliases=None):
+    total = sum(math.prod(a.shape) * a.dtype.itemsize for a in args)
+    total += sum(4 * math.prod(s) for s in outs)
+    options = {} if grid is None else {"grid": grid}
+    if aliases is not None:
+        options["input_output_aliases"] = aliases
+    return pl.pallas_call(
+        body,
+        out_shape=[jax.ShapeDtypeStruct(s, f32) for s in outs],
+        in_specs=specs,
+        out_specs=[VMEM] * len(outs) if out_specs is None else out_specs,
+        scratch_shapes=scratch,
+        compiler_params=pltpu.CompilerParams(vmem_limit_bytes=56 * 1024 * 1024),
+        cost_estimate=pl.CostEstimate(flops=flops, bytes_accessed=total if flops > 1 else 1, transcendentals=0),
+        **options,
+    )(*args)
+
+
+def mirror(side, index, count):
+    return index + side * (count - 1 - 2 * index)
+
+
+def sign_of(side):
+    return (1 - 2 * side).astype(f32)
+
+
+def transverse(u, v, w, value, other_sum, rows_high, rows_low, spread, depth_high, depth_low):
+    half, width = value.shape
+    high, low = split(value)
+    across = (
+        dot(rows_high[...], high)
+        + (dot(rows_high[...], low) + dot(rows_low[...], high))
+        + dot(spread[...], summary_operand(other_sum))
+    )
+    along = dot(high, depth_high[...]) + (dot(low, depth_high[...]) + dot(high, depth_low[...]))
+    advect = v * across[:half] + w * along[:, :width]
+    return value + time_step * (viscosity * (across[half:] + along[:, width:]) - advect)
+
+
+def own_planes_kernel(
+    velocity_ref, basis_ref, rows_high, rows_low, spread, depth_high, depth_low, out_ref, sent_ref
+):
+    side = lax.axis_index("group")
+    half = basis_ref.shape[1]
+    own = pl.ds(pl.multiple_of(side * half, half), half)
+    other = pl.ds(pl.multiple_of((1 - side) * half, half), half)
+    u, v, w = (velocity_ref[c, 0, own] for c in range(3))
+    sent_ref[0, :half] = velocity_ref[2, 0, other]
+    for c in range(3):
+        value = velocity_ref[c, 0, own]
+        kept = summary(basis_ref[...], velocity_ref[c, 0, other])
+        sent_ref[0, half + 8 * c : half + 8 * c + 8] = summary(basis_ref[...], value)
+        out_ref[c, 0] = transverse(u, v, w, value, kept, rows_high, rows_low, spread, depth_high, depth_low)
+
+
+def peer_planes_kernel(
+    uv_ref, w_ref, rows_high, rows_low, spread, depth_high, depth_low, out_ref
+):
+    half = uv_ref.shape[2]
+    u, v, w = (uv_ref[0, 0], uv_ref[1, 0], w_ref[0, :half])
+    for c in range(3):
+        other_sum = w_ref[0, half + 8 * c : half + 8 * c + 8]
+        out_ref[c, 0] = transverse(
+            u, v, w, (u, v, w)[c], other_sum, rows_high, rows_low, spread, depth_high, depth_low
+        )
+
+
+def star_planes(side, planes, raws, solids, u_of, outs):
+    sign = sign_of(side) * (time_step / 12.0)
+    for plane in range(4):
+        index = mirror(side, plane % 2, 2)
+        keep = 1.0 - solids[plane // 2][index].astype(f32)
+        near = planes[plane : plane + 5]
+        first = 8.0 * (near[3] - near[1]) - (near[4] - near[0])
+        second = 16.0 * (near[3] + near[1]) - (near[4] + near[0]) - 30.0 * near[2]
+        raw = raws[plane // 2][index]
+        outs[plane // 2][plane % 2] = (
+            raw + (time_step * viscosity / 12.0) * second - (u_of(plane) * sign) * first
+        ) * keep
+
+
+def eight(side, groups):
+    return [group[mirror(side, k, 2)] for group in groups for k in range(2)]
+
+
+def star_u_kernel(raw_own, raw_peer, own_ref, one_ref, peers, others, solid_own, solid_peer, near_ref, far_ref):
+    side = lax.axis_index("group")
+    planes = eight(side, (others.at[0], own_ref.at[0], peers.at[0], one_ref.at[0]))
+    star_planes(
+        side, planes, (raw_own.at[0], raw_peer.at[0]), (solid_own, solid_peer),
+        lambda plane: planes[plane + 2], (near_ref, far_ref),
+    )
+
+
+def star_vw_kernel(
+    raw_own, raw_peer, own_ref, one_ref, peers, peer_w, others, other_w, solid_own, solid_peer, basis_ref,
+    near_v, far_v, near_w, far_w, sum_ref,
+):
+    side = lax.axis_index("group")
+    step = pl.program_id(0)
+
+    def u_of(plane):
+        return (own_ref if plane < 2 else peers)[0, mirror(side, plane % 2, 2)]
+
+    for c, peer, other, outs in (
+        (1, peers.at[1], others.at[0], (near_v, far_v)),
+        (2, peer_w, other_w, (near_w, far_w)),
+    ):
+        planes = eight(side, (other, own_ref.at[c], peer, one_ref.at[c]))
+        star_planes(side, planes, (raw_own.at[c], raw_peer.at[c]), (solid_own, solid_peer), u_of, outs)
+
+    @pl.when(step == 0)
+    def _():
+        sum_ref[...] = jnp.zeros_like(sum_ref)
+
+    for plane in range(4):
+        sum_ref[plane] += summary(basis_ref[0], (near_v if plane < 2 else far_v)[plane % 2])
+
+
+def cross_kernel(near_v, far_v, near_w, far_w, rows_high, rows_low, depth_high, depth_low, out_ref):
+    half = near_v.shape[1]
+    for plane in range(4):
+        v, w = ((near_v, near_w) if plane < 2 else (far_v, far_w))
+        out_ref[plane] = dot_left(rows_high[:half], rows_low[:half], v[plane % 2]) + dot_right(
+            w[plane % 2], depth_high[...], depth_low[...]
+        )
+
+
+def source_kernel(
+    near_u, far_u, left_ref, right_ref, cross_ref, sum_ref, spread, near_r, far_r, head, tail
+):
+    sign = sign_of(lax.axis_index("group"))
+    rows = cross_ref.shape[1]
+    step = pl.program_id(0)
+    planes = [ref[k] for ref in (left_ref, near_u, far_u, right_ref) for k in range(2)]
+    values = []
+    for plane in range(4):
+        value = sign * first_of(planes[plane : plane + 5]) + cross_ref[plane]
+        value = value + dot(spread[...], summary_operand(sum_ref[3 - plane]))
+        (near_r if plane < 2 else far_r)[plane % 2] = value
+        values.append(value)
+
+    @pl.when(step == 0)
+    def _():
+        for plane in range(4):
+            head[plane] = values[plane][:HALO]
+
+    @pl.when(step == pl.num_programs(0) - 1)
+    def _():
+        for plane in range(4):
+            tail[plane] = values[plane][rows - HALO :]
+
+
+def fine_kernel(
+    pressure_tall, pressure_left, pressure_right,
+    near_r, far_r, left_ref, right_ref, edge_ref, left_edge, right_edge, depth_pick, rows_pick,
+    base_ref, coarse_ref, ahead_ref, behind_ref, source_ref, pressure_ref, one, two,
+):
+    side = lax.axis_index("group")
+    half = near_r.shape[1]
+
+    def fill(target, at, body, edge):
+        target[at, HALO : HALO + half] = body
+        target[at, :HALO] = edge[HALO:]
+        target[at, HALO + half :] = edge[:HALO]
+
+    for plane in range(2):
+        fill(source_ref, plane, left_ref[plane], left_edge[1 - plane])
+        fill(source_ref, 2 + plane, near_r[plane], edge_ref[3 - plane])
+        fill(source_ref, 4 + plane, far_r[plane], edge_ref[1 - plane])
+        fill(source_ref, 6 + plane, right_ref[plane], right_edge[1 - plane])
+    for plane in range(3):
+        at = mirror(side, plane, 3)
+        pressure_ref[plane] = pressure_left[at]
+        pressure_ref[7 + plane] = pressure_right[at]
+    for plane in range(4):
+        pressure_ref[3 + plane] = pressure_tall[mirror(side, plane, 4)]
+    for k in range(8):
+        centre = pressure_ref[k + 1]
+        total = pressure_ref[k] + pressure_ref[k + 2] + cross_sum(centre)
+        one[k] = centre + weight * (total - 6.0 * centre - source_ref[k])
+    for k in range(6):
+        centre = one[k + 1]
+        total = one[k] + one[k + 2] + cross_sum(centre)
+        two[k] = centre + weight * (total - 6.0 * centre - source_ref[k + 1])
+    for pair in range(2):
+        left = []
+        for k in (2 * pair, 2 * pair + 1):
+            centre = two[k + 1]
+            total = two[k] + two[k + 2] + cross_sum(centre)
+            residual = source_ref[k + 2] - (total - 6.0 * centre)
+            base_ref[k] = centre - weight * residual
+            left.append(residual)
+        coarse = 0.125 * pick_left(rows_pick[...], pick_right(left[0] + left[1], depth_pick[...]))
+        coarse_ref[pair] = coarse
+        rows, width = coarse.shape
+        ahead_ref[:rows, width * pair : width * (pair + 1)] = coarse
+        behind_ref[:rows, width * pair : width * (pair + 1)] = coarse
+    ahead_ref[rows:] = base_ref[3]
+    behind_ref[rows:] = base_ref[0]
+
+
+def middle_kernel(own_ref, left_ref, right_ref, depth_pick, rows_pick, base_ref, coarse_ref, one, two):
+    rows, width = own_ref.shape[1:]
+    source = []
+    for ref in (left_ref, own_ref, right_ref):
+        for k in range(2):
+            source.append(ref[k] if ref is own_ref else ref[:rows, width * k : width * (k + 1)])
+    for k in range(6):
+        one[k] = (-4.0 * weight) * source[k]
+    for k in range(4):
+        centre = one[k + 1]
+        total = one[k] + one[k + 2] + cross_sum(centre)
+        two[k] = centre + weight * (total - 6.0 * centre - 4.0 * source[k + 1])
+    left = []
+    for k in range(2):
+        centre = two[k + 1]
+        total = two[k] + two[k + 2] + cross_sum(centre)
+        residual = source[k + 2] - 0.25 * (total - 6.0 * centre)
+        base_ref[k] = centre - (4.0 * weight) * residual
+        left.append(residual)
+    width = own_ref.shape[2]
+    wide = pick_right(left[0] + left[1], depth_pick[...])
+    count = coarse_ref.shape[0]
+    coarse_ref[...] = 0.125 * (
+        pick_left(rows_pick[:count], wide[:, :width]) + pick_left(rows_pick[count:], wide[:, width:])
+    )
+
+
+def middle_base_kernel(base_ref, left_ref, right_ref, source_ref, out_ref):
+    rows = out_ref.shape[1]
+    planes = [left_ref[0], base_ref[0], base_ref[1], right_ref[0]]
+    for k in range(2):
+        centre = planes[k + 1]
+        total = planes[k] + planes[k + 2] + cross_sum(centre)
+        value = centre + weight * (total - 6.0 * centre - 4.0 * source_ref[k])
+        out_ref[k] = value[HALO // 2 : HALO // 2 + rows]
+
+
+def base_kernel(base_ref, left_ref, right_ref, near_r, far_r, near_ref, far_ref):
+    rows = near_ref.shape[1]
+    skip = left_ref.shape[0] - base_ref.shape[1]
+    for k in range(4):
+        before = left_ref[skip:] if k == 0 else base_ref[k - 1]
+        after = right_ref[skip:] if k == 3 else base_ref[k + 1]
+        centre = base_ref[k]
+        total = before + after + cross_sum(centre)
+        value = (centre + weight * (total - 6.0 * centre))[HALO : HALO + rows]
+        source, out = ((near_r, near_ref) if k < 2 else (far_r, far_ref))
+        out[k % 2] = value - weight * source[k % 2]
+
+
+def stream_kernel(near_ref, far_ref, left_ref, right_ref, near_u, far_u, own_ref, sent_ref):
+    sign = sign_of(lax.axis_index("group"))
+    planes = [ref[k] for ref in (left_ref, near_ref, far_ref, right_ref) for k in range(2)]
+    for plane in range(4):
+        star = (near_u if plane < 2 else far_u)[plane % 2]
+        (own_ref if plane < 2 else sent_ref)[plane % 2] = star - sign * first_of(planes[plane : plane + 5])
+
+
+def coarsest_kernel(all_ref, mid_depth, mid_rows, out_ref, source, one, two):
+    place = lax.axis_index("tunnel")
+    step = 1 - 2 * lax.axis_index("group")
+    count = all_ref.shape[0] // 2
+    quarter, width = all_ref.shape[1:]
+    lower = lax.broadcasted_iota(jnp.int32, (quarter, width), 1) < width // 2
+    for k in range(11):
+        plane = lax.rem(place + step * (k - 5) + 2 * count, count)
+        for part in range(2):
+            packed = all_ref[2 * plane + part]
+            turned = turn(packed, width // 2, 1)
+            source[k, 2 * part * quarter : (2 * part + 1) * quarter] = jnp.where(lower, packed, turned)
+            source[k, (2 * part + 1) * quarter : (2 * part + 2) * quarter] = jnp.where(lower, turned, packed)
+    for k in range(11):
+        one[k] = (-16.0 * weight) * source[k]
+    source_at, target = (one, two)
+    for sweep_index in range(1, COARSE_SWEEPS):
+        for k in range(sweep_index, 11 - sweep_index):
+            centre = source_at[k]
+            total = source_at[k - 1] + source_at[k + 1] + cross_sum(centre)
+            target[k] = centre + weight * (total - 6.0 * centre - 16.0 * source[k])
+        source_at, target = (target, source_at)
+    for k in range(5):
+        out_ref[k] = pick_left(mid_rows[...], pick_right(source_at[k + 3], mid_depth[...]))
+
+
+def correction_kernel(
+    spread_ref, own_mid, left_mid, right_mid,
+    near_base, far_base, peer_base, near_v, near_w, peer_vw, solid_ref,
+    sum_high, sum_low, diff_high, diff_low, depth_high, depth_low, fine_depth, fine_rows,
+    out_ref, potential_ref, base, mid, fine, first_sweep, delta, section,
+):
+    side = lax.axis_index("group")
+    sign = sign_of(side)
+    half = near_v.shape[1]
+    own_rows = pl.ds(pl.multiple_of(side * half, half), half)
+    peer_rows = pl.ds(pl.multiple_of((1 - side) * half, half), half)
+    mid_half = own_mid.shape[2]
+    own_mid_rows = pl.ds(pl.multiple_of(side * mid_half, mid_half), mid_half)
+    peer_mid_rows = pl.ds(pl.multiple_of((1 - side) * mid_half, mid_half), mid_half)
+    for k in range(5):
+        held = (left_mid, own_mid, right_mid)[k // 2]
+        base[k, own_mid_rows] = held[0, k % 2]
+        base[k, peer_mid_rows] = held[1, 1 - k % 2]
+    for k in range(1, 8):
+        centre = spread_ref[k // 2]
+        total = spread_ref[(k - 1) // 2] + spread_ref[(k + 1) // 2] + cross_sum(centre)
+        mid[k] = centre + weight * (total - 6.0 * centre)
+    for k in range(5):
+        centre = mid[k + 2]
+        total = mid[k + 1] + mid[k + 3] + cross_sum(centre)
+        value = base[k] + centre + weight * (total - 6.0 * centre)
+        fine[k] = pick_left(fine_rows[...], pick_right(value, fine_depth[...]))
+    for j in range(5):
+        centre = fine[j]
+        shared = centre + weight * (centre + cross_sum(centre) - 6.0 * centre)
+        if j > 0:
+            first_sweep[2 * j - 1] = shared + weight * fine[j - 1]
+        if j < 4:
+            first_sweep[2 * j] = shared + weight * fine[j + 1]
+    for k in range(6):
+        centre = first_sweep[k + 1]
+        total = first_sweep[k] + first_sweep[k + 2] + cross_sum(centre)
+        delta[k] = centre + weight * (total - 6.0 * centre)
+    for k in range(4):
+        smooth_part = (near_base if k < 2 else far_base)[k % 2]
+        potential_ref[mirror(side, k, 4)] = smooth_part + delta[k + 2, own_rows]
+    for k in range(2):
+        at = 2 + k
+        index = mirror(side, k, 2)
+        section[peer_rows] = delta[at, peer_rows] + peer_base[1 - k]
+        section[own_rows] = delta[at, own_rows] + near_base[k]
+        value = section[...]
+        keep = 1.0 - solid_ref[index].astype(f32)
+        out_ref[0, index] = sign * first_of([delta[at + offset] for offset in range(-2, 3)])
+        out_ref[2, index, own_rows] = near_w[k]
+        out_ref[2, index, peer_rows] = peer_vw[1, 1 - k]
+        out_ref[2, index] = (out_ref[2, index] - dot_right(value, depth_high[...], depth_low[...])) * keep
+        out_ref[1, index, own_rows] = near_v[k]
+        out_ref[1, index, peer_rows] = peer_vw[0, 1 - k]
+        top, low = (value[:half], value[half:])
+        even = dot_left(sum_high[...], sum_low[...], top + low)
+        odd = dot_left(diff_high[...], diff_low[...], top - low)
+        out_ref[1, index, :half] = (out_ref[1, index, :half] - (even + odd)) * keep[:half]
+        out_ref[1, index, half:] = (out_ref[1, index, half:] - (even - odd)) * keep[half:]
+
+
+def stream_correction_kernel(gradient_ref, own_u, peer_u, solid_ref, out_ref):
+    side = lax.axis_index("group")
+    half = own_u.shape[1]
+    index = pl.program_id(0)
+    k = mirror(side, index, 2)
+    own_rows = pl.ds(pl.multiple_of(side * half, half), half)
+    peer_rows = pl.ds(pl.multiple_of((1 - side) * half, half), half)
+    for rows, value in ((own_rows, own_u[k]), (peer_rows, peer_u[1 - k])):
+        keep = 1.0 - solid_ref[0, rows].astype(f32)
+        out_ref[0, 0, rows] = (value - gradient_ref[0, 0, rows]) * keep
+
+
+def pair_sums(fine, coarse):
+    return (np.arange(fine)[:, None] // 2 == np.arange(coarse)[None, :]).astype(ml_dtypes.bfloat16)
+
+
+def paired(velocity, obstacle, pressure):
+    rows, depth = velocity.shape[2:]
+    half = rows // 2
+    wide = half + 2 * HALO
+    tunnel_size = lax.axis_size("tunnel")
+    side = lax.axis_index("group")
+    both = ("tunnel", "group")
+    own, spread, basis, rows_first = half_tables(rows)
+    depth_first, depth_second = wave_tables(depth)
+    rows_high, rows_low = high_low(own)
+    spread_high, spread_low = high_low(spread)
+    spread_all = np.concatenate([spread_high, spread_high, spread_low, np.zeros_like(spread_low)], axis=1)
+    basis_both = np.concatenate(high_low(basis), axis=0)
+    depth_high, depth_low = high_low(np.concatenate([depth_first.T, depth_second.T], axis=1))
+    sum_high, sum_low = high_low((rows_first[:half, :half] + rows_first[:half, half:]) / 2.0)
+    diff_high, diff_low = high_low((rows_first[:half, :half] - rows_first[:half, half:]) / 2.0)
+
+    def swap(value):
+        return lax.ppermute(value, "group", [(0, 1), (1, 0)])
+
+    ahead_way, behind_way = ([], [])
+    for i in range(tunnel_size):
+        after, before = ((i + 1) % tunnel_size, (i - 1) % tunnel_size)
+        ahead_way += [(2 * i, 2 * after), (2 * i + 1, 2 * before + 1)]
+        behind_way += [(2 * i, 2 * before), (2 * i + 1, 2 * after + 1)]
+
+    def ahead(value):
+        return lax.ppermute(value, both, ahead_way)
+
+    def behind(value):
+        return lax.ppermute(value, both, behind_way)
+
+    def ahead_across(value):
+        return lax.ppermute(value, both, [(i, j ^ 1) for i, j in ahead_way])
+
+    def behind_across(value):
+        return lax.ppermute(value, both, [(i, j ^ 1) for i, j in behind_way])
+
+    def tied(value, *others):
+        return lax.optimization_barrier((value,) + others)[0]
+
+    def half_of(value, which, axis):
+        return lax.dynamic_slice_in_dim(value, which * half, half, axis=axis)
+
+    plane = (half, depth)
+    two_planes, four_planes = ((2,) + plane, (4,) + plane)
+    full = lambda shape: pl.BlockSpec(shape, lambda i: (0,) * len(shape))
+    by_plane = lambda shape, at: pl.BlockSpec(
+        shape[:at] + (1,) + shape[at + 1 :], lambda i: (0,) * at + (i,) + (0,) * (len(shape) - at - 1)
+    )
+    tables = (rows_high, rows_low, spread_all, depth_high, depth_low)
+    table_specs = [full(table.shape) for table in tables]
+
+    edges = jnp.concatenate([pressure[:, :HALO], pressure[:, half - HALO :]], axis=1)
+    pressure_edge = swap(edges)
+    tall = jnp.concatenate([pressure_edge[:, HALO:], pressure, pressure_edge[:, :HALO]], axis=1)
+    to_ahead = jnp.where(side == 0, tall[1:], tall[:3])
+    to_behind = jnp.where(side == 0, tall[:3], tall[1:])
+    sent_uv = half_of(velocity[:2], 1 - side, 2)
+    peer_uv = swap(sent_uv)
+    pressure_left = ahead(to_ahead)
+    pressure_right = behind(to_behind)
+    raw_own, sent_w = kernel_call(
+        own_planes_kernel,
+        [(3, 2) + plane, (2, half + 24, depth)],
+        [],
+        [by_plane(velocity.shape, 1), full(basis_both.shape)] + table_specs,
+        3 * 10**9,
+        velocity, basis_both, *tables,
+        grid=(2,),
+        out_specs=[by_plane((3, 2) + plane, 1), by_plane((2, half + 24, depth), 0)],
+    )
+    peer_w = swap(tied(sent_w, pressure_left, pressure_right))
+    own_half = half_of(tied(velocity, sent_w), side, 2)
+    one = behind(own_half)
+    other_uv = ahead(peer_uv)
+    other_w = ahead(peer_w[:, :half])
+    solid_peer = swap(half_of(obstacle, 1 - side, 1))
+    solid_own = half_of(obstacle, side, 1)
+    (raw_peer,) = kernel_call(
+        peer_planes_kernel,
+        [(3, 2) + plane],
+        [],
+        [by_plane((2, 2) + plane, 1), by_plane((2, half + 24, depth), 0)] + table_specs,
+        3 * 10**9,
+        peer_uv, peer_w, *tables,
+        grid=(2,),
+        out_specs=[by_plane((3, 2) + plane, 1)],
+    )
+    strip = 64
+
+    def strips(count, first=0):
+        return pl.BlockSpec((count, 2, strip, depth), lambda i: (first, 0, i, 0))
+
+    flat = pl.BlockSpec((2, strip, depth), lambda i: (0, i, 0))
+    near_u, far_u = kernel_call(
+        star_u_kernel,
+        [two_planes] * 2,
+        [],
+        [strips(1)] * 6 + [flat] * 2,
+        10**8,
+        raw_own, raw_peer, own_half, one, peer_uv, other_uv, solid_own, solid_peer,
+        grid=(half // strip,),
+        out_specs=[flat] * 2,
+    )
+    left_u, right_u = (ahead(far_u), behind(near_u))
+    basis_strips = basis_both.reshape(16, half // strip, strip).transpose(1, 0, 2).copy()
+    near_v, far_v, near_w, far_w, sum_v = kernel_call(
+        star_vw_kernel,
+        [two_planes] * 4 + [(4, 8, depth)],
+        [],
+        [strips(3)] * 4 + [strips(2), flat, strips(1, 1), flat, flat, flat]
+        + [pl.BlockSpec((1, 16, strip), lambda i: (i, 0, 0))],
+        10**8,
+        raw_own, raw_peer, tied(own_half, near_u), one, peer_uv, peer_w, other_uv, other_w, solid_own, solid_peer,
+        basis_strips,
+        grid=(half // strip,),
+        out_specs=[flat] * 4 + [full((4, 8, depth))],
+    )
+    peer_sum_v = swap(sum_v)
+    own_depth = (depth_high[:, :depth].copy(), depth_low[:, :depth].copy())
+    (cross,) = kernel_call(
+        cross_kernel,
+        [four_planes],
+        [],
+        [VMEM] * 8,
+        10**9,
+        near_v, far_v, near_w, far_w, rows_high, rows_low, *own_depth,
+    )
+    edge_shape = (4, HALO, depth)
+    near_r, far_r, head_r, tail_r = kernel_call(
+        source_kernel,
+        [two_planes, two_planes, edge_shape, edge_shape],
+        [],
+        [flat] * 4
+        + [pl.BlockSpec((4, strip, depth), lambda i: (0, i, 0)), full((4, 8, depth))]
+        + [pl.BlockSpec((strip, spread_all.shape[1]), lambda i: (i, 0))],
+        10**8,
+        near_u, far_u, left_u, right_u, cross, peer_sum_v, spread_all[:half].copy(),
+        grid=(half // strip,),
+        out_specs=[flat, flat, full(edge_shape), full(edge_shape)],
+    )
+    edge_r = jnp.concatenate([head_r, tail_r], axis=1)
+    left_r, right_r = (ahead(far_r), behind(near_r))
+    edges = swap(edge_r)
+    left_edge, right_edge = (ahead(edges[:2]), behind(edges[2:]))
+    peer_vw = swap(jnp.stack([tied(far_v, left_edge, right_edge), far_w]))
+
+    mid_rows, mid_depth = (wide // 2, depth // 2)
+    message = (mid_rows + wide, depth)
+    base_one, mid_source, sent_ahead, sent_behind = kernel_call(
+        fine_kernel,
+        [(4, wide, depth), (2, mid_rows, mid_depth), message, message],
+        [
+            pltpu.VMEM((8, wide, depth), f32),
+            pltpu.VMEM((10, wide, depth), f32),
+            pltpu.VMEM((8, wide, depth), f32),
+            pltpu.VMEM((6, wide, depth), f32),
+        ],
+        [VMEM] * 12,
+        10**8,
+        tall, pressure_left, pressure_right,
+        near_r, far_r, left_r, right_r, edges, left_edge, right_edge,
+        pair_sums(depth, mid_depth), pair_sums(wide, mid_rows).T,
+    )
+    left_one, right_one = (ahead(sent_ahead), behind(sent_behind))
+    near_base, far_base = kernel_call(
+        base_kernel,
+        [two_planes, two_planes],
+        [],
+        [VMEM] * 5,
+        10**8,
+        base_one, left_one, right_one, near_r, far_r,
+    )
+    low_depth = mid_depth // 2
+    halves = np.zeros((mid_depth, 2 * mid_depth), ml_dtypes.bfloat16)
+    halves[:, :low_depth] = pair_sums(mid_depth, low_depth)
+    halves[:, mid_depth + low_depth :] = pair_sums(mid_depth, low_depth)
+    own_pairs = pair_sums(half // 2, half // 4).T
+    own_pairs = np.pad(own_pairs, ((0, 0), (HALO // 2, HALO // 2)))
+    mid_one, low_source = kernel_call(
+        middle_kernel,
+        [(2, mid_rows, mid_depth), (half // 8, mid_depth)],
+        [pltpu.VMEM((6, mid_rows, mid_depth), f32), pltpu.VMEM((4, mid_rows, mid_depth), f32)],
+        [VMEM] * 5,
+        10**8,
+        tied(mid_source, near_base), left_one, right_one, halves, own_pairs,
+    )
+    left_two, right_two = (ahead(mid_one[1:]), behind(mid_one[:1]))
+    (mid_base,) = kernel_call(
+        middle_base_kernel,
+        [(2, half // 2, mid_depth)],
+        [],
+        [VMEM] * 4,
+        10**7,
+        mid_one, tied(left_two, peer_vw), right_two, mid_source,
+    )
+    peer_mid = swap(mid_base)
+    both_mid = jnp.stack([mid_base, peer_mid])
+    left_mid, right_mid = (ahead(both_mid), behind(both_mid))
+    low_all = lax.all_to_all(
+        jnp.broadcast_to(tied(low_source, mid_base), (2 * tunnel_size,) + low_source.shape), both, 0, 0, tiled=True
+    )
+    left_b, right_b = (ahead(tied(far_base, mid_base)), behind(tied(near_base, mid_base)))
+    peer_base = swap(tied(far_base, peer_mid))
+    own_u, sent_u = kernel_call(
+        stream_kernel,
+        [two_planes, two_planes],
+        [],
+        [VMEM] * 6,
+        10**8,
+        near_base, far_base, left_b, right_b, near_u, far_u,
+    )
+    peer_u = swap(sent_u)
+    low_plane = (half // 2, mid_depth)
+    mid_plane = (half, mid_depth)
+    fine_plane = (rows, depth)
+    expand_low = np.zeros((mid_depth, mid_depth), ml_dtypes.bfloat16)
+    expand_low[:low_depth] = pair_sums(mid_depth, low_depth).T
+    (spread_low,) = kernel_call(
+        coarsest_kernel,
+        [(5,) + mid_plane],
+        [pltpu.VMEM((11,) + low_plane, f32)] * 3,
+        [VMEM] * 3,
+        10**7,
+        low_all, expand_low, pair_sums(half, half // 2),
+    )
+    corrected, potential = kernel_call(
+        correction_kernel,
+        [(3, 2) + fine_plane, four_planes],
+        [
+            pltpu.VMEM((5,) + mid_plane, f32),
+            pltpu.VMEM((9,) + mid_plane, f32),
+            pltpu.VMEM((5,) + fine_plane, f32),
+            pltpu.VMEM((8,) + fine_plane, f32),
+            pltpu.VMEM((6,) + fine_plane, f32),
+            pltpu.VMEM(fine_plane, f32),
+        ],
+        [VMEM] * 19,
+        10**9,
+        spread_low, both_mid, left_mid, right_mid, near_base, far_base, peer_base, near_v, near_w, peer_vw, obstacle,
+        sum_high, sum_low, diff_high, diff_low, *own_depth,
+        pair_sums(depth, mid_depth).T.copy(), pair_sums(rows, half),
+    )
+    stream = pl.BlockSpec((1, 1) + fine_plane, lambda i: (0, i, 0, 0))
+    (corrected,) = kernel_call(
+        stream_correction_kernel,
+        [corrected.shape],
+        [],
+        [stream] + [full(two_planes)] * 2 + [by_plane(obstacle.shape, 0)],
+        10**7,
+        corrected, own_u, peer_u, obstacle,
+        grid=(2,),
+        out_specs=[stream],
+        aliases={0: 0},
+    )
+    return (corrected, potential)
+
+
+def step(velocity, obstacle, pressure):
+    planes, rows, depth = velocity.shape[1:]
+    fits = lax.axis_size("group") == 2 and planes == 2 and pressure.shape[0] == 4
+    fits = fits and lax.axis_size("tunnel") > 10 and rows % 512 == 0 and depth % 256 == 0
+    if fits:
+        return paired(velocity, obstacle, pressure)
+    return local(velocity, obstacle, pressure)
+
+
 def solution(mesh):
     in_specs = (
         P(None, ("tunnel", "group"), None, None),
@@ -182,4 +931,4 @@
         P("tunnel", "group", None),
     )
     out_specs = (P(None, ("tunnel", "group"), None, None), P("tunnel", "group", None))
-    return jax.shard_map(local, mesh=mesh, in_specs=in_specs, out_specs=out_specs, check_vma=False)
+    return jax.shard_map(step, mesh=mesh, in_specs=in_specs, out_specs=out_specs, check_vma=False)

time: 590 us -> 205 us (0.35); the launches traced: 580 us -> 205 us
  local copies, waits for them, and re-layouts: 149 us -> 19.8 us
  waiting for transfers between devices: 173 us -> 48.7 us
  other arithmetic: 85.3 us -> 2.57 us
  Pallas kernels: 0 us -> 67 us
  matrix products: 57.2 us -> 0 us
  starting transfers between devices: 113 us -> 65.5 us
    ppermute x62 -> x29, waiting for transfers between devices: 154 us -> 48.7 us  [the longest x10 25.4 us: ahead(): return lax.ppermute(value, both, ahead_way)]
    reshape x2 -> x0, local copies, waits for them, and re-layouts: 69.4 us -> none  [the longest x1 68.4 us: restrict(): blocks = field.reshape(planes // 2, 2, rows // 2, 2, depth // 2, 2)]
    pallas_call x0 -> x14, Pallas kernels: none -> 67 us  [kernel_call(): pl.pallas_call(body, out_shape=[jax.ShapeDtypeStruct(s, f32) for s in out...]
    dot_general x14 -> x0, matrix products: 57.2 us -> none  [the longest x3 16.1 us: along_rows(): return jnp.einsum('ij,...jz->...iz', matrix, field, precision=highest)]
    ppermute x62 -> x29, starting transfers between devices: 106 us -> 61 us  [the longest x9 25.5 us: behind(): return lax.ppermute(value, both, behind_way)]
    slice x54 -> x7, local copies, waits for them, and re-layouts: 38.6 us -> 3.46 us  [the longest x2 1.59 us: paired(): sent_uv = half_of(velocity[:2], 1 - side, 2)]
    add x12 -> x0, other arithmetic: 32 us -> none  [the longest x10 30.7 us: relax_padded(): interior + relax_weight / 6.0 * (padded_neighbours(padded) - 6.0 * interi...]
    reduce_sum x3 -> x0, other arithmetic: 23.7 us -> none  [restrict(): return jnp.sum(blocks, axis=(1, 3, 5)) * 0.125]
  transfers between devices with their start and end apart: 64 -> 30, of which waited for: 49 -> 11; matrix products, arithmetic and copies ran while one was open for 42% -> 2% of each run, Pallas kernels for 0% -> 28%
where the time goes in v2:
time: 205 us
  Pallas kernels  67 us (33%)
  starting transfers between devices  65.5 us (32%)
  waiting for transfers between devices  48.7 us (24%)
  local copies, waits for them, and re-layouts  19.8 us (10%)
  other arithmetic  2.57 us (1%)
    pallas_call x14, Pallas kernels, kernel_call(): pl.pallas_call(body, out_shape=[jax.ShapeDtypeStruct(s, f32) for s in out...  67 us
    ppermute x9, starting transfers between devices, behind(): return lax.ppermute(value, both, behind_way)  25.5 us
    ppermute x10, waiting for transfers between devices, ahead(): return lax.ppermute(value, both, ahead_way)  25.4 us
    ppermute x10, starting transfers between devices, ahead(): return lax.ppermute(value, both, ahead_way)  23.5 us
    ppermute x10, waiting for transfers between devices, swap(): return lax.ppermute(value, 'group', [(0, 1), (1, 0)])  21.1 us
    unnamed x74, local copies, waits for them, and re-layouts  12.6 us
    ppermute x10, starting transfers between devices, swap(): return lax.ppermute(value, 'group', [(0, 1), (1, 0)])  11.9 us
    all_to_all x1, starting transfers between devices, paired(): lax.all_to_all(jnp.broadcast_to(tied(low_source, mid_base), (2 * tunnel_s...  4.53 us
  transfers between devices with their start and end apart: 30, of which 11 were waited for; matrix products, arithmetic and copies ran while one was open for 2% of the time, Pallas kernels for 28%

profile of v2, /device:TPU:0, one launch (start us, length us, event | category | flops | bytes accessed | tf_op | source)
XLA Modules:
  0.0 204.5 jit_solution(8313575874560717166)
XLA Ops:
  0.6 0.9 fusion
  1.5 3.0 %collective-permute-start = (f32[4,32,256]{2,1,0:T(8,128)S(1)}, f32[4,32,256]{2,1,0:T(8,128)S(1)}, u32[]{:S(2)}, u32[]{:S(2)}) collective-permute-start(f32[4,32,256]{2,1,0:T(8,128)S(1)} %pad_maximum_fusion.3), channel_id=1, source_target_pairs={{0,1},{1,0},{2,3},{3,2},{4,5},{5,4},{6,7},{7,6},{8,9},{9,8},{10,11... | collective-permute-start | bytes 393224 | tf_op jit(solution)/shard_map/ppermute | solution.py:677
  4.6 1.6 slice-done
  6.2 1.1 constant_dynamic-slice_fusion.3
  7.2 0.8 collective-permute-done
  8.2 1.5 slice_select_fusion
  9.8 3.3 %collective-permute-start.2 = (f32[3,288,256]{2,1,0:T(8,128)}, f32[3,288,256]{2,1,0:T(8,128)}, u32[]{:S(2)}, u32[]{:S(2)}) collective-permute-start(f32[3,288,256]{2,1,0:T(8,128)} %get-tuple-element.72), channel_id=1, source_target_pairs={{0,30},{1,3},{2,0},{3,5},{4,2},{5,7},{6,4},{7,9},{8,6},{9,11},{10,... | collective-permute-start | bytes 2654216 | tf_op jit(solution)/shard_map/ppermute | solution.py:689
  13.1 6.6 %shard_map.248 = (f32[3,2,256,256]{3,2,1,0:T(8,128)}, f32[2,280,256]{2,1,0:T(8,128)}) custom-call(f32[3,2,512,256]{3,2,1,0:T(8,128)} %velocity_ref.1, bf16[16,256]{1,0:T(8,128)(2,1)} %constant.54.clone.basis_ref, bf16[512,256]{1,0:T(8,128)(2,1)} %constant.55.clone.rows_high, bf16[512,256]{1,0:T(8,128)(2,1)} %constant.56.clone.rows_low, ...), custom_call_target="tpu_custom_call" | custom-call | flops 3000000000 | bytes 6381568 | tf_op jit(solution)/shard_map/pallas_call | solution.py:302
  19.9 4.3 %collective-permute-start.5 = (f32[3,2,256,256]{3,2,1,0:T(8,128)S(1)}, f32[3,2,256,256]{3,2,1,0:T(8,128)S(1)}, u32[]{:S(2)}, u32[]{:S(2)}) collective-permute-start(f32[3,2,256,256]{3,2,1,0:T(8,128)S(1)} %constant_dynamic-slice_fusion.2.own_ref), channel_id=1, source_target_pairs={{0,30},{1,3},{2,0},{3,5},{4,2},{5,7},{6,4},{7,9},{8,6},{9,11},{10,... | collective-permute-start | bytes 4718600 | tf_op jit(solution)/shard_map/ppermute | solution.py:689
  24.2 8.0 %collective-permute-done.3.uv_ref.peers = f32[2,2,256,256]{3,2,1,0:T(8,128)} collective-permute-done((f32[2,2,256,256]{3,2,1,0:T(8,128)}, f32[2,2,256,256]{3,2,1,0:T(8,128)}, u32[]{:S(2)}, u32[]{:S(2)}) %collective-permute-start.3) | collective-permute-done | bytes 1048608 | tf_op jit(solution)/shard_map/ppermute | solution.py:677
  32.2 3.3 %collective-permute-start.4 = (f32[2,280,256]{2,1,0:T(8,128)S(1)}, f32[2,280,256]{2,1,0:T(8,128)S(1)}, u32[]{:S(2)}, u32[]{:S(2)}) collective-permute-start(f32[2,280,256]{2,1,0:T(8,128)S(1)} %copy-done.36), channel_id=1, source_target_pairs={{0,1},{1,0},{2,3},{3,2},{4,5},{5,4},{6,7},{7,6},{8,9},{9,8},{10,11... | collective-permute-start | bytes 1720328 | tf_op jit(solution)/shard_map/ppermute | solution.py:677
  35.5 0.9 constant_dynamic-slice_fusion
  36.5 6.7 %collective-permute-done.4.w_ref.peer_w = f32[2,280,256]{2,1,0:T(8,128)S(1)} collective-permute-done((f32[2,280,256]{2,1,0:T(8,128)S(1)}, f32[2,280,256]{2,1,0:T(8,128)S(1)}, u32[]{:S(2)}, u32[]{:S(2)}) %collective-permute-start.4) | collective-permute-done | bytes 573472 | tf_op jit(solution)/shard_map/ppermute | solution.py:677
  43.2 15.9 %collective-permute-start.10 = (f32[2,256,256]{2,1,0:T(8,128)S(1)}, f32[2,256,256]{2,1,0:T(8,128)S(1)}, u32[]{:S(2)}, u32[]{:S(2)}) collective-permute-start(f32[2,256,256]{2,1,0:T(8,128)S(1)} %slice.54), channel_id=1, source_target_pairs={{0,2},{1,31},{2,4},{3,1},{4,6},{5,3},{6,8},{7,5},{8,10},{9,7},{10,... | collective-permute-start | bytes 1572872 | tf_op jit(solution)/shard_map/ppermute | solution.py:686
  59.2 5.6 %shard_map.249.raw_peer = f32[3,2,256,256]{3,2,1,0:T(8,128)} custom-call(f32[2,2,256,256]{3,2,1,0:T(8,128)} %collective-permute-done.3.uv_ref.peers, f32[2,280,256]{2,1,0:T(8,128)} %copy-done.6, bf16[512,256]{1,0:T(8,128)(2,1)} %constant.55.clone.rows_high, bf16[512,256]{1,0:T(8,128)(2,1)} %constant.56.clone.rows_low, ...), custom_call_target="tpu_custom_call" | custom-call | flops 3000000000 | bytes 4276224 | tf_op jit(solution)/shard_map/pallas_call | solution.py:302
  64.9 0.7 copy-done.7
  66.5 4.3 %shard_map.250 = (f32[2,256,256]{2,1,0:T(8,128)}, f32[2,256,256]{2,1,0:T(8,128)}) custom-call(f32[3,2,256,256]{3,2,1,0:T(8,128)} %get-tuple-element.37.raw_own, f32[3,2,256,256]{3,2,1,0:T(8,128)} %shard_map.249.raw_peer, f32[3,2,256,256]{3,2,1,0:T(8,128)} %copy-done.1, f32[3,2,256,256]{3,2,1,0:T(8,128)} %copy-done.3, ...), custom_call_target="tpu_custom_call" | custom-call | flops 100000000 | bytes 10485760 | tf_op jit(solution)/shard_map/pallas_call | solution.py:302
  70.8 1.4 collective-permute-start.8
  72.2 3.1 %collective-permute-start.9 = (f32[2,256,256]{2,1,0:T(8,128)}, f32[2,256,256]{2,1,0:T(8,128)S(1)}, u32[]{:S(2)}, u32[]{:S(2)}) collective-permute-start(f32[2,256,256]{2,1,0:T(8,128)} %get-tuple-element.41.near_u), channel_id=1, source_target_pairs={{0,30},{1,3},{2,0},{3,5},{4,2},{5,7},{6,4},{7,9},{8,6},{9,11},{10,... | collective-permute-start | bytes 1572872 | tf_op jit(solution)/shard_map/ppermute | solution.py:689
  75.3 0.8 copy-done.23
  76.1 6.3 %shard_map.251 = (f32[2,256,256]{2,1,0:T(8,128)}, f32[2,256,256]{2,1,0:T(8,128)}, f32[2,256,256]{2,1,0:T(8,128)}, f32[2,256,256]{2,1,0:T(8,128)}, f32[4,8,256]{2,1,0:T(8,128)}) custom-call(f32[3,2,256,256]{3,2,1,0:T(8,128)} %get-tuple-element.37.raw_own, f32[3,2,256,256]{3,2,1,0:T(8,128)} %shard_map.249.raw_peer, f32[3,2,256,256]{3,2,1,0:T(8,128)} %copy-done.1, ...), custom_call_target="tpu_custom_call" | custom-call | flops 100000000 | bytes 12673024 | tf_op jit(solution)/shard_map/pallas_call | solution.py:302
  82.9 3.7 %shard_map.252.cross_ref = f32[4,256,256]{2,1,0:T(8,128)} custom-call(f32[2,256,256]{2,1,0:T(8,128)} %get-tuple-element.44.near_v, f32[2,256,256]{2,1,0:T(8,128)} %get-tuple-element.61.far_v, f32[2,256,256]{2,1,0:T(8,128)} %get-tuple-element.46.near_w, f32[2,256,256]{2,1,0:T(8,128)} %get-tuple-element.47.far_w, bf16[512,256]{1,0:T(8,128)(2,1)} %constant.55.clone.rows_high, ...), custom_call_target="tpu_custom_call" | custom-call | flops 1000000000 | bytes 3932160 | tf_op jit(solution)/shard_map/pallas_call | solution.py:302
  87.4 0.8 copy-done.24
  88.2 4.2 %shard_map.253 = (f32[2,256,256]{2,1,0:T(8,128)}, f32[2,256,256]{2,1,0:T(8,128)}, f32[4,16,256]{2,1,0:T(8,128)}, f32[4,16,256]{2,1,0:T(8,128)}) custom-call(f32[2,256,256]{2,1,0:T(8,128)} %get-tuple-element.41.near_u, f32[2,256,256]{2,1,0:T(8,128)} %get-tuple-element.42.far_u, f32[2,256,256]{2,1,0:T(8,128)} %copy-done.21, f32[2,256,256]{2,1,0:T(8,128)} %copy-done.24, ...), custom_call_target="tpu_custom_call" | custom-call | flops 100000000 | bytes 4374528 | tf_op jit(solution)/shard_map/pallas_call | solution.py:302
  92.5 0.9 pad_maximum_fusion.4
  93.4 1.6 collective-permute-start.14
  95.0 2.6 %collective-permute-start.13 = (f32[2,256,256]{2,1,0:T(8,128)}, f32[2,256,256]{2,1,0:T(8,128)S(1)}, u32[]{:S(2)}, u32[]{:S(2)}) collective-permute-start(f32[2,256,256]{2,1,0:T(8,128)} %get-tuple-element.49.near_r), channel_id=1, source_target_pairs={{0,30},{1,3},{2,0},{3,5},{4,2},{5,7},{6,4},{7,9},{8,6},{9,11},{10,... | collective-permute-start | bytes 1572872 | tf_op jit(solution)/shard_map/ppermute | solution.py:689
  97.7 1.1 collective-permute-done.14.edge_ref
  98.8 4.4 %collective-permute-start.16 = (f32[2,32,256]{2,1,0:T(8,128)S(1)}, f32[2,32,256]{2,1,0:T(8,128)S(1)}, u32[]{:S(2)}, u32[]{:S(2)}) collective-permute-start(f32[2,32,256]{2,1,0:T(8,128)S(1)} %get-tuple-element.80), channel_id=1, source_target_pairs={{0,30},{1,3},{2,0},{3,5},{4,2},{5,7},{6,4},{7,9},{8,6},{9,11},{10,... | collective-permute-start | bytes 196616 | tf_op jit(solution)/shard_map/ppermute | solution.py:689
  103.1 2.1 %collective-permute-done.16.right_edge = f32[2,32,256]{2,1,0:T(8,128)S(1)} collective-permute-done((f32[2,32,256]{2,1,0:T(8,128)S(1)}, f32[2,32,256]{2,1,0:T(8,128)S(1)}, u32[]{:S(2)}, u32[]{:S(2)}) %collective-permute-start.16) | collective-permute-done | bytes 65568 | tf_op jit(solution)/shard_map/ppermute | solution.py:689
  105.3 4.7 %collective-permute-done.15.left_edge = f32[2,32,256]{2,1,0:T(8,128)S(1)} collective-permute-done((f32[2,32,256]{2,1,0:T(8,128)S(1)}, f32[2,32,256]{2,1,0:T(8,128)S(1)}, u32[]{:S(2)}, u32[]{:S(2)}) %collective-permute-start.15) | collective-permute-done | bytes 65568 | tf_op jit(solution)/shard_map/ppermute | solution.py:686
  111.0 0.8 copy-done.22
  111.8 7.5 %shard_map.254 = (f32[4,288,256]{2,1,0:T(8,128)}, f32[2,144,128]{2,1,0:T(8,128)}, f32[432,256]{1,0:T(8,128)}, f32[432,256]{1,0:T(8,128)}) custom-call(f32[4,288,256]{2,1,0:T(8,128)} %copy-done, f32[3,288,256]{2,1,0:T(8,128)} %collective-permute-done.1.pressure_left, f32[3,288,256]{2,1,0:T(8,128)} %collective-permute-done.2.pressure_right, ...), custom_call_target="tpu_custom_call" | custom-call | flops 100000000 | bytes 7668736 | tf_op jit(solution)/shard_map/pallas_call | solution.py:302
  119.2 1.7 collective-permute-start.17
  120.9 2.7 %collective-permute-start.18 = (f32[432,256]{1,0:T(8,128)}, f32[432,256]{1,0:T(8,128)S(1)}, u32[]{:S(2)}, u32[]{:S(2)}) collective-permute-start(f32[432,256]{1,0:T(8,128)} %get-tuple-element.56), channel_id=1, source_target_pairs={{0,30},{1,3},{2,0},{3,5},{4,2},{5,7},{6,4},{7,9},{8,6},{9,11},{10,... | collective-permute-start | bytes 1327112 | tf_op jit(solution)/shard_map/ppermute | solution.py:689
  123.7 6.3 %collective-permute-done.17.left_ref = f32[432,256]{1,0:T(8,128)S(1)} collective-permute-done((f32[432,256]{1,0:T(8,128)}, f32[432,256]{1,0:T(8,128)S(1)}, u32[]{:S(2)}, u32[]{:S(2)}) %collective-permute-start.17) | collective-permute-done | bytes 442400 | tf_op jit(solution)/shard_map/ppermute | solution.py:686
  130.0 0.8 copy-done.13
  131.0 3.5 %shard_map.255 = (f32[2,256,256]{2,1,0:T(8,128)}, f32[2,256,256]{2,1,0:T(8,128)}) custom-call(f32[4,288,256]{2,1,0:T(8,128)} %get-tuple-element.54.base_ref, f32[432,256]{1,0:T(8,128)} %copy-done.13, f32[432,256]{1,0:T(8,128)} %copy-done.14, f32[2,256,256]{2,1,0:T(8,128)} %get-tuple-element.49.near_r, f32[2,256,256]{2,1,0:T(8,128)} %get-tuple-element.50.far_r), custom_call_target="tpu_custom_call" | custom-call | flops 100000000 | bytes 4161536 | tf_op jit(solution)/shard_map/pallas_call | solution.py:302
  134.4 2.7 %shard_map.256 = (f32[2,144,128]{2,1,0:T(8,128)}, f32[32,128]{1,0:T(8,128)}) custom-call(f32[2,144,128]{2,1,0:T(8,128)} %get-tuple-element.58.own_ref.source_ref, f32[432,256]{1,0:T(8,128)} %copy-done.13, f32[432,256]{1,0:T(8,128)} %copy-done.14, bf16[128,256]{1,0:T(8,128)(2,1)} %constant.66.clone.depth_pick, bf16[64,144]{1,0:T(8,128)(2,1)} %constant.67.clone.rows_pick), custom_call_target="tpu_custom_call" | custom-call | flops 100000000 | bytes 1280000 | tf_op jit(solution)/shard_map/pallas_call | solution.py:302
  137.1 0.9 fusion.1
  138.0 4.1 %collective-permute-start.19 = (f32[1,144,128]{2,1,0:T(8,128)S(1)}, f32[1,144,128]{2,1,0:T(8,128)S(1)}, u32[]{:S(2)}, u32[]{:S(2)}) collective-permute-start(f32[1,144,128]{2,1,0:T(8,128)S(1)} %get-tuple-element.79), channel_id=1, source_target_pairs={{0,2},{1,31},{2,4},{3,1},{4,6},{5,3},{6,8},{7,5},{8,10},{9,7},{10,... | collective-permute-start | bytes 221192 | tf_op jit(solution)/shard_map/ppermute | solution.py:686
  142.5 2.0 collective-permute-done.19.left_ref
  144.6 0.6 copy-done.31
  145.2 0.6 copy-done.32
  145.8 1.9 shard_map.257
  147.7 1.6 broadcast_in_dim.3
  149.3 4.5 %all-to-all-start = ((f32[32,32,128]{2,1,0:T(8,128)}), f32[32,32,128]{2,1,0:T(8,128)S(1)}, u32[]{:S(2)}, u32[]{:S(2)}) async-start(f32[32,32,128]{2,1,0:T(8,128)} %broadcast_in_dim.3), calls=%async_computation | async-start | bytes 1048576 | tf_op jit(solution)/shard_map/all_to_all | solution.py:859
  154.2 4.2 %collective-permute-start.27 = (f32[2,256,256]{2,1,0:T(8,128)S(1)}, f32[2,256,256]{2,1,0:T(8,128)S(1)}, u32[]{:S(2)}, u32[]{:S(2)}) collective-permute-start(f32[2,256,256]{2,1,0:T(8,128)S(1)} %copy-done.8), channel_id=1, source_target_pairs={{0,30},{1,3},{2,0},{3,5},{4,2},{5,7},{6,4},{7,9},{8,6},{9,11},{10,... | collective-permute-start | bytes 1572872 | tf_op jit(solution)/shard_map/ppermute | solution.py:689
  158.3 1.4 collective-permute-start.22
  159.8 4.5 %collective-permute-done.22 = f32[2,128,128]{2,1,0:T(8,128)S(1)} collective-permute-done((f32[2,128,128]{2,1,0:T(8,128)S(1)}, f32[2,128,128]{2,1,0:T(8,128)S(1)}, u32[]{:S(2)}, u32[]{:S(2)}) %collective-permute-start.22) | collective-permute-done | bytes 131104 | tf_op jit(solution)/shard_map/ppermute | solution.py:677
  164.3 1.1 collective-permute-start.25
  165.4 8.1 %collective-permute-done.26.left_ref = f32[2,256,256]{2,1,0:T(8,128)S(1)} collective-permute-done((f32[2,256,256]{2,1,0:T(8,128)S(1)}, f32[2,256,256]{2,1,0:T(8,128)S(1)}, u32[]{:S(2)}, u32[]{:S(2)}) %collective-permute-start.26) | collective-permute-done | bytes 524320 | tf_op jit(solution)/shard_map/ppermute | solution.py:686
  173.5 0.8 copy-done.26
  174.3 0.8 copy-done.27
  175.1 3.0 %shard_map.260 = (f32[2,256,256]{2,1,0:T(8,128)}, f32[2,256,256]{2,1,0:T(8,128)}) custom-call(f32[2,256,256]{2,1,0:T(8,128)} %get-tuple-element.68.near_base.near_ref, f32[2,256,256]{2,1,0:T(8,128)} %get-tuple-element.67.far_base.far_ref, f32[2,256,256]{2,1,0:T(8,128)} %copy-done.26, f32[2,256,256]{2,1,0:T(8,128)} %copy-done.27, ...), custom_call_target="tpu_custom_call" | custom-call | flops 100000000 | bytes 4194304 | tf_op jit(solution)/shard_map/pallas_call | solution.py:302
  178.1 0.7 collective-permute-start.28
  179.4 0.8 copy-done.12
  180.2 3.4 %shard_map.258.spread_ref = f32[5,256,128]{2,1,0:T(8,128)} custom-call(f32[32,32,128]{2,1,0:T(8,128)} %copy-done.12, bf16[128,128]{1,0:T(8,128)(2,1)} %constant.68.clone.mid_depth, bf16[256,128]{1,0:T(8,128)(2,1)} %constant.64.clone.depth_pick.mid_rows), custom_call_target="tpu_custom_call" | custom-call | flops 10000000 | bytes 1277952 | tf_op jit(solution)/shard_map/pallas_call | solution.py:302
  183.6 4.3 %collective-permute-done.23.left_mid = f32[2,2,128,128]{3,2,1,0:T(8,128)S(1)} collective-permute-done((f32[2,2,128,128]{3,2,1,0:T(8,128)S(1)}, f32[2,2,128,128]{3,2,1,0:T(8,128)S(1)}, u32[]{:S(2)}, u32[]{:S(2)}) %collective-permute-start.23) | collective-permute-done | bytes 262176 | tf_op jit(solution)/shard_map/ppermute | solution.py:686
  187.9 0.7 copy-done.30
  188.6 0.8 copy-done.18
  189.4 11.6 %shard_map.259 = (f32[3,2,512,256]{3,2,1,0:T(8,128)}, f32[4,256,256]{2,1,0:T(8,128)}) custom-call(f32[5,256,128]{2,1,0:T(8,128)} %shard_map.258.spread_ref, f32[2,2,128,128]{3,2,1,0:T(8,128)} %copy-done.16, f32[2,2,128,128]{3,2,1,0:T(8,128)} %copy-done.30, f32[2,2,128,128]{3,2,1,0:T(8,128)} %copy-done.29, ...), custom_call_target="tpu_custom_call" | custom-call | flops 1000000000 | bytes 11468800 | tf_op jit(solution)/shard_map/pallas_call | solution.py:302
  201.0 0.8 copy-done.19
  201.8 2.7 %shard_map.261 = f32[3,2,512,256]{3,2,1,0:T(8,128)} custom-call(f32[3,2,512,256]{3,2,1,0:T(8,128)} %get-tuple-element.66.gradient_ref, f32[2,256,256]{2,1,0:T(8,128)} %get-tuple-element.69.own_u, f32[2,256,256]{2,1,0:T(8,128)} %copy-done.19, s32[2,512,256]{2,1,0:T(8,128)} %solid_ref.3), custom_call_target="tpu_custom_call", output_to_operand_aliasing={{}: (0, {})} | custom-call | flops 10000000 | bytes 8388608 | tf_op jit(solution)/shard_map/pallas_call | solution.py:302
  (101 shorter events, 5.1 us)
Async XLA Ops:
  1.5 6.5 %collective-permute-start = (f32[4,32,256]{2,1,0:T(8,128)S(1)}, f32[4,32,256]{2,1,0:T(8,128)S(1)}, u32[]{:S(2)}, u32[]{:S(2)}) collective-permute-start(f32[4,32,256]{2,1,0:T(8,128)S(1)} %pad_maximum_fusion.3), channel_id=1, source_target_pairs={{0,1},{1,0},{2,3},{3,2},{4,5},{5,4},{6,7},{7,6},{8,9},{9,8},{10,11... | collective-permute-start | bytes 393224 | tf_op jit(solution)/shard_map/ppermute | solution.py:677
  4.6 1.6 slice-start
  4.6 3.5 %copy-start.15 = (f32[4,256,256]{2,1,0:T(8,128)S(1)}, f32[4,256,256]{2,1,0:T(8,128)}, u32[]{:S(2)}) copy-start(f32[4,256,256]{2,1,0:T(8,128)} %param.27) | copy-start | bytes 3145732
  7.2 24.9 %collective-permute-start.3 = (f32[2,2,256,256]{3,2,1,0:T(8,128)}, f32[2,2,256,256]{3,2,1,0:T(8,128)}, u32[]{:S(2)}, u32[]{:S(2)}) collective-permute-start(f32[2,2,256,256]{3,2,1,0:T(8,128)} %constant_dynamic-slice_fusion.3), channel_id=1, source_target_pairs={{0,1},{1,0},{2,3},{3,2},{4,5},{5,4},{6,7},{7,6},{8,9},{9,8},{10,11... | collective-permute-start | bytes 3145736 | tf_op jit(solution)/shard_map/ppermute | solution.py:677
  8.2 1.6 copy-start
  9.8 22.4 %collective-permute-start.2 = (f32[3,288,256]{2,1,0:T(8,128)}, f32[3,288,256]{2,1,0:T(8,128)}, u32[]{:S(2)}, u32[]{:S(2)}) collective-permute-start(f32[3,288,256]{2,1,0:T(8,128)} %get-tuple-element.72), channel_id=1, source_target_pairs={{0,30},{1,3},{2,0},{3,5},{4,2},{5,7},{6,4},{7,9},{8,6},{9,11},{10,... | collective-permute-start | bytes 2654216 | tf_op jit(solution)/shard_map/ppermute | solution.py:689
  13.1 6.6 %copy-start.4 = (f32[3,2,512,256]{3,2,1,0:T(8,128)S(1)}, f32[3,2,512,256]{3,2,1,0:T(8,128)}, u32[]{:S(2)}) copy-start(f32[3,2,512,256]{3,2,1,0:T(8,128)} %velocity_ref.1) | copy-start | bytes 9437188
  13.1 19.0 %collective-permute-start.1 = (f32[3,288,256]{2,1,0:T(8,128)}, f32[3,288,256]{2,1,0:T(8,128)}, u32[]{:S(2)}, u32[]{:S(2)}) collective-permute-start(f32[3,288,256]{2,1,0:T(8,128)} %get-tuple-element.73), channel_id=1, source_target_pairs={{0,2},{1,31},{2,4},{3,1},{4,6},{5,3},{6,8},{7,5},{8,10},{9,7},{10,... | collective-permute-start | bytes 2654216 | tf_op jit(solution)/shard_map/ppermute | solution.py:686
  19.7 12.4 %copy-start.36 = (f32[2,280,256]{2,1,0:T(8,128)S(1)}, f32[2,280,256]{2,1,0:T(8,128)}, u32[]{:S(2)}) copy-start(f32[2,280,256]{2,1,0:T(8,128)} %get-tuple-element.39) | copy-start | bytes 1720324
  19.7 15.8 %copy-start.2 = (s32[2,512,256]{2,1,0:T(8,128)S(1)}, s32[2,512,256]{2,1,0:T(8,128)}, u32[]{:S(2)}) copy-start(s32[2,512,256]{2,1,0:T(8,128)} %solid_ref.3) | copy-start | bytes 3145732
  19.9 23.4 %copy-start.1 = (f32[3,2,256,256]{3,2,1,0:T(8,128)}, f32[3,2,256,256]{3,2,1,0:T(8,128)S(1)}, u32[]{:S(2)}) copy-start(f32[3,2,256,256]{3,2,1,0:T(8,128)S(1)} %constant_dynamic-slice_fusion.2.own_ref) | copy-start | bytes 4718596
  19.9 45.0 %collective-permute-start.5 = (f32[3,2,256,256]{3,2,1,0:T(8,128)S(1)}, f32[3,2,256,256]{3,2,1,0:T(8,128)S(1)}, u32[]{:S(2)}, u32[]{:S(2)}) collective-permute-start(f32[3,2,256,256]{3,2,1,0:T(8,128)S(1)} %constant_dynamic-slice_fusion.2.own_ref), channel_id=1, source_target_pairs={{0,30},{1,3},{2,0},{3,5},{4,2},{5,7},{6,4},{7,9},{8,6},{9,11},{10,... | collective-permute-start | bytes 4718600 | tf_op jit(solution)/shard_map/ppermute | solution.py:689
  32.1 32.7 %collective-permute-start.6 = (f32[2,2,256,256]{3,2,1,0:T(8,128)}, f32[2,2,256,256]{3,2,1,0:T(8,128)S(1)}, u32[]{:S(2)}, u32[]{:S(2)}) collective-permute-start(f32[2,2,256,256]{3,2,1,0:T(8,128)} %collective-permute-done.3.uv_ref.peers), channel_id=1, source_target_pairs={{0,2},{1,31},{2,4},{3,1},{4,6},{5,3},{6,8},{7,5},{8,10},{9,7},{10,... | collective-permute-start | bytes 3145736 | tf_op jit(solution)/shard_map/ppermute | solution.py:686
  32.2 11.0 %collective-permute-start.4 = (f32[2,280,256]{2,1,0:T(8,128)S(1)}, f32[2,280,256]{2,1,0:T(8,128)S(1)}, u32[]{:S(2)}, u32[]{:S(2)}) collective-permute-start(f32[2,280,256]{2,1,0:T(8,128)S(1)} %copy-done.36), channel_id=1, source_target_pairs={{0,1},{1,0},{2,3},{3,2},{4,5},{5,4},{6,7},{7,6},{8,9},{9,8},{10,11... | collective-permute-start | bytes 1720328 | tf_op jit(solution)/shard_map/ppermute | solution.py:677
  36.4 28.4 %collective-permute-start.7 = (s32[2,256,256]{2,1,0:T(8,128)S(1)}, s32[2,256,256]{2,1,0:T(8,128)S(1)}, u32[]{:S(2)}, u32[]{:S(2)}) collective-permute-start(s32[2,256,256]{2,1,0:T(8,128)S(1)} %get-tuple-element.74), channel_id=1, source_target_pairs={{0,1},{1,0},{2,3},{3,2},{4,5},{5,4},{6,7},{7,6},{8,9},{9,8},{10,11... | collective-permute-start | bytes 1572872 | tf_op jit(solution)/shard_map/ppermute | solution.py:677
  43.2 16.0 %copy-start.6 = (f32[2,280,256]{2,1,0:T(8,128)}, f32[2,280,256]{2,1,0:T(8,128)S(1)}, u32[]{:S(2)}) copy-start(f32[2,280,256]{2,1,0:T(8,128)S(1)} %collective-permute-done.4.w_ref.peer_w) | copy-start | bytes 1720324
  43.2 32.0 %collective-permute-start.10 = (f32[2,256,256]{2,1,0:T(8,128)S(1)}, f32[2,256,256]{2,1,0:T(8,128)S(1)}, u32[]{:S(2)}, u32[]{:S(2)}) collective-permute-start(f32[2,256,256]{2,1,0:T(8,128)S(1)} %slice.54), channel_id=1, source_target_pairs={{0,2},{1,31},{2,4},{3,1},{4,6},{5,3},{6,8},{7,5},{8,10},{9,7},{10,... | collective-permute-start | bytes 1572872 | tf_op jit(solution)/shard_map/ppermute | solution.py:686
  64.8 0.8 copy-start.7
  64.8 1.3 copy-start.3
  64.9 1.6 copy-start.5
  70.8 15.8 %collective-permute-start.8 = (f32[2,256,256]{2,1,0:T(8,128)}, f32[2,256,256]{2,1,0:T(8,128)S(1)}, u32[]{:S(2)}, u32[]{:S(2)}) collective-permute-start(f32[2,256,256]{2,1,0:T(8,128)} %get-tuple-element.42.far_u), channel_id=1, source_target_pairs={{0,2},{1,31},{2,4},{3,1},{4,6},{5,3},{6,8},{7,5},{8,10},{9,7},{10,... | collective-permute-start | bytes 1572872 | tf_op jit(solution)/shard_map/ppermute | solution.py:686
  72.2 14.5 %collective-permute-start.9 = (f32[2,256,256]{2,1,0:T(8,128)}, f32[2,256,256]{2,1,0:T(8,128)S(1)}, u32[]{:S(2)}, u32[]{:S(2)}) collective-permute-start(f32[2,256,256]{2,1,0:T(8,128)} %get-tuple-element.41.near_u), channel_id=1, source_target_pairs={{0,30},{1,3},{2,0},{3,5},{4,2},{5,7},{6,4},{7,9},{8,6},{9,11},{10,... | collective-permute-start | bytes 1572872 | tf_op jit(solution)/shard_map/ppermute | solution.py:689
  75.3 0.8 copy-start.23
  82.4 4.2 %collective-permute-start.11 = (f32[4,8,256]{2,1,0:T(8,128)}, f32[4,8,256]{2,1,0:T(8,128)S(1)}, u32[]{:S(2)}, u32[]{:S(2)}) collective-permute-start(f32[4,8,256]{2,1,0:T(8,128)} %get-tuple-element.48), channel_id=1, source_target_pairs={{0,1},{1,0},{2,3},{3,2},{4,5},{5,4},{6,7},{7,6},{8,9},{9,8},{10,11... | collective-permute-start | bytes 98312 | tf_op jit(solution)/shard_map/ppermute | solution.py:677
  86.6 23.4 %copy-start.10 = (f32[2,256,256]{2,1,0:T(8,128)S(1)}, f32[2,256,256]{2,1,0:T(8,128)}, u32[]{:S(2)}) copy-start(f32[2,256,256]{2,1,0:T(8,128)} %get-tuple-element.61.far_v) | copy-start | bytes 1572868
  86.6 23.4 %copy-start.11 = (f32[2,256,256]{2,1,0:T(8,128)S(1)}, f32[2,256,256]{2,1,0:T(8,128)}, u32[]{:S(2)}) copy-start(f32[2,256,256]{2,1,0:T(8,128)} %get-tuple-element.47.far_w) | copy-start | bytes 1572868
  86.6 0.8 copy-start.21
  87.4 0.8 copy-start.24
  93.4 5.4 %collective-permute-start.14 = (f32[4,32,256]{2,1,0:T(8,128)S(1)}, f32[4,32,256]{2,1,0:T(8,128)S(1)}, u32[]{:S(2)}, u32[]{:S(2)}) collective-permute-start(f32[4,32,256]{2,1,0:T(8,128)S(1)} %pad_maximum_fusion.4), channel_id=1, source_target_pairs={{0,1},{1,0},{2,3},{3,2},{4,5},{5,4},{6,7},{7,6},{8,9},{9,8},{10,11... | collective-permute-start | bytes 393224 | tf_op jit(solution)/shard_map/ppermute | solution.py:677
  95.0 15.1 %collective-permute-start.13 = (f32[2,256,256]{2,1,0:T(8,128)}, f32[2,256,256]{2,1,0:T(8,128)S(1)}, u32[]{:S(2)}, u32[]{:S(2)}) collective-permute-start(f32[2,256,256]{2,1,0:T(8,128)} %get-tuple-element.49.near_r), channel_id=1, source_target_pairs={{0,30},{1,3},{2,0},{3,5},{4,2},{5,7},{6,4},{7,9},{8,6},{9,11},{10,... | collective-permute-start | bytes 1572872 | tf_op jit(solution)/shard_map/ppermute | solution.py:689
  97.7 12.5 %collective-permute-start.12 = (f32[2,256,256]{2,1,0:T(8,128)}, f32[2,256,256]{2,1,0:T(8,128)S(1)}, u32[]{:S(2)}, u32[]{:S(2)}) collective-permute-start(f32[2,256,256]{2,1,0:T(8,128)} %get-tuple-element.50.far_r), channel_id=1, source_target_pairs={{0,2},{1,31},{2,4},{3,1},{4,6},{5,3},{6,8},{7,5},{8,10},{9,7},{10,... | collective-permute-start | bytes 1572872 | tf_op jit(solution)/shard_map/ppermute | solution.py:686
  98.7 11.4 %copy-start.25 = (f32[4,32,256]{2,1,0:T(8,128)}, f32[4,32,256]{2,1,0:T(8,128)S(1)}, u32[]{:S(2)}) copy-start(f32[4,32,256]{2,1,0:T(8,128)S(1)} %collective-permute-done.14.edge_ref) | copy-start | bytes 393220
  98.8 6.5 %collective-permute-start.16 = (f32[2,32,256]{2,1,0:T(8,128)S(1)}, f32[2,32,256]{2,1,0:T(8,128)S(1)}, u32[]{:S(2)}, u32[]{:S(2)}) collective-permute-start(f32[2,32,256]{2,1,0:T(8,128)S(1)} %get-tuple-element.80), channel_id=1, source_target_pairs={{0,30},{1,3},{2,0},{3,5},{4,2},{5,7},{6,4},{7,9},{8,6},{9,11},{10,... | collective-permute-start | bytes 196616 | tf_op jit(solution)/shard_map/ppermute | solution.py:689
  103.1 6.8 %collective-permute-start.15 = (f32[2,32,256]{2,1,0:T(8,128)S(1)}, f32[2,32,256]{2,1,0:T(8,128)S(1)}, u32[]{:S(2)}, u32[]{:S(2)}) collective-permute-start(f32[2,32,256]{2,1,0:T(8,128)S(1)} %get-tuple-element.81), channel_id=1, source_target_pairs={{0,2},{1,31},{2,4},{3,1},{4,6},{5,3},{6,8},{7,5},{8,10},{9,7},{10,... | collective-permute-start | bytes 196616 | tf_op jit(solution)/shard_map/ppermute | solution.py:686
  105.3 4.9 %copy-start.33 = (f32[2,32,256]{2,1,0:T(8,128)}, f32[2,32,256]{2,1,0:T(8,128)S(1)}, u32[]{:S(2)}) copy-start(f32[2,32,256]{2,1,0:T(8,128)S(1)} %collective-permute-done.16.right_edge) | copy-start | bytes 196612
  110.1 34.5 %collective-permute-start.20 = (f32[2,2,256,256]{3,2,1,0:T(8,128)S(1)}, f32[2,2,256,256]{3,2,1,0:T(8,128)S(1)}, u32[]{:S(2)}, u32[]{:S(2)}) collective-permute-start(f32[2,2,256,256]{3,2,1,0:T(8,128)S(1)} %pad_maximum_fusion.1), channel_id=1, source_target_pairs={{0,1},{1,0},{2,3},{3,2},{4,5},{5,4},{6,7},{7,6},{8,9},{9,8},{10,11... | collective-permute-start | bytes 3145736 | tf_op jit(solution)/shard_map/ppermute | solution.py:677
  110.2 0.8 copy-start.20
  111.0 0.8 copy-start.22
  119.2 10.7 %collective-permute-start.17 = (f32[432,256]{1,0:T(8,128)}, f32[432,256]{1,0:T(8,128)S(1)}, u32[]{:S(2)}, u32[]{:S(2)}) collective-permute-start(f32[432,256]{1,0:T(8,128)} %get-tuple-element.55), channel_id=1, source_target_pairs={{0,2},{1,31},{2,4},{3,1},{4,6},{5,3},{6,8},{7,5},{8,10},{9,7},{10,... | collective-permute-start | bytes 1327112 | tf_op jit(solution)/shard_map/ppermute | solution.py:686
  120.9 9.0 %collective-permute-start.18 = (f32[432,256]{1,0:T(8,128)}, f32[432,256]{1,0:T(8,128)S(1)}, u32[]{:S(2)}, u32[]{:S(2)}) collective-permute-start(f32[432,256]{1,0:T(8,128)} %get-tuple-element.56), channel_id=1, source_target_pairs={{0,30},{1,3},{2,0},{3,5},{4,2},{5,7},{6,4},{7,9},{8,6},{9,11},{10,... | collective-permute-start | bytes 1327112 | tf_op jit(solution)/shard_map/ppermute | solution.py:689
  130.0 0.8 copy-start.13
  130.0 1.0 copy-start.14
  134.4 19.4 %copy-start.9 = (f32[2,256,256]{2,1,0:T(8,128)S(1)}, f32[2,256,256]{2,1,0:T(8,128)}, u32[]{:S(2)}) copy-start(f32[2,256,256]{2,1,0:T(8,128)} %get-tuple-element.67.far_base.far_ref) | copy-start | bytes 1572868
  134.4 19.7 %copy-start.8 = (f32[2,256,256]{2,1,0:T(8,128)S(1)}, f32[2,256,256]{2,1,0:T(8,128)}, u32[]{:S(2)}) copy-start(f32[2,256,256]{2,1,0:T(8,128)} %get-tuple-element.68.near_base.near_ref) | copy-start | bytes 1572868
  138.0 6.5 %collective-permute-start.19 = (f32[1,144,128]{2,1,0:T(8,128)S(1)}, f32[1,144,128]{2,1,0:T(8,128)S(1)}, u32[]{:S(2)}, u32[]{:S(2)}) collective-permute-start(f32[1,144,128]{2,1,0:T(8,128)S(1)} %get-tuple-element.79), channel_id=1, source_target_pairs={{0,2},{1,31},{2,4},{3,1},{4,6},{5,3},{6,8},{7,5},{8,10},{9,7},{10,... | collective-permute-start | bytes 221192 | tf_op jit(solution)/shard_map/ppermute | solution.py:686
  142.2 2.4 %collective-permute-start.21 = (f32[1,144,128]{2,1,0:T(8,128)S(1)}, f32[1,144,128]{2,1,0:T(8,128)S(1)}, u32[]{:S(2)}, u32[]{:S(2)}) collective-permute-start(f32[1,144,128]{2,1,0:T(8,128)S(1)} %get-tuple-element.78), channel_id=1, source_target_pairs={{0,30},{1,3},{2,0},{3,5},{4,2},{5,7},{6,4},{7,9},{8,6},{9,11},{10,... | collective-permute-start | bytes 221192 | tf_op jit(solution)/shard_map/ppermute | solution.py:689
  144.6 33.6 %copy-start.17 = (f32[2,2,256,256]{3,2,1,0:T(8,128)}, f32[2,2,256,256]{3,2,1,0:T(8,128)S(1)}, u32[]{:S(2)}) copy-start(f32[2,2,256,256]{3,2,1,0:T(8,128)S(1)} %collective-permute-done.20.peer_vw) | copy-start | bytes 3145732
  147.7 10.7 %copy-start.28 = (f32[2,128,128]{2,1,0:T(8,128)S(1)}, f32[2,128,128]{2,1,0:T(8,128)}, u32[]{:S(2)}) copy-start(f32[2,128,128]{2,1,0:T(8,128)} %shard_map.257) | copy-start | bytes 393220
  149.3 30.1 %all-to-all-start = ((f32[32,32,128]{2,1,0:T(8,128)}), f32[32,32,128]{2,1,0:T(8,128)S(1)}, u32[]{:S(2)}, u32[]{:S(2)}) async-start(f32[32,32,128]{2,1,0:T(8,128)} %broadcast_in_dim.3), calls=%async_computation | async-start | bytes 1048576 | tf_op jit(solution)/shard_map/all_to_all | solution.py:859
  153.8 19.7 %collective-permute-start.26 = (f32[2,256,256]{2,1,0:T(8,128)S(1)}, f32[2,256,256]{2,1,0:T(8,128)S(1)}, u32[]{:S(2)}, u32[]{:S(2)}) collective-permute-start(f32[2,256,256]{2,1,0:T(8,128)S(1)} %copy-done.9), channel_id=1, source_target_pairs={{0,2},{1,31},{2,4},{3,1},{4,6},{5,3},{6,8},{7,5},{8,10},{9,7},{10,... | collective-permute-start | bytes 1572872 | tf_op jit(solution)/shard_map/ppermute | solution.py:686
  154.2 19.4 %collective-permute-start.27 = (f32[2,256,256]{2,1,0:T(8,128)S(1)}, f32[2,256,256]{2,1,0:T(8,128)S(1)}, u32[]{:S(2)}, u32[]{:S(2)}) collective-permute-start(f32[2,256,256]{2,1,0:T(8,128)S(1)} %copy-done.8), channel_id=1, source_target_pairs={{0,30},{1,3},{2,0},{3,5},{4,2},{5,7},{6,4},{7,9},{8,6},{9,11},{10,... | collective-permute-start | bytes 1572872 | tf_op jit(solution)/shard_map/ppermute | solution.py:689
  158.3 5.9 %collective-permute-start.22 = (f32[2,128,128]{2,1,0:T(8,128)S(1)}, f32[2,128,128]{2,1,0:T(8,128)S(1)}, u32[]{:S(2)}, u32[]{:S(2)}) collective-permute-start(f32[2,128,128]{2,1,0:T(8,128)S(1)} %copy-done.28), channel_id=1, source_target_pairs={{0,1},{1,0},{2,3},{3,2},{4,5},{5,4},{6,7},{7,6},{8,9},{9,8},{10,11... | collective-permute-start | bytes 393224 | tf_op jit(solution)/shard_map/ppermute | solution.py:677
  164.3 23.6 %collective-permute-start.25 = (f32[2,256,256]{2,1,0:T(8,128)S(1)}, f32[2,256,256]{2,1,0:T(8,128)S(1)}, u32[]{:S(2)}, u32[]{:S(2)}) collective-permute-start(f32[2,256,256]{2,1,0:T(8,128)S(1)} %copy-done.9), channel_id=1, source_target_pairs={{0,1},{1,0},{2,3},{3,2},{4,5},{5,4},{6,7},{7,6},{8,9},{9,8},{10,11... | collective-permute-start | bytes 1572872 | tf_op jit(solution)/shard_map/ppermute | solution.py:677
  173.5 0.8 copy-start.26
  174.3 0.8 copy-start.27
  178.1 22.8 %collective-permute-start.28 = (f32[2,256,256]{2,1,0:T(8,128)}, f32[2,256,256]{2,1,0:T(8,128)S(1)}, u32[]{:S(2)}, u32[]{:S(2)}) collective-permute-start(f32[2,256,256]{2,1,0:T(8,128)} %get-tuple-element.70), channel_id=1, source_target_pairs={{0,1},{1,0},{2,3},{3,2},{4,5},{5,4},{6,7},{7,6},{8,9},{9,8},{10,11... | collective-permute-start | bytes 1572872 | tf_op jit(solution)/shard_map/ppermute | solution.py:677
  178.9 9.1 %copy-start.16 = (f32[2,2,128,128]{3,2,1,0:T(8,128)}, f32[2,2,128,128]{3,2,1,0:T(8,128)S(1)}, u32[]{:S(2)}) copy-start(f32[2,2,128,128]{3,2,1,0:T(8,128)S(1)} %pad_maximum_fusion.2.own_mid) | copy-start | bytes 786436
  178.9 4.8 %collective-permute-start.24 = (f32[2,2,128,128]{3,2,1,0:T(8,128)S(1)}, f32[2,2,128,128]{3,2,1,0:T(8,128)S(1)}, u32[]{:S(2)}, u32[]{:S(2)}) collective-permute-start(f32[2,2,128,128]{3,2,1,0:T(8,128)S(1)} %pad_maximum_fusion.2.own_mid), channel_id=1, source_target_pairs={{0,30},{1,3},{2,0},{3,5},{4,2},{5,7},{6,4},{7,9},{8,6},{9,11},{10,... | collective-permute-start | bytes 786440 | tf_op jit(solution)/shard_map/ppermute | solution.py:689
  179.4 8.5 %collective-permute-start.23 = (f32[2,2,128,128]{3,2,1,0:T(8,128)S(1)}, f32[2,2,128,128]{3,2,1,0:T(8,128)S(1)}, u32[]{:S(2)}, u32[]{:S(2)}) collective-permute-start(f32[2,2,128,128]{3,2,1,0:T(8,128)S(1)} %pad_maximum_fusion.2.own_mid), channel_id=1, source_target_pairs={{0,2},{1,31},{2,4},{3,1},{4,6},{5,3},{6,8},{7,5},{8,10},{9,7},{10,... | collective-permute-start | bytes 786440 | tf_op jit(solution)/shard_map/ppermute | solution.py:686
  179.4 0.8 copy-start.12
  183.6 4.3 %copy-start.29 = (f32[2,2,128,128]{3,2,1,0:T(8,128)}, f32[2,2,128,128]{3,2,1,0:T(8,128)S(1)}, u32[]{:S(2)}) copy-start(f32[2,2,128,128]{3,2,1,0:T(8,128)S(1)} %collective-permute-done.24.right_mid) | copy-start | bytes 786436
  187.9 0.7 copy-start.30
  188.6 0.8 copy-start.18
  201.0 0.8 copy-start.19
  (4 other events, 2.5 us)

commit v3 on v2

--- a/solution.py
+++ b/solution.py
@@ -1,4 +1,3 @@
-import functools
 import math
 
 import jax
@@ -305,7 +304,7 @@
         in_specs=specs,
         out_specs=[VMEM] * len(outs) if out_specs is None else out_specs,
         scratch_shapes=scratch,
-        compiler_params=pltpu.CompilerParams(vmem_limit_bytes=56 * 1024 * 1024),
+        compiler_params=pltpu.CompilerParams(vmem_limit_bytes=36 * 1024 * 1024),
         cost_estimate=pl.CostEstimate(flops=flops, bytes_accessed=total if flops > 1 else 1, transcendentals=0),
         **options,
     )(*args)
@@ -449,7 +448,7 @@
 def fine_kernel(
     pressure_tall, pressure_left, pressure_right,
     near_r, far_r, left_ref, right_ref, edge_ref, left_edge, right_edge, depth_pick, rows_pick,
-    base_ref, coarse_ref, ahead_ref, behind_ref, source_ref, pressure_ref, one, two,
+    base_ref, coarse_ref, ahead_ref, behind_ref, source_ref, one, two,
 ):
     side = lax.axis_index("group")
     half = near_r.shape[1]
@@ -464,15 +463,12 @@
         fill(source_ref, 2 + plane, near_r[plane], edge_ref[3 - plane])
         fill(source_ref, 4 + plane, far_r[plane], edge_ref[1 - plane])
         fill(source_ref, 6 + plane, right_ref[plane], right_edge[1 - plane])
-    for plane in range(3):
-        at = mirror(side, plane, 3)
-        pressure_ref[plane] = pressure_left[at]
-        pressure_ref[7 + plane] = pressure_right[at]
-    for plane in range(4):
-        pressure_ref[3 + plane] = pressure_tall[mirror(side, plane, 4)]
+    pressure = [pressure_left.at[mirror(side, k, 3)] for k in range(3)]
+    pressure += [pressure_tall.at[mirror(side, k, 4)] for k in range(4)]
+    pressure += [pressure_right.at[mirror(side, k, 3)] for k in range(3)]
     for k in range(8):
-        centre = pressure_ref[k + 1]
-        total = pressure_ref[k] + pressure_ref[k + 2] + cross_sum(centre)
+        centre = pressure[k + 1][...]
+        total = pressure[k][...] + pressure[k + 2][...] + cross_sum(centre)
         one[k] = centre + weight * (total - 6.0 * centre - source_ref[k])
     for k in range(6):
         centre = one[k + 1]
@@ -583,7 +579,7 @@
     spread_ref, own_mid, left_mid, right_mid,
     near_base, far_base, peer_base, near_v, near_w, peer_vw, solid_ref,
     sum_high, sum_low, diff_high, diff_low, depth_high, depth_low, fine_depth, fine_rows,
-    out_ref, potential_ref, base, mid, fine, first_sweep, delta, section,
+    out_ref, potential_ref, base, mid, fine, first_sweep, delta,
 ):
     side = lax.axis_index("group")
     sign = sign_of(side)
@@ -623,21 +619,18 @@
     for k in range(2):
         at = 2 + k
         index = mirror(side, k, 2)
-        section[peer_rows] = delta[at, peer_rows] + peer_base[1 - k]
-        section[own_rows] = delta[at, own_rows] + near_base[k]
-        value = section[...]
-        keep = 1.0 - solid_ref[index].astype(f32)
         out_ref[0, index] = sign * first_of([delta[at + offset] for offset in range(-2, 3)])
-        out_ref[2, index, own_rows] = near_w[k]
-        out_ref[2, index, peer_rows] = peer_vw[1, 1 - k]
-        out_ref[2, index] = (out_ref[2, index] - dot_right(value, depth_high[...], depth_low[...])) * keep
-        out_ref[1, index, own_rows] = near_v[k]
-        out_ref[1, index, peer_rows] = peer_vw[0, 1 - k]
-        top, low = (value[:half], value[half:])
-        even = dot_left(sum_high[...], sum_low[...], top + low)
-        odd = dot_left(diff_high[...], diff_low[...], top - low)
-        out_ref[1, index, :half] = (out_ref[1, index, :half] - (even + odd)) * keep[:half]
-        out_ref[1, index, half:] = (out_ref[1, index, half:] - (even - odd)) * keep[half:]
+        own = delta[at, own_rows] + near_base[k]
+        peer = delta[at, peer_rows] + peer_base[1 - k]
+        even = dot_left(sum_high[...], sum_low[...], own + peer)
+        odd = dot_left(diff_high[...], diff_low[...], own - peer)
+        for rows, value, gradient, v, w in (
+            (own_rows, own, even + odd, near_v[k], near_w[k]),
+            (peer_rows, peer, even - odd, peer_vw[0, 1 - k], peer_vw[1, 1 - k]),
+        ):
+            keep = 1.0 - solid_ref[index, rows].astype(f32)
+            out_ref[1, index, rows] = (v - gradient) * keep
+            out_ref[2, index, rows] = (w - dot_right(value, depth_high[...], depth_low[...])) * keep
 
 
 def stream_correction_kernel(gradient_ref, own_u, peer_u, solid_ref, out_ref):
@@ -732,7 +725,6 @@
     own_half = half_of(tied(velocity, sent_w), side, 2)
     one = behind(own_half)
     other_uv = ahead(peer_uv)
-    other_w = ahead(peer_w[:, :half])
     solid_peer = swap(half_of(obstacle, 1 - side, 1))
     solid_own = half_of(obstacle, side, 1)
     (raw_peer,) = kernel_call(
@@ -745,6 +737,7 @@
         grid=(2,),
         out_specs=[by_plane((3, 2) + plane, 1)],
     )
+    other_w = ahead(tied(peer_w, raw_peer, solid_peer)[:, :half])
     strip = 64
 
     def strips(count, first=0):
@@ -811,7 +804,6 @@
         [(4, wide, depth), (2, mid_rows, mid_depth), message, message],
         [
             pltpu.VMEM((8, wide, depth), f32),
-            pltpu.VMEM((10, wide, depth), f32),
             pltpu.VMEM((8, wide, depth), f32),
             pltpu.VMEM((6, wide, depth), f32),
         ],
@@ -861,18 +853,8 @@
     )
     left_b, right_b = (ahead(tied(far_base, mid_base)), behind(tied(near_base, mid_base)))
     peer_base = swap(tied(far_base, peer_mid))
-    own_u, sent_u = kernel_call(
-        stream_kernel,
-        [two_planes, two_planes],
-        [],
-        [VMEM] * 6,
-        10**8,
-        near_base, far_base, left_b, right_b, near_u, far_u,
-    )
-    peer_u = swap(sent_u)
     low_plane = (half // 2, mid_depth)
     mid_plane = (half, mid_depth)
-    fine_plane = (rows, depth)
     expand_low = np.zeros((mid_depth, mid_depth), ml_dtypes.bfloat16)
     expand_low[:low_depth] = pair_sums(mid_depth, low_depth).T
     (spread_low,) = kernel_call(
@@ -883,6 +865,16 @@
         10**7,
         low_all, expand_low, pair_sums(half, half // 2),
     )
+    own_u, sent_u = kernel_call(
+        stream_kernel,
+        [two_planes, two_planes],
+        [],
+        [VMEM] * 6,
+        10**8,
+        near_base, far_base, left_b, tied(right_b, spread_low, left_mid, right_mid), near_u, far_u,
+    )
+    peer_u = swap(sent_u)
+    fine_plane = (rows, depth)
     corrected, potential = kernel_call(
         correction_kernel,
         [(3, 2) + fine_plane, four_planes],
@@ -892,7 +884,6 @@
             pltpu.VMEM((5,) + fine_plane, f32),
             pltpu.VMEM((8,) + fine_plane, f32),
             pltpu.VMEM((6,) + fine_plane, f32),
-            pltpu.VMEM(fine_plane, f32),
         ],
         [VMEM] * 19,
         10**9,

time: 205 us -> 182 us (0.89)
  Pallas kernels: 67 us -> 36.5 us
  starting transfers between devices: 65.5 us -> 84.5 us
  local copies, waits for them, and re-layouts: 19.8 us -> 11 us
  waiting for transfers between devices: 48.7 us -> 42.4 us
    pallas_call x14, Pallas kernels: 67 us -> 36.5 us  [kernel_call(): pl.pallas_call(body, out_shape=[jax.ShapeDtypeStruct(s, f32) for s in out...]
    ppermute x10, starting transfers between devices: 23.5 us -> 35.1 us  [ahead(): return lax.ppermute(value, both, ahead_way)]
    ppermute x10, waiting for transfers between devices: 25.4 us -> 15.7 us  [ahead(): return lax.ppermute(value, both, ahead_way)]
    unnamed x74 -> x90, local copies, waits for them, and re-layouts: 12.6 us -> 4.78 us
    ppermute x10, starting transfers between devices: 11.9 us -> 18.5 us  [swap(): return lax.ppermute(value, 'group', [(0, 1), (1, 0)])]
    ppermute x10, waiting for transfers between devices: 21.1 us -> 23.8 us  [swap(): return lax.ppermute(value, 'group', [(0, 1), (1, 0)])]
    all_to_all x1, starting transfers between devices: 4.53 us -> 6.67 us  [paired(): lax.all_to_all(jnp.broadcast_to(tied(low_source, mid_base), (2 * tunnel_s...]
  transfers between devices with their start and end apart: 30 -> 30, of which waited for: 11 -> 13; matrix products, arithmetic and copies ran while one was open for 2% -> 4% of each run, Pallas kernels for 28% -> 18%
where the time goes in v3:
time: 182 us; the launch traced here: 180 us
  starting transfers between devices  84.5 us (46%)
  waiting for transfers between devices  42.4 us (23%)
  Pallas kernels  36.5 us (20%)
  local copies, waits for them, and re-layouts  11 us (6%)
  other arithmetic  3.81 us (2%)
    pallas_call x14, Pallas kernels, kernel_call(): pl.pallas_call(body, out_shape=[jax.ShapeDtypeStruct(s, f32) for s in out...  36.5 us
    ppermute x10, starting transfers between devices, ahead(): return lax.ppermute(value, both, ahead_way)  35.1 us
    ppermute x9, starting transfers between devices, behind(): return lax.ppermute(value, both, behind_way)  24.2 us
    ppermute x10, waiting for transfers between devices, swap(): return lax.ppermute(value, 'group', [(0, 1), (1, 0)])  23.8 us
    ppermute x10, starting transfers between devices, swap(): return lax.ppermute(value, 'group', [(0, 1), (1, 0)])  18.5 us
    ppermute x10, waiting for transfers between devices, ahead(): return lax.ppermute(value, both, ahead_way)  15.7 us
    all_to_all x1, starting transfers between devices, paired(): lax.all_to_all(jnp.broadcast_to(tied(low_source, mid_base), (2 * tunnel_s...  6.67 us
    unnamed x90, local copies, waits for them, and re-layouts  4.78 us
  transfers between devices with their start and end apart: 30, of which 13 were waited for; matrix products, arithmetic and copies ran while one was open for 4% of the time, Pallas kernels for 18%

profile of v3, /device:TPU:0, one launch (start us, length us, event | category | flops | bytes accessed | tf_op | source)
XLA Modules:
  0.0 179.6 jit_solution(13397426084196989365)
XLA Ops:
  0.6 0.9 fusion
  1.5 3.0 %collective-permute-start = (f32[4,32,256]{2,1,0:T(8,128)S(1)}, f32[4,32,256]{2,1,0:T(8,128)S(1)}, u32[]{:S(2)}, u32[]{:S(2)}) collective-permute-start(f32[4,32,256]{2,1,0:T(8,128)S(1)} %pad_maximum_fusion.3), channel_id=1, source_target_pairs={{0,1},{1,0},{2,3},{3,2},{4,5},{5,4},{6,7},{7,6},{8,9},{9,8},{10,11... | collective-permute-start | bytes 393224 | tf_op jit(solution)/shard_map/ppermute | solution.py:670
  4.6 1.6 slice-done
  6.2 1.1 constant_dynamic-slice_fusion.3
  7.2 0.8 collective-permute-done
  8.1 1.4 pad_maximum_fusion.pressure_tall
  9.6 1.4 slice_select_fusion
  11.0 3.3 %collective-permute-start.2 = (f32[3,288,256]{2,1,0:T(8,128)}, f32[3,288,256]{2,1,0:T(8,128)}, u32[]{:S(2)}, u32[]{:S(2)}) collective-permute-start(f32[3,288,256]{2,1,0:T(8,128)} %get-tuple-element.76), channel_id=1, source_target_pairs={{0,30},{1,3},{2,0},{3,5},{4,2},{5,7},{6,4},{7,9},{8,6},{9,11},{10,... | collective-permute-start | bytes 2654216 | tf_op jit(solution)/shard_map/ppermute | solution.py:682
  14.3 4.0 %shard_map.248 = (f32[3,2,256,256]{3,2,1,0:T(8,128)S(1)}, f32[2,280,256]{2,1,0:T(8,128)S(1)}) custom-call(f32[3,2,512,256]{3,2,1,0:T(8,128)S(1)} %copy-done.3, bf16[16,256]{1,0:T(8,128)(2,1)S(1)} %copy-done.44, bf16[512,256]{1,0:T(8,128)(2,1)S(1)} %copy-done.23, bf16[512,256]{1,0:T(8,128)(2,1)S(1)} %copy-done.21, bf16[512,32]{1,0:T(8,128)(2,1)S(1)} %copy-done.42, ...), custom_call_target="tpu_custom_call" | custom-call | flops 3000000000 | bytes 6381568 | tf_op jit(solution)/shard_map/pallas_call | solution.py:301
  18.4 1.1 copy-done.1
  19.5 0.8 copy-done.36
  20.4 1.7 constant_dynamic-slice_fusion.2.own_ref
  22.2 4.5 %collective-permute-start.5 = (f32[3,2,256,256]{3,2,1,0:T(8,128)S(1)}, f32[3,2,256,256]{3,2,1,0:T(8,128)S(1)}, u32[]{:S(2)}, u32[]{:S(2)}) collective-permute-start(f32[3,2,256,256]{3,2,1,0:T(8,128)S(1)} %constant_dynamic-slice_fusion.2.own_ref), channel_id=1, source_target_pairs={{0,30},{1,3},{2,0},{3,5},{4,2},{5,7},{6,4},{7,9},{8,6},{9,11},{10,... | collective-permute-start | bytes 4718600 | tf_op jit(solution)/shard_map/ppermute | solution.py:682
  26.6 5.4 %collective-permute-done.3.uv_ref.peers = f32[2,2,256,256]{3,2,1,0:T(8,128)S(1)} collective-permute-done((f32[2,2,256,256]{3,2,1,0:T(8,128)}, f32[2,2,256,256]{3,2,1,0:T(8,128)S(1)}, u32[]{:S(2)}, u32[]{:S(2)}) %collective-permute-start.3) | collective-permute-done | bytes 1048608 | tf_op jit(solution)/shard_map/ppermute | solution.py:670
  32.1 3.4 %collective-permute-start.4 = (f32[2,280,256]{2,1,0:T(8,128)S(1)}, f32[2,280,256]{2,1,0:T(8,128)S(1)}, u32[]{:S(2)}, u32[]{:S(2)}) collective-permute-start(f32[2,280,256]{2,1,0:T(8,128)S(1)} %copy-done.37), channel_id=1, source_target_pairs={{0,1},{1,0},{2,3},{3,2},{4,5},{5,4},{6,7},{7,6},{8,9},{9,8},{10,11... | collective-permute-start | bytes 1720328 | tf_op jit(solution)/shard_map/ppermute | solution.py:670
  35.5 0.1 constant_dynamic-slice_fusion
  35.6 0.1 collective-permute-start.7
  35.7 7.5 %collective-permute-done.4.w_ref.peer_w = f32[2,280,256]{2,1,0:T(8,128)S(1)} collective-permute-done((f32[2,280,256]{2,1,0:T(8,128)S(1)}, f32[2,280,256]{2,1,0:T(8,128)S(1)}, u32[]{:S(2)}, u32[]{:S(2)}) %collective-permute-start.4) | collective-permute-done | bytes 573472 | tf_op jit(solution)/shard_map/ppermute | solution.py:670
  43.2 3.5 %shard_map.249.raw_peer = f32[3,2,256,256]{3,2,1,0:T(8,128)S(1)} custom-call(f32[2,2,256,256]{3,2,1,0:T(8,128)S(1)} %collective-permute-done.3.uv_ref.peers, f32[2,280,256]{2,1,0:T(8,128)S(1)} %collective-permute-done.4.w_ref.peer_w, bf16[512,256]{1,0:T(8,128)(2,1)S(1)} %copy-done.24, bf16[512,256]{1,0:T(8,128)(2,1)S(1)} %copy-done.21, ...), custom_call_target="tpu_custom_call" | custom-call | flops 3000000000 | bytes 4276224 | tf_op jit(solution)/shard_map/pallas_call | solution.py:301
  46.7 2.1 %collective-permute-done.7.solid_peer = s32[2,256,256]{2,1,0:T(8,128)S(1)} collective-permute-done((s32[2,256,256]{2,1,0:T(8,128)S(1)}, s32[2,256,256]{2,1,0:T(8,128)S(1)}, u32[]{:S(2)}, u32[]{:S(2)}) %collective-permute-start.7) | collective-permute-done | bytes 524320 | tf_op jit(solution)/shard_map/ppermute | solution.py:670
  48.9 17.1 %collective-permute-start.10 = (f32[2,256,256]{2,1,0:T(8,128)S(1)}, f32[2,256,256]{2,1,0:T(8,128)S(1)}, u32[]{:S(2)}, u32[]{:S(2)}) collective-permute-start(f32[2,256,256]{2,1,0:T(8,128)S(1)} %slice.45), channel_id=1, source_target_pairs={{0,2},{1,31},{2,4},{3,1},{4,6},{5,3},{6,8},{7,5},{8,10},{9,7},{10,... | collective-permute-start | bytes 1572872 | tf_op jit(solution)/shard_map/ppermute | solution.py:679
  66.0 1.1 shard_map.250
  67.1 1.4 collective-permute-start.8
  68.6 3.1 %collective-permute-start.9 = (f32[2,256,256]{2,1,0:T(8,128)S(1)}, f32[2,256,256]{2,1,0:T(8,128)S(1)}, u32[]{:S(2)}, u32[]{:S(2)}) collective-permute-start(f32[2,256,256]{2,1,0:T(8,128)S(1)} %get-tuple-element.43.near_u), channel_id=1, source_target_pairs={{0,30},{1,3},{2,0},{3,5},{4,2},{5,7},{6,4},{7,9},{8,6},{9,11},{10,... | collective-permute-start | bytes 1572872 | tf_op jit(solution)/shard_map/ppermute | solution.py:682
  71.6 3.0 %shard_map.251 = (f32[2,256,256]{2,1,0:T(8,128)S(1)}, f32[2,256,256]{2,1,0:T(8,128)S(1)}, f32[2,256,256]{2,1,0:T(8,128)S(1)}, f32[2,256,256]{2,1,0:T(8,128)S(1)}, f32[4,8,256]{2,1,0:T(8,128)S(1)}) custom-call(f32[3,2,256,256]{3,2,1,0:T(8,128)S(1)} %copy-done.2, f32[3,2,256,256]{3,2,1,0:T(8,128)S(1)} %shard_map.249.raw_peer, ...), custom_call_target="tpu_custom_call" | custom-call | flops 100000000 | bytes 12673024 | tf_op jit(solution)/shard_map/pallas_call | solution.py:301
  74.7 0.6 collective-permute-start.11
  75.3 1.0 shard_map.252.cross_ref
  76.3 2.4 %collective-permute-done.11.sum_ref = f32[4,8,256]{2,1,0:T(8,128)S(1)} collective-permute-done((f32[4,8,256]{2,1,0:T(8,128)S(1)}, f32[4,8,256]{2,1,0:T(8,128)S(1)}, u32[]{:S(2)}, u32[]{:S(2)}) %collective-permute-start.11) | collective-permute-done | bytes 32800 | tf_op jit(solution)/shard_map/ppermute | solution.py:670
  78.7 1.1 shard_map.253
  79.8 4.9 %collective-permute-start.14 = (f32[4,32,256]{2,1,0:T(8,128)S(1)}, f32[4,32,256]{2,1,0:T(8,128)S(1)}, u32[]{:S(2)}, u32[]{:S(2)}) collective-permute-start(f32[4,32,256]{2,1,0:T(8,128)S(1)} %pad_maximum_fusion.4), channel_id=1, source_target_pairs={{0,1},{1,0},{2,3},{3,2},{4,5},{5,4},{6,7},{7,6},{8,9},{9,8},{10,11... | collective-permute-start | bytes 393224 | tf_op jit(solution)/shard_map/ppermute | solution.py:670
  84.7 7.0 %collective-permute-start.12 = (f32[2,256,256]{2,1,0:T(8,128)S(1)}, f32[2,256,256]{2,1,0:T(8,128)S(1)}, u32[]{:S(2)}, u32[]{:S(2)}) collective-permute-start(f32[2,256,256]{2,1,0:T(8,128)S(1)} %get-tuple-element.53.far_r), channel_id=1, source_target_pairs={{0,2},{1,31},{2,4},{3,1},{4,6},{5,3},{6,8},{7,5},{8,10},{9,7},{10,... | collective-permute-start | bytes 1572872 | tf_op jit(solution)/shard_map/ppermute | solution.py:679
  91.7 4.8 %collective-permute-start.16 = (f32[2,32,256]{2,1,0:T(8,128)S(1)}, f32[2,32,256]{2,1,0:T(8,128)S(1)}, u32[]{:S(2)}, u32[]{:S(2)}) collective-permute-start(f32[2,32,256]{2,1,0:T(8,128)S(1)} %get-tuple-element.84), channel_id=1, source_target_pairs={{0,30},{1,3},{2,0},{3,5},{4,2},{5,7},{6,4},{7,9},{8,6},{9,11},{10,... | collective-permute-start | bytes 196616 | tf_op jit(solution)/shard_map/ppermute | solution.py:682
  96.4 1.9 %collective-permute-done.16.right_edge = f32[2,32,256]{2,1,0:T(8,128)S(1)} collective-permute-done((f32[2,32,256]{2,1,0:T(8,128)S(1)}, f32[2,32,256]{2,1,0:T(8,128)S(1)}, u32[]{:S(2)}, u32[]{:S(2)}) %collective-permute-start.16) | collective-permute-done | bytes 65568 | tf_op jit(solution)/shard_map/ppermute | solution.py:682
  98.3 5.7 %collective-permute-done.15.left_edge = f32[2,32,256]{2,1,0:T(8,128)S(1)} collective-permute-done((f32[2,32,256]{2,1,0:T(8,128)S(1)}, f32[2,32,256]{2,1,0:T(8,128)S(1)}, u32[]{:S(2)}, u32[]{:S(2)}) %collective-permute-start.15) | collective-permute-done | bytes 65568 | tf_op jit(solution)/shard_map/ppermute | solution.py:679
  104.0 0.1 pad_maximum_fusion.1
  104.1 0.1 collective-permute-start.20
  104.2 5.6 %shard_map.254 = (f32[4,288,256]{2,1,0:T(8,128)S(1)}, f32[2,144,128]{2,1,0:T(8,128)S(1)}, f32[432,256]{1,0:T(8,128)S(1)}, f32[432,256]{1,0:T(8,128)S(1)}) custom-call(f32[4,288,256]{2,1,0:T(8,128)S(1)} %pad_maximum_fusion.pressure_tall, f32[3,288,256]{2,1,0:T(8,128)} %collective-permute-done.1.pressure_left, ...), custom_call_target="tpu_custom_call" | custom-call | flops 100000000 | bytes 7668736 | tf_op jit(solution)/shard_map/pallas_call | solution.py:301
  109.8 4.3 %collective-permute-start.17 = (f32[432,256]{1,0:T(8,128)S(1)}, f32[432,256]{1,0:T(8,128)S(1)}, u32[]{:S(2)}, u32[]{:S(2)}) collective-permute-start(f32[432,256]{1,0:T(8,128)S(1)} %get-tuple-element.58), channel_id=1, source_target_pairs={{0,2},{1,31},{2,4},{3,1},{4,6},{5,3},{6,8},{7,5},{8,10},{9,7},{10,... | collective-permute-start | bytes 1327112 | tf_op jit(solution)/shard_map/ppermute | solution.py:679
  114.1 0.2 collective-permute-start.18
  114.3 6.0 %collective-permute-done.17.left_ref = f32[432,256]{1,0:T(8,128)S(1)} collective-permute-done((f32[432,256]{1,0:T(8,128)S(1)}, f32[432,256]{1,0:T(8,128)S(1)}, u32[]{:S(2)}, u32[]{:S(2)}) %collective-permute-start.17) | collective-permute-done | bytes 442400 | tf_op jit(solution)/shard_map/ppermute | solution.py:679
  120.3 0.9 shard_map.255
  121.2 0.7 shard_map.256
  122.0 5.3 %collective-permute-start.19 = (f32[1,144,128]{2,1,0:T(8,128)S(1)}, f32[1,144,128]{2,1,0:T(8,128)S(1)}, u32[]{:S(2)}, u32[]{:S(2)}) collective-permute-start(f32[1,144,128]{2,1,0:T(8,128)S(1)} %get-tuple-element.83), channel_id=1, source_target_pairs={{0,2},{1,31},{2,4},{3,1},{4,6},{5,3},{6,8},{7,5},{8,10},{9,7},{10,... | collective-permute-start | bytes 221192 | tf_op jit(solution)/shard_map/ppermute | solution.py:679
  127.3 1.2 collective-permute-done.19.left_ref
  128.6 1.0 copy-done.12
  129.5 1.0 collective-permute-done.21.right_ref
  130.5 0.1 shard_map.257
  130.7 0.9 broadcast_in_dim.3
  131.6 6.7 %all-to-all-start = ((f32[32,32,128]{2,1,0:T(8,128)}), f32[32,32,128]{2,1,0:T(8,128)}, u32[]{:S(2)}, u32[]{:S(2)}) async-start(f32[32,32,128]{2,1,0:T(8,128)} %broadcast_in_dim.3), calls=%async_computation | async-start | bytes 1048576 | tf_op jit(solution)/shard_map/all_to_all | solution.py:851
  138.3 4.3 %collective-permute-start.27 = (f32[2,256,256]{2,1,0:T(8,128)S(1)}, f32[2,256,256]{2,1,0:T(8,128)}, u32[]{:S(2)}, u32[]{:S(2)}) collective-permute-start(f32[2,256,256]{2,1,0:T(8,128)S(1)} %get-tuple-element.71.near_base.near_ref), channel_id=1, source_target_pairs={{0,30},{1,3},{2,0},{3,5},{4,2},{5,7},{6,4},{7,9},{8,6},{9,11},{10,... | collective-permute-start | bytes 1572872 | tf_op jit(solution)/shard_map/ppermute | solution.py:682
  142.5 1.9 %collective-permute-start.22 = (f32[2,128,128]{2,1,0:T(8,128)S(1)}, f32[2,128,128]{2,1,0:T(8,128)S(1)}, u32[]{:S(2)}, u32[]{:S(2)}) collective-permute-start(f32[2,128,128]{2,1,0:T(8,128)S(1)} %shard_map.257), channel_id=1, source_target_pairs={{0,1},{1,0},{2,3},{3,2},{4,5},{5,4},{6,7},{7,6},{8,9},{9,8},{10,11... | collective-permute-start | bytes 393224 | tf_op jit(solution)/shard_map/ppermute | solution.py:670
  144.4 4.2 %collective-permute-done.22 = f32[2,128,128]{2,1,0:T(8,128)S(1)} collective-permute-done((f32[2,128,128]{2,1,0:T(8,128)S(1)}, f32[2,128,128]{2,1,0:T(8,128)S(1)}, u32[]{:S(2)}, u32[]{:S(2)}) %collective-permute-start.22) | collective-permute-done | bytes 131104 | tf_op jit(solution)/shard_map/ppermute | solution.py:670
  148.7 0.9 pad_maximum_fusion.2.own_mid
  149.6 4.1 %collective-permute-start.24 = (f32[2,2,128,128]{3,2,1,0:T(8,128)S(1)}, f32[2,2,128,128]{3,2,1,0:T(8,128)}, u32[]{:S(2)}, u32[]{:S(2)}) collective-permute-start(f32[2,2,128,128]{3,2,1,0:T(8,128)S(1)} %pad_maximum_fusion.2.own_mid), channel_id=1, source_target_pairs={{0,30},{1,3},{2,0},{3,5},{4,2},{5,7},{6,4},{7,9},{8,6},{9,11},{10,... | collective-permute-start | bytes 786440 | tf_op jit(solution)/shard_map/ppermute | solution.py:682
  153.7 1.8 collective-permute-start.25
  155.5 0.8 copy-done.20
  156.3 0.8 copy-done.33
  157.1 2.5 %shard_map.258.spread_ref = f32[5,256,128]{2,1,0:T(8,128)S(1)} custom-call(f32[32,32,128]{2,1,0:T(8,128)} %all-to-all-done.all_ref, bf16[128,128]{1,0:T(8,128)(2,1)S(1)} %copy-done.33, bf16[256,128]{1,0:T(8,128)(2,1)S(1)} %copy-done.20), custom_call_target="tpu_custom_call" | custom-call | flops 10000000 | bytes 1277952 | tf_op jit(solution)/shard_map/pallas_call | solution.py:301
  159.8 2.7 %collective-permute-done.23.left_mid = f32[2,2,128,128]{3,2,1,0:T(8,128)} collective-permute-done((f32[2,2,128,128]{3,2,1,0:T(8,128)S(1)}, f32[2,2,128,128]{3,2,1,0:T(8,128)}, u32[]{:S(2)}, u32[]{:S(2)}) %collective-permute-start.23) | collective-permute-done | bytes 262176 | tf_op jit(solution)/shard_map/ppermute | solution.py:679
  162.5 1.4 shard_map.260
  163.9 2.7 %collective-permute-start.28 = (f32[2,256,256]{2,1,0:T(8,128)S(1)}, f32[2,256,256]{2,1,0:T(8,128)S(1)}, u32[]{:S(2)}, u32[]{:S(2)}) collective-permute-start(f32[2,256,256]{2,1,0:T(8,128)S(1)} %get-tuple-element.74), channel_id=1, source_target_pairs={{0,1},{1,0},{2,3},{3,2},{4,5},{5,4},{6,7},{7,6},{8,9},{9,8},{10,11... | collective-permute-start | bytes 1572872 | tf_op jit(solution)/shard_map/ppermute | solution.py:670
  166.7 9.4 %shard_map.259 = (f32[3,2,512,256]{3,2,1,0:T(8,128)}, f32[4,256,256]{2,1,0:T(8,128)}) custom-call(f32[5,256,128]{2,1,0:T(8,128)S(1)} %shard_map.258.spread_ref, f32[2,2,128,128]{3,2,1,0:T(8,128)S(1)} %pad_maximum_fusion.2.own_mid, f32[2,2,128,128]{3,2,1,0:T(8,128)} %collective-permute-done.23.left_mid, f32[2,2,128,128]{3,2,1,0:T(8,128)} %collective-permute-done.24.right_mid, ...), custom_call_target="tpu_custom_call" | custom-call | flops 1000000000 | bytes 11468800 | tf_op jit(solution)/shard_map/pallas_call | solution.py:301
  176.1 1.4 collective-permute-done.28.peer_u
  177.5 2.1 %shard_map.261 = f32[3,2,512,256]{3,2,1,0:T(8,128)} custom-call(f32[3,2,512,256]{3,2,1,0:T(8,128)} %get-tuple-element.69.gradient_ref, f32[2,256,256]{2,1,0:T(8,128)S(1)} %get-tuple-element.73.own_u, f32[2,256,256]{2,1,0:T(8,128)S(1)} %collective-permute-done.28.peer_u, s32[2,512,256]{2,1,0:T(8,128)S(1)} %copy-done), custom_call_target="tpu_custom_call", output_to_operand_aliasing={{}: (0, {})} | custom-call | flops 10000000 | bytes 8388608 | tf_op jit(solution)/shard_map/pallas_call | solution.py:301
  (117 shorter events, 0.4 us)
Async XLA Ops:
  1.5 6.5 %collective-permute-start = (f32[4,32,256]{2,1,0:T(8,128)S(1)}, f32[4,32,256]{2,1,0:T(8,128)S(1)}, u32[]{:S(2)}, u32[]{:S(2)}) collective-permute-start(f32[4,32,256]{2,1,0:T(8,128)S(1)} %pad_maximum_fusion.3), channel_id=1, source_target_pairs={{0,1},{1,0},{2,3},{3,2},{4,5},{5,4},{6,7},{7,6},{8,9},{9,8},{10,11... | collective-permute-start | bytes 393224 | tf_op jit(solution)/shard_map/ppermute | solution.py:670
  7.2 24.8 %collective-permute-start.3 = (f32[2,2,256,256]{3,2,1,0:T(8,128)}, f32[2,2,256,256]{3,2,1,0:T(8,128)S(1)}, u32[]{:S(2)}, u32[]{:S(2)}) collective-permute-start(f32[2,2,256,256]{3,2,1,0:T(8,128)} %constant_dynamic-slice_fusion.3), channel_id=1, source_target_pairs={{0,1},{1,0},{2,3},{3,2},{4,5},{5,4},{6,7},{7,6},{8,9},{9,8},{10,11... | collective-permute-start | bytes 3145736 | tf_op jit(solution)/shard_map/ppermute | solution.py:670
  8.1 6.2 %copy-start.23 = (bf16[512,256]{1,0:T(8,128)(2,1)S(1)}, bf16[512,256]{1,0:T(8,128)(2,1)}, u32[]{:S(2)}) copy-start(bf16[512,256]{1,0:T(8,128)(2,1)} %constant.55.clone.rows_high) | copy-start | bytes 786436
  8.1 6.2 %copy-start.38 = (bf16[256,512]{1,0:T(8,128)(2,1)S(1)}, bf16[256,512]{1,0:T(8,128)(2,1)}, u32[]{:S(2)}) copy-start(bf16[256,512]{1,0:T(8,128)(2,1)} %constant.59.clone.depth_low) | copy-start | bytes 786436
  8.1 6.2 %copy-start.40 = (bf16[256,512]{1,0:T(8,128)(2,1)S(1)}, bf16[256,512]{1,0:T(8,128)(2,1)}, u32[]{:S(2)}) copy-start(bf16[256,512]{1,0:T(8,128)(2,1)} %constant.58.clone.depth_high) | copy-start | bytes 786436
  8.1 6.2 %copy-start.44 = (bf16[16,256]{1,0:T(8,128)(2,1)S(1)}, bf16[16,256]{1,0:T(8,128)(2,1)}, u32[]{:S(2)}) copy-start(bf16[16,256]{1,0:T(8,128)(2,1)} %constant.54.clone.basis_ref) | copy-start | bytes 24580
  11.0 21.1 %collective-permute-start.2 = (f32[3,288,256]{2,1,0:T(8,128)}, f32[3,288,256]{2,1,0:T(8,128)}, u32[]{:S(2)}, u32[]{:S(2)}) collective-permute-start(f32[3,288,256]{2,1,0:T(8,128)} %get-tuple-element.76), channel_id=1, source_target_pairs={{0,30},{1,3},{2,0},{3,5},{4,2},{5,7},{6,4},{7,9},{8,6},{9,11},{10,... | collective-permute-start | bytes 2654216 | tf_op jit(solution)/shard_map/ppermute | solution.py:682
  14.3 17.8 %collective-permute-start.1 = (f32[3,288,256]{2,1,0:T(8,128)}, f32[3,288,256]{2,1,0:T(8,128)}, u32[]{:S(2)}, u32[]{:S(2)}) collective-permute-start(f32[3,288,256]{2,1,0:T(8,128)} %get-tuple-element.77), channel_id=1, source_target_pairs={{0,2},{1,31},{2,4},{3,1},{4,6},{5,3},{6,8},{7,5},{8,10},{9,7},{10,... | collective-permute-start | bytes 2654216 | tf_op jit(solution)/shard_map/ppermute | solution.py:679
  20.4 11.7 %copy-start.37 = (f32[2,280,256]{2,1,0:T(8,128)S(1)}, f32[2,280,256]{2,1,0:T(8,128)}, u32[]{:S(2)}) copy-start(f32[2,280,256]{2,1,0:T(8,128)} %copy-done.36) | copy-start | bytes 1720324
  20.4 15.1 %copy-start = (s32[2,512,256]{2,1,0:T(8,128)S(1)}, s32[2,512,256]{2,1,0:T(8,128)}, u32[]{:S(2)}) copy-start(s32[2,512,256]{2,1,0:T(8,128)} %solid_ref.3) | copy-start | bytes 3145732
  22.1 21.1 %copy-start.24 = (bf16[512,256]{1,0:T(8,128)(2,1)S(1)}, bf16[512,256]{1,0:T(8,128)(2,1)}, u32[]{:S(2)}) copy-start(bf16[512,256]{1,0:T(8,128)(2,1)} %constant.55.clone.rows_high) | copy-start | bytes 786436
  22.1 21.1 %copy-start.39 = (bf16[256,512]{1,0:T(8,128)(2,1)S(1)}, bf16[256,512]{1,0:T(8,128)(2,1)}, u32[]{:S(2)}) copy-start(bf16[256,512]{1,0:T(8,128)(2,1)} %constant.59.clone.depth_low) | copy-start | bytes 786436
  22.1 21.1 %copy-start.41 = (bf16[256,512]{1,0:T(8,128)(2,1)S(1)}, bf16[256,512]{1,0:T(8,128)(2,1)}, u32[]{:S(2)}) copy-start(bf16[256,512]{1,0:T(8,128)(2,1)} %constant.58.clone.depth_high) | copy-start | bytes 786436
  22.1 21.1 %copy-start.43 = (bf16[512,32]{1,0:T(8,128)(2,1)S(1)}, bf16[512,32]{1,0:T(8,128)(2,1)}, u32[]{:S(2)}) copy-start(bf16[512,32]{1,0:T(8,128)(2,1)} %constant.57.clone.spread) | copy-start | bytes 98308
  22.2 43.8 %collective-permute-start.5 = (f32[3,2,256,256]{3,2,1,0:T(8,128)S(1)}, f32[3,2,256,256]{3,2,1,0:T(8,128)S(1)}, u32[]{:S(2)}, u32[]{:S(2)}) collective-permute-start(f32[3,2,256,256]{3,2,1,0:T(8,128)S(1)} %constant_dynamic-slice_fusion.2.own_ref), channel_id=1, source_target_pairs={{0,30},{1,3},{2,0},{3,5},{4,2},{5,7},{6,4},{7,9},{8,6},{9,11},{10,... | collective-permute-start | bytes 4718600 | tf_op jit(solution)/shard_map/ppermute | solution.py:682
  32.0 33.9 %collective-permute-start.6 = (f32[2,2,256,256]{3,2,1,0:T(8,128)S(1)}, f32[2,2,256,256]{3,2,1,0:T(8,128)S(1)}, u32[]{:S(2)}, u32[]{:S(2)}) collective-permute-start(f32[2,2,256,256]{3,2,1,0:T(8,128)S(1)} %collective-permute-done.3.uv_ref.peers), channel_id=1, source_target_pairs={{0,2},{1,31},{2,4},{3,1},{4,6},{5,3},{6,8},{7,5},{8,10},{9,7},{10,... | collective-permute-start | bytes 3145736 | tf_op jit(solution)/shard_map/ppermute | solution.py:679
  32.1 11.1 %collective-permute-start.4 = (f32[2,280,256]{2,1,0:T(8,128)S(1)}, f32[2,280,256]{2,1,0:T(8,128)S(1)}, u32[]{:S(2)}, u32[]{:S(2)}) collective-permute-start(f32[2,280,256]{2,1,0:T(8,128)S(1)} %copy-done.37), channel_id=1, source_target_pairs={{0,1},{1,0},{2,3},{3,2},{4,5},{5,4},{6,7},{7,6},{8,9},{9,8},{10,11... | collective-permute-start | bytes 1720328 | tf_op jit(solution)/shard_map/ppermute | solution.py:670
  35.6 13.2 %collective-permute-start.7 = (s32[2,256,256]{2,1,0:T(8,128)S(1)}, s32[2,256,256]{2,1,0:T(8,128)S(1)}, u32[]{:S(2)}, u32[]{:S(2)}) collective-permute-start(s32[2,256,256]{2,1,0:T(8,128)S(1)} %get-tuple-element.78), channel_id=1, source_target_pairs={{0,1},{1,0},{2,3},{3,2},{4,5},{5,4},{6,7},{7,6},{8,9},{9,8},{10,11... | collective-permute-start | bytes 1572872 | tf_op jit(solution)/shard_map/ppermute | solution.py:670
  43.2 22.7 %copy-start.2 = (f32[3,2,256,256]{3,2,1,0:T(8,128)S(1)}, f32[3,2,256,256]{3,2,1,0:T(8,128)}, u32[]{:S(2)}) copy-start(f32[3,2,256,256]{3,2,1,0:T(8,128)} %copy-done.1) | copy-start | bytes 4718596
  48.9 22.8 %collective-permute-start.10 = (f32[2,256,256]{2,1,0:T(8,128)S(1)}, f32[2,256,256]{2,1,0:T(8,128)S(1)}, u32[]{:S(2)}, u32[]{:S(2)}) collective-permute-start(f32[2,256,256]{2,1,0:T(8,128)S(1)} %slice.45), channel_id=1, source_target_pairs={{0,2},{1,31},{2,4},{3,1},{4,6},{5,3},{6,8},{7,5},{8,10},{9,7},{10,... | collective-permute-start | bytes 1572872 | tf_op jit(solution)/shard_map/ppermute | solution.py:679
  66.0 5.7 %copy-start.35 = (bf16[4,16,64]{2,1,0:T(8,128)(2,1)S(1)}, bf16[4,16,64]{2,1,0:T(8,128)(2,1)}, u32[]{:S(2)}) copy-start(bf16[4,16,64]{2,1,0:T(8,128)(2,1)} %constant.60.clone.basis_ref) | copy-start | bytes 24580
  67.1 11.6 %copy-start.8 = (f32[2,256,256]{2,1,0:T(8,128)}, f32[2,256,256]{2,1,0:T(8,128)S(1)}, u32[]{:S(2)}) copy-start(f32[2,256,256]{2,1,0:T(8,128)S(1)} %get-tuple-element.43.near_u) | copy-start | bytes 1572868
  67.1 11.6 %copy-start.10 = (f32[2,256,256]{2,1,0:T(8,128)}, f32[2,256,256]{2,1,0:T(8,128)S(1)}, u32[]{:S(2)}) copy-start(f32[2,256,256]{2,1,0:T(8,128)S(1)} %get-tuple-element.44.far_u) | copy-start | bytes 1572868
  67.1 11.5 %collective-permute-start.8 = (f32[2,256,256]{2,1,0:T(8,128)S(1)}, f32[2,256,256]{2,1,0:T(8,128)S(1)}, u32[]{:S(2)}, u32[]{:S(2)}) collective-permute-start(f32[2,256,256]{2,1,0:T(8,128)S(1)} %get-tuple-element.44.far_u), channel_id=1, source_target_pairs={{0,2},{1,31},{2,4},{3,1},{4,6},{5,3},{6,8},{7,5},{8,10},{9,7},{10,... | collective-permute-start | bytes 1572872 | tf_op jit(solution)/shard_map/ppermute | solution.py:679
  68.6 6.7 %copy-start.14 = (bf16[256,256]{1,0:T(8,128)(2,1)S(1)}, bf16[256,256]{1,0:T(8,128)(2,1)}, u32[]{:S(2)}) copy-start(bf16[256,256]{1,0:T(8,128)(2,1)} %constant.62.clone.depth_low) | copy-start | bytes 393220
  68.6 6.7 %copy-start.15 = (bf16[256,256]{1,0:T(8,128)(2,1)S(1)}, bf16[256,256]{1,0:T(8,128)(2,1)}, u32[]{:S(2)}) copy-start(bf16[256,256]{1,0:T(8,128)(2,1)} %constant.61.clone.depth_high) | copy-start | bytes 393220
  68.6 6.7 %copy-start.22 = (bf16[512,256]{1,0:T(8,128)(2,1)S(1)}, bf16[512,256]{1,0:T(8,128)(2,1)}, u32[]{:S(2)}) copy-start(bf16[512,256]{1,0:T(8,128)(2,1)} %constant.56.clone.rows_low) | copy-start | bytes 786436
  68.6 10.1 %collective-permute-start.9 = (f32[2,256,256]{2,1,0:T(8,128)S(1)}, f32[2,256,256]{2,1,0:T(8,128)S(1)}, u32[]{:S(2)}, u32[]{:S(2)}) collective-permute-start(f32[2,256,256]{2,1,0:T(8,128)S(1)} %get-tuple-element.43.near_u), channel_id=1, source_target_pairs={{0,30},{1,3},{2,0},{3,5},{4,2},{5,7},{6,4},{7,9},{8,6},{9,11},{10,... | collective-permute-start | bytes 1572872 | tf_op jit(solution)/shard_map/ppermute | solution.py:682
  74.7 4.0 %collective-permute-start.11 = (f32[4,8,256]{2,1,0:T(8,128)S(1)}, f32[4,8,256]{2,1,0:T(8,128)S(1)}, u32[]{:S(2)}, u32[]{:S(2)}) collective-permute-start(f32[4,8,256]{2,1,0:T(8,128)S(1)} %get-tuple-element.51), channel_id=1, source_target_pairs={{0,1},{1,0},{2,3},{3,2},{4,5},{5,4},{6,7},{7,6},{8,9},{9,8},{10,11... | collective-permute-start | bytes 98312 | tf_op jit(solution)/shard_map/ppermute | solution.py:670
  79.8 24.4 %copy-start.19 = (bf16[256,128]{1,0:T(8,128)(2,1)S(1)}, bf16[256,128]{1,0:T(8,128)(2,1)}, u32[]{:S(2)}) copy-start(bf16[256,128]{1,0:T(8,128)(2,1)} %constant.64.clone.depth_pick.mid_rows) | copy-start | bytes 196612
  79.8 24.4 %copy-start.29 = (bf16[144,288]{1,0:T(8,128)(2,1)S(1)}, bf16[144,288]{1,0:T(8,128)(2,1)}, u32[]{:S(2)}) copy-start(bf16[144,288]{1,0:T(8,128)(2,1)} %constant.65.clone.rows_pick) | copy-start | bytes 248836
  79.8 11.8 %collective-permute-start.14 = (f32[4,32,256]{2,1,0:T(8,128)S(1)}, f32[4,32,256]{2,1,0:T(8,128)S(1)}, u32[]{:S(2)}, u32[]{:S(2)}) collective-permute-start(f32[4,32,256]{2,1,0:T(8,128)S(1)} %pad_maximum_fusion.4), channel_id=1, source_target_pairs={{0,1},{1,0},{2,3},{3,2},{4,5},{5,4},{6,7},{7,6},{8,9},{9,8},{10,11... | collective-permute-start | bytes 393224 | tf_op jit(solution)/shard_map/ppermute | solution.py:670
  84.7 19.5 %collective-permute-start.13 = (f32[2,256,256]{2,1,0:T(8,128)S(1)}, f32[2,256,256]{2,1,0:T(8,128)S(1)}, u32[]{:S(2)}, u32[]{:S(2)}) collective-permute-start(f32[2,256,256]{2,1,0:T(8,128)S(1)} %get-tuple-element.52.near_r), channel_id=1, source_target_pairs={{0,30},{1,3},{2,0},{3,5},{4,2},{5,7},{6,4},{7,9},{8,6},{9,11},{10,... | collective-permute-start | bytes 1572872 | tf_op jit(solution)/shard_map/ppermute | solution.py:682
  84.7 19.5 %collective-permute-start.12 = (f32[2,256,256]{2,1,0:T(8,128)S(1)}, f32[2,256,256]{2,1,0:T(8,128)S(1)}, u32[]{:S(2)}, u32[]{:S(2)}) collective-permute-start(f32[2,256,256]{2,1,0:T(8,128)S(1)} %get-tuple-element.53.far_r), channel_id=1, source_target_pairs={{0,2},{1,31},{2,4},{3,1},{4,6},{5,3},{6,8},{7,5},{8,10},{9,7},{10,... | collective-permute-start | bytes 1572872 | tf_op jit(solution)/shard_map/ppermute | solution.py:679
  91.7 6.7 %collective-permute-start.16 = (f32[2,32,256]{2,1,0:T(8,128)S(1)}, f32[2,32,256]{2,1,0:T(8,128)S(1)}, u32[]{:S(2)}, u32[]{:S(2)}) collective-permute-start(f32[2,32,256]{2,1,0:T(8,128)S(1)} %get-tuple-element.84), channel_id=1, source_target_pairs={{0,30},{1,3},{2,0},{3,5},{4,2},{5,7},{6,4},{7,9},{8,6},{9,11},{10,... | collective-permute-start | bytes 196616 | tf_op jit(solution)/shard_map/ppermute | solution.py:682
  96.4 7.6 %collective-permute-start.15 = (f32[2,32,256]{2,1,0:T(8,128)S(1)}, f32[2,32,256]{2,1,0:T(8,128)S(1)}, u32[]{:S(2)}, u32[]{:S(2)}) collective-permute-start(f32[2,32,256]{2,1,0:T(8,128)S(1)} %get-tuple-element.85), channel_id=1, source_target_pairs={{0,2},{1,31},{2,4},{3,1},{4,6},{5,3},{6,8},{7,5},{8,10},{9,7},{10,... | collective-permute-start | bytes 196616 | tf_op jit(solution)/shard_map/ppermute | solution.py:679
  104.1 24.4 %collective-permute-start.20 = (f32[2,2,256,256]{3,2,1,0:T(8,128)S(1)}, f32[2,2,256,256]{3,2,1,0:T(8,128)S(1)}, u32[]{:S(2)}, u32[]{:S(2)}) collective-permute-start(f32[2,2,256,256]{3,2,1,0:T(8,128)S(1)} %pad_maximum_fusion.1), channel_id=1, source_target_pairs={{0,1},{1,0},{2,3},{3,2},{4,5},{5,4},{6,7},{7,6},{8,9},{9,8},{10,11... | collective-permute-start | bytes 3145736 | tf_op jit(solution)/shard_map/ppermute | solution.py:670
  109.8 11.4 %copy-start.31 = (bf16[128,256]{1,0:T(8,128)(2,1)S(1)}, bf16[128,256]{1,0:T(8,128)(2,1)}, u32[]{:S(2)}) copy-start(bf16[128,256]{1,0:T(8,128)(2,1)} %constant.66.clone.depth_pick) | copy-start | bytes 196612
  109.8 11.4 %copy-start.34 = (bf16[64,144]{1,0:T(8,128)(2,1)S(1)}, bf16[64,144]{1,0:T(8,128)(2,1)}, u32[]{:S(2)}) copy-start(bf16[64,144]{1,0:T(8,128)(2,1)} %constant.67.clone.rows_pick) | copy-start | bytes 55300
  109.8 10.5 %collective-permute-start.17 = (f32[432,256]{1,0:T(8,128)S(1)}, f32[432,256]{1,0:T(8,128)S(1)}, u32[]{:S(2)}, u32[]{:S(2)}) collective-permute-start(f32[432,256]{1,0:T(8,128)S(1)} %get-tuple-element.58), channel_id=1, source_target_pairs={{0,2},{1,31},{2,4},{3,1},{4,6},{5,3},{6,8},{7,5},{8,10},{9,7},{10,... | collective-permute-start | bytes 1327112 | tf_op jit(solution)/shard_map/ppermute | solution.py:679
  114.1 6.2 %collective-permute-start.18 = (f32[432,256]{1,0:T(8,128)S(1)}, f32[432,256]{1,0:T(8,128)S(1)}, u32[]{:S(2)}, u32[]{:S(2)}) collective-permute-start(f32[432,256]{1,0:T(8,128)S(1)} %get-tuple-element.59), channel_id=1, source_target_pairs={{0,30},{1,3},{2,0},{3,5},{4,2},{5,7},{6,4},{7,9},{8,6},{9,11},{10,... | collective-permute-start | bytes 1327112 | tf_op jit(solution)/shard_map/ppermute | solution.py:682
  122.0 6.6 %collective-permute-start.19 = (f32[1,144,128]{2,1,0:T(8,128)S(1)}, f32[1,144,128]{2,1,0:T(8,128)S(1)}, u32[]{:S(2)}, u32[]{:S(2)}) collective-permute-start(f32[1,144,128]{2,1,0:T(8,128)S(1)} %get-tuple-element.83), channel_id=1, source_target_pairs={{0,2},{1,31},{2,4},{3,1},{4,6},{5,3},{6,8},{7,5},{8,10},{9,7},{10,... | collective-permute-start | bytes 221192 | tf_op jit(solution)/shard_map/ppermute | solution.py:679
  127.3 3.2 %collective-permute-start.21 = (f32[1,144,128]{2,1,0:T(8,128)S(1)}, f32[1,144,128]{2,1,0:T(8,128)S(1)}, u32[]{:S(2)}, u32[]{:S(2)}) collective-permute-start(f32[1,144,128]{2,1,0:T(8,128)S(1)} %get-tuple-element.82), channel_id=1, source_target_pairs={{0,30},{1,3},{2,0},{3,5},{4,2},{5,7},{6,4},{7,9},{8,6},{9,11},{10,... | collective-permute-start | bytes 221192 | tf_op jit(solution)/shard_map/ppermute | solution.py:682
  130.7 18.0 %copy-start.17 = (f32[2,128,128]{2,1,0:T(8,128)}, f32[2,128,128]{2,1,0:T(8,128)S(1)}, u32[]{:S(2)}) copy-start(f32[2,128,128]{2,1,0:T(8,128)S(1)} %shard_map.257) | copy-start | bytes 393220
  130.7 31.8 %copy-start.9 = (f32[2,256,256]{2,1,0:T(8,128)S(1)}, f32[2,256,256]{2,1,0:T(8,128)}, u32[]{:S(2)}) copy-start(f32[2,256,256]{2,1,0:T(8,128)} %copy-done.8) | copy-start | bytes 1572868
  130.7 31.8 %copy-start.11 = (f32[2,256,256]{2,1,0:T(8,128)S(1)}, f32[2,256,256]{2,1,0:T(8,128)}, u32[]{:S(2)}) copy-start(f32[2,256,256]{2,1,0:T(8,128)} %copy-done.10) | copy-start | bytes 1572868
  131.6 23.9 %all-to-all-start = ((f32[32,32,128]{2,1,0:T(8,128)}), f32[32,32,128]{2,1,0:T(8,128)}, u32[]{:S(2)}, u32[]{:S(2)}) async-start(f32[32,32,128]{2,1,0:T(8,128)} %broadcast_in_dim.3), calls=%async_computation | async-start | bytes 1048576 | tf_op jit(solution)/shard_map/all_to_all | solution.py:851
  138.3 24.2 %collective-permute-start.27 = (f32[2,256,256]{2,1,0:T(8,128)S(1)}, f32[2,256,256]{2,1,0:T(8,128)}, u32[]{:S(2)}, u32[]{:S(2)}) collective-permute-start(f32[2,256,256]{2,1,0:T(8,128)S(1)} %get-tuple-element.71.near_base.near_ref), channel_id=1, source_target_pairs={{0,30},{1,3},{2,0},{3,5},{4,2},{5,7},{6,4},{7,9},{8,6},{9,11},{10,... | collective-permute-start | bytes 1572872 | tf_op jit(solution)/shard_map/ppermute | solution.py:682
  142.5 19.9 %collective-permute-start.26 = (f32[2,256,256]{2,1,0:T(8,128)S(1)}, f32[2,256,256]{2,1,0:T(8,128)}, u32[]{:S(2)}, u32[]{:S(2)}) collective-permute-start(f32[2,256,256]{2,1,0:T(8,128)S(1)} %get-tuple-element.70.far_base.far_ref), channel_id=1, source_target_pairs={{0,2},{1,31},{2,4},{3,1},{4,6},{5,3},{6,8},{7,5},{8,10},{9,7},{10,... | collective-permute-start | bytes 1572872 | tf_op jit(solution)/shard_map/ppermute | solution.py:679
  142.5 6.1 %collective-permute-start.22 = (f32[2,128,128]{2,1,0:T(8,128)S(1)}, f32[2,128,128]{2,1,0:T(8,128)S(1)}, u32[]{:S(2)}, u32[]{:S(2)}) collective-permute-start(f32[2,128,128]{2,1,0:T(8,128)S(1)} %shard_map.257), channel_id=1, source_target_pairs={{0,1},{1,0},{2,3},{3,2},{4,5},{5,4},{6,7},{7,6},{8,9},{9,8},{10,11... | collective-permute-start | bytes 393224 | tf_op jit(solution)/shard_map/ppermute | solution.py:670
  149.6 10.2 %collective-permute-start.24 = (f32[2,2,128,128]{3,2,1,0:T(8,128)S(1)}, f32[2,2,128,128]{3,2,1,0:T(8,128)}, u32[]{:S(2)}, u32[]{:S(2)}) collective-permute-start(f32[2,2,128,128]{3,2,1,0:T(8,128)S(1)} %pad_maximum_fusion.2.own_mid), channel_id=1, source_target_pairs={{0,30},{1,3},{2,0},{3,5},{4,2},{5,7},{6,4},{7,9},{8,6},{9,11},{10,... | collective-permute-start | bytes 786440 | tf_op jit(solution)/shard_map/ppermute | solution.py:682
  153.7 8.8 %collective-permute-start.23 = (f32[2,2,128,128]{3,2,1,0:T(8,128)S(1)}, f32[2,2,128,128]{3,2,1,0:T(8,128)}, u32[]{:S(2)}, u32[]{:S(2)}) collective-permute-start(f32[2,2,128,128]{3,2,1,0:T(8,128)S(1)} %pad_maximum_fusion.2.own_mid), channel_id=1, source_target_pairs={{0,2},{1,31},{2,4},{3,1},{4,6},{5,3},{6,8},{7,5},{8,10},{9,7},{10,... | collective-permute-start | bytes 786440 | tf_op jit(solution)/shard_map/ppermute | solution.py:679
  153.7 12.9 %collective-permute-start.25 = (f32[2,256,256]{2,1,0:T(8,128)S(1)}, f32[2,256,256]{2,1,0:T(8,128)}, u32[]{:S(2)}, u32[]{:S(2)}) collective-permute-start(f32[2,256,256]{2,1,0:T(8,128)S(1)} %get-tuple-element.70.far_base.far_ref), channel_id=1, source_target_pairs={{0,1},{1,0},{2,3},{3,2},{4,5},{5,4},{6,7},{7,6},{8,9},{9,8},{10,11... | collective-permute-start | bytes 1572872 | tf_op jit(solution)/shard_map/ppermute | solution.py:670
  159.6 7.0 %copy-start.5 = (f32[2,256,256]{2,1,0:T(8,128)S(1)}, f32[2,256,256]{2,1,0:T(8,128)}, u32[]{:S(2)}) copy-start(f32[2,256,256]{2,1,0:T(8,128)} %copy-done.4) | copy-start | bytes 1572868
  159.6 7.0 %copy-start.7 = (f32[2,256,256]{2,1,0:T(8,128)S(1)}, f32[2,256,256]{2,1,0:T(8,128)}, u32[]{:S(2)}) copy-start(f32[2,256,256]{2,1,0:T(8,128)} %copy-done.6) | copy-start | bytes 1572868
  159.7 7.0 %copy-start.13 = (f32[2,2,256,256]{3,2,1,0:T(8,128)S(1)}, f32[2,2,256,256]{3,2,1,0:T(8,128)}, u32[]{:S(2)}) copy-start(f32[2,2,256,256]{3,2,1,0:T(8,128)} %copy-done.12) | copy-start | bytes 3145732
  159.7 7.0 %copy-start.16 = (bf16[256,256]{1,0:T(8,128)(2,1)S(1)}, bf16[256,256]{1,0:T(8,128)(2,1)}, u32[]{:S(2)}) copy-start(bf16[256,256]{1,0:T(8,128)(2,1)} %constant.61.clone.depth_high) | copy-start | bytes 393220
  159.7 7.0 %copy-start.18 = (bf16[512,256]{1,0:T(8,128)(2,1)S(1)}, bf16[512,256]{1,0:T(8,128)(2,1)}, u32[]{:S(2)}) copy-start(bf16[512,256]{1,0:T(8,128)(2,1)} %constant.74.clone.fine_rows) | copy-start | bytes 786436
  159.7 7.0 %copy-start.25 = (bf16[256,256]{1,0:T(8,128)(2,1)S(1)}, bf16[256,256]{1,0:T(8,128)(2,1)}, u32[]{:S(2)}) copy-start(bf16[256,256]{1,0:T(8,128)(2,1)} %constant.72.clone.diff_low) | copy-start | bytes 393220
  159.7 7.0 %copy-start.26 = (bf16[256,256]{1,0:T(8,128)(2,1)S(1)}, bf16[256,256]{1,0:T(8,128)(2,1)}, u32[]{:S(2)}) copy-start(bf16[256,256]{1,0:T(8,128)(2,1)} %constant.71.clone.diff_high) | copy-start | bytes 393220
  159.7 7.0 %copy-start.27 = (bf16[256,256]{1,0:T(8,128)(2,1)S(1)}, bf16[256,256]{1,0:T(8,128)(2,1)}, u32[]{:S(2)}) copy-start(bf16[256,256]{1,0:T(8,128)(2,1)} %constant.70.clone.sum_low) | copy-start | bytes 393220
  159.7 7.0 %copy-start.28 = (bf16[256,256]{1,0:T(8,128)(2,1)S(1)}, bf16[256,256]{1,0:T(8,128)(2,1)}, u32[]{:S(2)}) copy-start(bf16[256,256]{1,0:T(8,128)(2,1)} %constant.69.clone.sum_high) | copy-start | bytes 393220
  159.7 7.0 %copy-start.30 = (bf16[128,256]{1,0:T(8,128)(2,1)S(1)}, bf16[128,256]{1,0:T(8,128)(2,1)}, u32[]{:S(2)}) copy-start(bf16[128,256]{1,0:T(8,128)(2,1)} %constant.73.clone.fine_depth) | copy-start | bytes 196612
  163.9 13.5 %collective-permute-start.28 = (f32[2,256,256]{2,1,0:T(8,128)S(1)}, f32[2,256,256]{2,1,0:T(8,128)S(1)}, u32[]{:S(2)}, u32[]{:S(2)}) collective-permute-start(f32[2,256,256]{2,1,0:T(8,128)S(1)} %get-tuple-element.74), channel_id=1, source_target_pairs={{0,1},{1,0},{2,3},{3,2},{4,5},{5,4},{6,7},{7,6},{8,9},{9,8},{10,11... | collective-permute-start | bytes 1572872 | tf_op jit(solution)/shard_map/ppermute | solution.py:670
  (12 other events, 27.1 us)

commit v4 on v3

--- a/solution.py
+++ b/solution.py
@@ -724,7 +724,8 @@
     peer_w = swap(tied(sent_w, pressure_left, pressure_right))
     own_half = half_of(tied(velocity, sent_w), side, 2)
     one = behind(own_half)
-    other_uv = ahead(peer_uv)
+    other_uv = ahead(tied(peer_uv, sent_w))
+    other_w = ahead(peer_w[:, :half])
     solid_peer = swap(half_of(obstacle, 1 - side, 1))
     solid_own = half_of(obstacle, side, 1)
     (raw_peer,) = kernel_call(
@@ -737,7 +738,6 @@
         grid=(2,),
         out_specs=[by_plane((3, 2) + plane, 1)],
     )
-    other_w = ahead(tied(peer_w, raw_peer, solid_peer)[:, :half])
     strip = 64
 
     def strips(count, first=0):
@@ -849,7 +849,7 @@
     both_mid = jnp.stack([mid_base, peer_mid])
     left_mid, right_mid = (ahead(both_mid), behind(both_mid))
     low_all = lax.all_to_all(
-        jnp.broadcast_to(tied(low_source, mid_base), (2 * tunnel_size,) + low_source.shape), both, 0, 0, tiled=True
+        jnp.broadcast_to(tied(low_source, left_two, right_two), (2 * tunnel_size,) + low_source.shape), both, 0, 0, tiled=True
     )
     left_b, right_b = (ahead(tied(far_base, mid_base)), behind(tied(near_base, mid_base)))
     peer_base = swap(tied(far_base, peer_mid))

time: 182 us -> 179 us (0.984)
  starting transfers between devices: 84.5 us -> 77.3 us
  waiting for transfers between devices: 42.4 us -> 44.9 us
    ppermute x10, starting transfers between devices: 35.1 us -> 21.2 us  [ahead(): return lax.ppermute(value, both, ahead_way)]
    ppermute x9, starting transfers between devices: 24.2 us -> 35.6 us  [behind(): return lax.ppermute(value, both, behind_way)]
    all_to_all x1, starting transfers between devices: 6.67 us -> 3.47 us  [paired(): lax.all_to_all(jnp.broadcast_to(tied(low_source, left_two, right_two), (2...]
  transfers between devices with their start and end apart: 30 -> 30, of which waited for: 13 -> 14; matrix products, arithmetic and copies ran while one was open for 4% -> 4% of each run, Pallas kernels for 18% -> 16%
where the time goes in v4:
time: 179 us; the launch traced here: 176 us
  starting transfers between devices  77.3 us (43%)
  waiting for transfers between devices  44.9 us (25%)
  Pallas kernels  36.6 us (20%)
  local copies, waits for them, and re-layouts  11.4 us (6%)
  other arithmetic  3.86 us (2%)
    pallas_call x14, Pallas kernels, kernel_call(): pl.pallas_call(body, out_shape=[jax.ShapeDtypeStruct(s, f32) for s in out...  36.6 us
    ppermute x9, starting transfers between devices, behind(): return lax.ppermute(value, both, behind_way)  35.6 us
    ppermute x10, waiting for transfers between devices, swap(): return lax.ppermute(value, 'group', [(0, 1), (1, 0)])  24.2 us
    ppermute x10, starting transfers between devices, ahead(): return lax.ppermute(value, both, ahead_way)  21.2 us
    ppermute x10, starting transfers between devices, swap(): return lax.ppermute(value, 'group', [(0, 1), (1, 0)])  17.1 us
    ppermute x10, waiting for transfers between devices, ahead(): return lax.ppermute(value, both, ahead_way)  16.8 us
    unnamed x90, local copies, waits for them, and re-layouts  5.22 us
    ppermute x9, waiting for transfers between devices, behind(): return lax.ppermute(value, both, behind_way)  3.9 us
  transfers between devices with their start and end apart: 30, of which 14 were waited for; matrix products, arithmetic and copies ran while one was open for 4% of the time, Pallas kernels for 16%

profile of v4, /device:TPU:0, one launch (start us, length us, event | category | flops | bytes accessed | tf_op | source)
XLA Modules:
  0.0 175.5 jit_solution(5430970347500608799)
XLA Ops:
  0.6 0.9 fusion
  1.5 3.0 %collective-permute-start = (f32[4,32,256]{2,1,0:T(8,128)S(1)}, f32[4,32,256]{2,1,0:T(8,128)S(1)}, u32[]{:S(2)}, u32[]{:S(2)}) collective-permute-start(f32[4,32,256]{2,1,0:T(8,128)S(1)} %pad_maximum_fusion.3), channel_id=1, source_target_pairs={{0,1},{1,0},{2,3},{3,2},{4,5},{5,4},{6,7},{7,6},{8,9},{9,8},{10,11... | collective-permute-start | bytes 393224 | tf_op jit(solution)/shard_map/ppermute | solution.py:670
  4.6 1.6 slice-done
  6.2 1.1 constant_dynamic-slice_fusion.3
  7.2 0.8 collective-permute-done
  8.1 1.4 pad_maximum_fusion.pressure_tall
  9.6 1.4 slice_select_fusion
  11.0 3.3 %collective-permute-start.2 = (f32[3,288,256]{2,1,0:T(8,128)}, f32[3,288,256]{2,1,0:T(8,128)}, u32[]{:S(2)}, u32[]{:S(2)}) collective-permute-start(f32[3,288,256]{2,1,0:T(8,128)} %get-tuple-element.76), channel_id=1, source_target_pairs={{0,30},{1,3},{2,0},{3,5},{4,2},{5,7},{6,4},{7,9},{8,6},{9,11},{10,... | collective-permute-start | bytes 2654216 | tf_op jit(solution)/shard_map/ppermute | solution.py:682
  14.3 4.1 %shard_map.248 = (f32[3,2,256,256]{3,2,1,0:T(8,128)S(1)}, f32[2,280,256]{2,1,0:T(8,128)S(1)}) custom-call(f32[3,2,512,256]{3,2,1,0:T(8,128)S(1)} %copy-done.3, bf16[16,256]{1,0:T(8,128)(2,1)S(1)} %copy-done.44, bf16[512,256]{1,0:T(8,128)(2,1)S(1)} %copy-done.19, bf16[512,256]{1,0:T(8,128)(2,1)S(1)} %copy-done.18, bf16[512,32]{1,0:T(8,128)(2,1)S(1)} %copy-done.42, ...), custom_call_target="tpu_custom_call" | custom-call | flops 3000000000 | bytes 6381568 | tf_op jit(solution)/shard_map/pallas_call | solution.py:301
  18.4 1.1 copy-done.1
  19.6 0.8 copy-done.36
  20.4 1.7 constant_dynamic-slice_fusion.2.own_ref
  22.2 4.5 %collective-permute-start.5 = (f32[3,2,256,256]{3,2,1,0:T(8,128)S(1)}, f32[3,2,256,256]{3,2,1,0:T(8,128)S(1)}, u32[]{:S(2)}, u32[]{:S(2)}) collective-permute-start(f32[3,2,256,256]{3,2,1,0:T(8,128)S(1)} %constant_dynamic-slice_fusion.2.own_ref), channel_id=1, source_target_pairs={{0,30},{1,3},{2,0},{3,5},{4,2},{5,7},{6,4},{7,9},{8,6},{9,11},{10,... | collective-permute-start | bytes 4718600 | tf_op jit(solution)/shard_map/ppermute | solution.py:682
  26.6 5.4 %collective-permute-done.3.uv_ref.peers = f32[2,2,256,256]{3,2,1,0:T(8,128)S(1)} collective-permute-done((f32[2,2,256,256]{3,2,1,0:T(8,128)}, f32[2,2,256,256]{3,2,1,0:T(8,128)S(1)}, u32[]{:S(2)}, u32[]{:S(2)}) %collective-permute-start.3) | collective-permute-done | bytes 1048608 | tf_op jit(solution)/shard_map/ppermute | solution.py:670
  32.1 3.4 %collective-permute-start.4 = (f32[2,280,256]{2,1,0:T(8,128)S(1)}, f32[2,280,256]{2,1,0:T(8,128)S(1)}, u32[]{:S(2)}, u32[]{:S(2)}) collective-permute-start(f32[2,280,256]{2,1,0:T(8,128)S(1)} %copy-done.37), channel_id=1, source_target_pairs={{0,1},{1,0},{2,3},{3,2},{4,5},{5,4},{6,7},{7,6},{8,9},{9,8},{10,11... | collective-permute-start | bytes 1720328 | tf_op jit(solution)/shard_map/ppermute | solution.py:670
  35.5 0.1 constant_dynamic-slice_fusion
  35.6 0.1 collective-permute-start.7
  35.7 7.5 %collective-permute-done.4.w_ref.peer_w = f32[2,280,256]{2,1,0:T(8,128)S(1)} collective-permute-done((f32[2,280,256]{2,1,0:T(8,128)S(1)}, f32[2,280,256]{2,1,0:T(8,128)S(1)}, u32[]{:S(2)}, u32[]{:S(2)}) %collective-permute-start.4) | collective-permute-done | bytes 573472 | tf_op jit(solution)/shard_map/ppermute | solution.py:670
  43.2 17.1 %collective-permute-start.10 = (f32[2,256,256]{2,1,0:T(8,128)S(1)}, f32[2,256,256]{2,1,0:T(8,128)S(1)}, u32[]{:S(2)}, u32[]{:S(2)}) collective-permute-start(f32[2,256,256]{2,1,0:T(8,128)S(1)} %slice.54), channel_id=1, source_target_pairs={{0,2},{1,31},{2,4},{3,1},{4,6},{5,3},{6,8},{7,5},{8,10},{9,7},{10,... | collective-permute-start | bytes 1572872 | tf_op jit(solution)/shard_map/ppermute | solution.py:679
  60.4 3.5 %shard_map.249.raw_peer = f32[3,2,256,256]{3,2,1,0:T(8,128)S(1)} custom-call(f32[2,2,256,256]{3,2,1,0:T(8,128)S(1)} %collective-permute-done.3.uv_ref.peers, f32[2,280,256]{2,1,0:T(8,128)S(1)} %collective-permute-done.4.w_ref.peer_w, bf16[512,256]{1,0:T(8,128)(2,1)S(1)} %copy-done.20, bf16[512,256]{1,0:T(8,128)(2,1)S(1)} %copy-done.18, ...), custom_call_target="tpu_custom_call" | custom-call | flops 3000000000 | bytes 4276224 | tf_op jit(solution)/shard_map/pallas_call | solution.py:301
  63.9 1.1 shard_map.250
  65.1 3.1 %collective-permute-start.8 = (f32[2,256,256]{2,1,0:T(8,128)S(1)}, f32[2,256,256]{2,1,0:T(8,128)S(1)}, u32[]{:S(2)}, u32[]{:S(2)}) collective-permute-start(f32[2,256,256]{2,1,0:T(8,128)S(1)} %get-tuple-element.45.far_u), channel_id=1, source_target_pairs={{0,2},{1,31},{2,4},{3,1},{4,6},{5,3},{6,8},{7,5},{8,10},{9,7},{10,... | collective-permute-start | bytes 1572872 | tf_op jit(solution)/shard_map/ppermute | solution.py:679
  68.1 1.4 collective-permute-start.9
  69.6 3.0 %shard_map.251 = (f32[2,256,256]{2,1,0:T(8,128)S(1)}, f32[2,256,256]{2,1,0:T(8,128)S(1)}, f32[2,256,256]{2,1,0:T(8,128)S(1)}, f32[2,256,256]{2,1,0:T(8,128)S(1)}, f32[4,8,256]{2,1,0:T(8,128)S(1)}) custom-call(f32[3,2,256,256]{3,2,1,0:T(8,128)S(1)} %copy-done.2, f32[3,2,256,256]{3,2,1,0:T(8,128)S(1)} %shard_map.249.raw_peer, ...), custom_call_target="tpu_custom_call" | custom-call | flops 100000000 | bytes 12673024 | tf_op jit(solution)/shard_map/pallas_call | solution.py:301
  72.6 0.6 collective-permute-start.11
  73.2 1.0 shard_map.252.cross_ref
  74.2 2.4 %collective-permute-done.11.sum_ref = f32[4,8,256]{2,1,0:T(8,128)S(1)} collective-permute-done((f32[4,8,256]{2,1,0:T(8,128)S(1)}, f32[4,8,256]{2,1,0:T(8,128)S(1)}, u32[]{:S(2)}, u32[]{:S(2)}) %collective-permute-start.11) | collective-permute-done | bytes 32800 | tf_op jit(solution)/shard_map/ppermute | solution.py:670
  76.6 1.1 shard_map.253
  77.7 4.4 %collective-permute-start.13 = (f32[2,256,256]{2,1,0:T(8,128)S(1)}, f32[2,256,256]{2,1,0:T(8,128)S(1)}, u32[]{:S(2)}, u32[]{:S(2)}) collective-permute-start(f32[2,256,256]{2,1,0:T(8,128)S(1)} %get-tuple-element.52.near_r), channel_id=1, source_target_pairs={{0,30},{1,3},{2,0},{3,5},{4,2},{5,7},{6,4},{7,9},{8,6},{9,11},{10,... | collective-permute-start | bytes 1572872 | tf_op jit(solution)/shard_map/ppermute | solution.py:682
  82.1 1.0 collective-permute-start.12
  83.1 4.0 %collective-permute-start.14 = (f32[4,32,256]{2,1,0:T(8,128)S(1)}, f32[4,32,256]{2,1,0:T(8,128)S(1)}, u32[]{:S(2)}, u32[]{:S(2)}) collective-permute-start(f32[4,32,256]{2,1,0:T(8,128)S(1)} %pad_maximum_fusion.4), channel_id=1, source_target_pairs={{0,1},{1,0},{2,3},{3,2},{4,5},{5,4},{6,7},{7,6},{8,9},{9,8},{10,11... | collective-permute-start | bytes 393224 | tf_op jit(solution)/shard_map/ppermute | solution.py:670
  87.1 3.1 %collective-permute-done.14.edge_ref = f32[4,32,256]{2,1,0:T(8,128)S(1)} collective-permute-done((f32[4,32,256]{2,1,0:T(8,128)S(1)}, f32[4,32,256]{2,1,0:T(8,128)S(1)}, u32[]{:S(2)}, u32[]{:S(2)}) %collective-permute-start.14) | collective-permute-done | bytes 131104 | tf_op jit(solution)/shard_map/ppermute | solution.py:670
  90.3 5.6 %collective-permute-start.16 = (f32[2,32,256]{2,1,0:T(8,128)S(1)}, f32[2,32,256]{2,1,0:T(8,128)S(1)}, u32[]{:S(2)}, u32[]{:S(2)}) collective-permute-start(f32[2,32,256]{2,1,0:T(8,128)S(1)} %get-tuple-element.84), channel_id=1, source_target_pairs={{0,30},{1,3},{2,0},{3,5},{4,2},{5,7},{6,4},{7,9},{8,6},{9,11},{10,... | collective-permute-start | bytes 196616 | tf_op jit(solution)/shard_map/ppermute | solution.py:682
  95.9 1.9 %collective-permute-done.16.right_edge = f32[2,32,256]{2,1,0:T(8,128)S(1)} collective-permute-done((f32[2,32,256]{2,1,0:T(8,128)S(1)}, f32[2,32,256]{2,1,0:T(8,128)S(1)}, u32[]{:S(2)}, u32[]{:S(2)}) %collective-permute-start.16) | collective-permute-done | bytes 65568 | tf_op jit(solution)/shard_map/ppermute | solution.py:682
  97.8 4.5 %collective-permute-done.15.left_edge = f32[2,32,256]{2,1,0:T(8,128)S(1)} collective-permute-done((f32[2,32,256]{2,1,0:T(8,128)S(1)}, f32[2,32,256]{2,1,0:T(8,128)S(1)}, u32[]{:S(2)}, u32[]{:S(2)}) %collective-permute-start.15) | collective-permute-done | bytes 65568 | tf_op jit(solution)/shard_map/ppermute | solution.py:679
  102.3 5.4 %shard_map.254 = (f32[4,288,256]{2,1,0:T(8,128)S(1)}, f32[2,144,128]{2,1,0:T(8,128)S(1)}, f32[432,256]{1,0:T(8,128)S(1)}, f32[432,256]{1,0:T(8,128)S(1)}) custom-call(f32[4,288,256]{2,1,0:T(8,128)S(1)} %pad_maximum_fusion.pressure_tall, f32[3,288,256]{2,1,0:T(8,128)} %collective-permute-done.1.pressure_left, ...), custom_call_target="tpu_custom_call" | custom-call | flops 100000000 | bytes 7668736 | tf_op jit(solution)/shard_map/pallas_call | solution.py:301
  107.7 4.4 %collective-permute-start.18 = (f32[432,256]{1,0:T(8,128)S(1)}, f32[432,256]{1,0:T(8,128)S(1)}, u32[]{:S(2)}, u32[]{:S(2)}) collective-permute-start(f32[432,256]{1,0:T(8,128)S(1)} %get-tuple-element.59), channel_id=1, source_target_pairs={{0,30},{1,3},{2,0},{3,5},{4,2},{5,7},{6,4},{7,9},{8,6},{9,11},{10,... | collective-permute-start | bytes 1327112 | tf_op jit(solution)/shard_map/ppermute | solution.py:682
  112.2 1.0 pad_maximum_fusion.1
  113.2 5.0 %collective-permute-done.17.left_ref = f32[432,256]{1,0:T(8,128)S(1)} collective-permute-done((f32[432,256]{1,0:T(8,128)S(1)}, f32[432,256]{1,0:T(8,128)S(1)}, u32[]{:S(2)}, u32[]{:S(2)}) %collective-permute-start.17) | collective-permute-done | bytes 442400 | tf_op jit(solution)/shard_map/ppermute | solution.py:679
  118.3 0.8 shard_map.255
  119.1 0.7 shard_map.256
  119.8 4.4 %collective-permute-start.20 = (f32[1,144,128]{2,1,0:T(8,128)S(1)}, f32[1,144,128]{2,1,0:T(8,128)S(1)}, u32[]{:S(2)}, u32[]{:S(2)}) collective-permute-start(f32[1,144,128]{2,1,0:T(8,128)S(1)} %get-tuple-element.82), channel_id=1, source_target_pairs={{0,30},{1,3},{2,0},{3,5},{4,2},{5,7},{6,4},{7,9},{8,6},{9,11},{10,... | collective-permute-start | bytes 221192 | tf_op jit(solution)/shard_map/ppermute | solution.py:682
  124.2 2.0 %collective-permute-done.20.right_ref = f32[1,144,128]{2,1,0:T(8,128)S(1)} collective-permute-done((f32[1,144,128]{2,1,0:T(8,128)S(1)}, f32[1,144,128]{2,1,0:T(8,128)S(1)}, u32[]{:S(2)}, u32[]{:S(2)}) %collective-permute-start.20) | collective-permute-done | bytes 73760 | tf_op jit(solution)/shard_map/ppermute | solution.py:682
  126.2 0.6 copy-done.26
  126.8 3.9 %collective-permute-done.19.left_ref = f32[1,144,128]{2,1,0:T(8,128)S(1)} collective-permute-done((f32[1,144,128]{2,1,0:T(8,128)S(1)}, f32[1,144,128]{2,1,0:T(8,128)S(1)}, u32[]{:S(2)}, u32[]{:S(2)}) %collective-permute-start.19) | collective-permute-done | bytes 73760 | tf_op jit(solution)/shard_map/ppermute | solution.py:679
  130.7 0.6 copy-done.28
  131.3 0.9 broadcast_in_dim.3
  132.2 3.5 %all-to-all-start = ((f32[32,32,128]{2,1,0:T(8,128)}), f32[32,32,128]{2,1,0:T(8,128)}, u32[]{:S(2)}, u32[]{:S(2)}) async-start(f32[32,32,128]{2,1,0:T(8,128)} %broadcast_in_dim.3), calls=%async_computation | async-start | bytes 1048576 | tf_op jit(solution)/shard_map/all_to_all | solution.py:851
  135.7 0.9 copy-done.27
  136.6 0.9 copy-done.29
  137.5 0.1 shard_map.258
  137.6 4.3 %collective-permute-start.27 = (f32[2,256,256]{2,1,0:T(8,128)S(1)}, f32[2,256,256]{2,1,0:T(8,128)}, u32[]{:S(2)}, u32[]{:S(2)}) collective-permute-start(f32[2,256,256]{2,1,0:T(8,128)S(1)} %get-tuple-element.71.near_base.near_ref), channel_id=1, source_target_pairs={{0,30},{1,3},{2,0},{3,5},{4,2},{5,7},{6,4},{7,9},{8,6},{9,11},{10,... | collective-permute-start | bytes 1572872 | tf_op jit(solution)/shard_map/ppermute | solution.py:682
  141.9 1.8 %collective-permute-start.22 = (f32[2,128,128]{2,1,0:T(8,128)S(1)}, f32[2,128,128]{2,1,0:T(8,128)S(1)}, u32[]{:S(2)}, u32[]{:S(2)}) collective-permute-start(f32[2,128,128]{2,1,0:T(8,128)S(1)} %shard_map.258), channel_id=1, source_target_pairs={{0,1},{1,0},{2,3},{3,2},{4,5},{5,4},{6,7},{7,6},{8,9},{9,8},{10,11... | collective-permute-start | bytes 393224 | tf_op jit(solution)/shard_map/ppermute | solution.py:670
  143.7 3.8 %collective-permute-done.22 = f32[2,128,128]{2,1,0:T(8,128)S(1)} collective-permute-done((f32[2,128,128]{2,1,0:T(8,128)S(1)}, f32[2,128,128]{2,1,0:T(8,128)S(1)}, u32[]{:S(2)}, u32[]{:S(2)}) %collective-permute-start.22) | collective-permute-done | bytes 131104 | tf_op jit(solution)/shard_map/ppermute | solution.py:670
  147.5 3.3 %collective-permute-start.24 = (f32[2,2,128,128]{3,2,1,0:T(8,128)S(1)}, f32[2,2,128,128]{3,2,1,0:T(8,128)}, u32[]{:S(2)}, u32[]{:S(2)}) collective-permute-start(f32[2,2,128,128]{3,2,1,0:T(8,128)S(1)} %pad_maximum_fusion.2.own_mid), channel_id=1, source_target_pairs={{0,30},{1,3},{2,0},{3,5},{4,2},{5,7},{6,4},{7,9},{8,6},{9,11},{10,... | collective-permute-start | bytes 786440 | tf_op jit(solution)/shard_map/ppermute | solution.py:682
  150.8 2.7 %collective-permute-start.25 = (f32[2,256,256]{2,1,0:T(8,128)S(1)}, f32[2,256,256]{2,1,0:T(8,128)}, u32[]{:S(2)}, u32[]{:S(2)}) collective-permute-start(f32[2,256,256]{2,1,0:T(8,128)S(1)} %get-tuple-element.70.far_base.far_ref), channel_id=1, source_target_pairs={{0,1},{1,0},{2,3},{3,2},{4,5},{5,4},{6,7},{7,6},{8,9},{9,8},{10,11... | collective-permute-start | bytes 1572872 | tf_op jit(solution)/shard_map/ppermute | solution.py:670
  153.6 2.5 %shard_map.257.spread_ref = f32[5,256,128]{2,1,0:T(8,128)S(1)} custom-call(f32[32,32,128]{2,1,0:T(8,128)} %all-to-all-done.all_ref, bf16[128,128]{1,0:T(8,128)(2,1)S(1)} %copy-done.33, bf16[256,128]{1,0:T(8,128)(2,1)S(1)} %copy-done.17), custom_call_target="tpu_custom_call" | custom-call | flops 10000000 | bytes 1277952 | tf_op jit(solution)/shard_map/pallas_call | solution.py:301
  156.2 3.4 %collective-permute-done.23.left_mid = f32[2,2,128,128]{3,2,1,0:T(8,128)} collective-permute-done((f32[2,2,128,128]{3,2,1,0:T(8,128)S(1)}, f32[2,2,128,128]{3,2,1,0:T(8,128)}, u32[]{:S(2)}, u32[]{:S(2)}) %collective-permute-start.23) | collective-permute-done | bytes 262176 | tf_op jit(solution)/shard_map/ppermute | solution.py:679
  159.6 1.4 shard_map.260
  161.1 1.4 collective-permute-start.28
  162.4 0.2 collective-permute-done.25.peer_base
  162.7 9.7 %shard_map.259 = (f32[3,2,512,256]{3,2,1,0:T(8,128)}, f32[4,256,256]{2,1,0:T(8,128)}) custom-call(f32[5,256,128]{2,1,0:T(8,128)S(1)} %shard_map.257.spread_ref, f32[2,2,128,128]{3,2,1,0:T(8,128)S(1)} %pad_maximum_fusion.2.own_mid, f32[2,2,128,128]{3,2,1,0:T(8,128)} %collective-permute-done.23.left_mid, f32[2,2,128,128]{3,2,1,0:T(8,128)} %collective-permute-done.24.right_mid, ...), custom_call_target="tpu_custom_call" | custom-call | flops 1000000000 | bytes 11468800 | tf_op jit(solution)/shard_map/pallas_call | solution.py:301
  172.4 1.0 collective-permute-done.28.peer_u
  173.4 2.1 %shard_map.261 = f32[3,2,512,256]{3,2,1,0:T(8,128)} custom-call(f32[3,2,512,256]{3,2,1,0:T(8,128)} %get-tuple-element.69.gradient_ref, f32[2,256,256]{2,1,0:T(8,128)S(1)} %get-tuple-element.73.own_u, f32[2,256,256]{2,1,0:T(8,128)S(1)} %collective-permute-done.28.peer_u, s32[2,512,256]{2,1,0:T(8,128)S(1)} %copy-done), custom_call_target="tpu_custom_call", output_to_operand_aliasing={{}: (0, {})} | custom-call | flops 10000000 | bytes 8388608 | tf_op jit(solution)/shard_map/pallas_call | solution.py:301
  (117 shorter events, 0.5 us)
Async XLA Ops:
  1.5 6.5 %collective-permute-start = (f32[4,32,256]{2,1,0:T(8,128)S(1)}, f32[4,32,256]{2,1,0:T(8,128)S(1)}, u32[]{:S(2)}, u32[]{:S(2)}) collective-permute-start(f32[4,32,256]{2,1,0:T(8,128)S(1)} %pad_maximum_fusion.3), channel_id=1, source_target_pairs={{0,1},{1,0},{2,3},{3,2},{4,5},{5,4},{6,7},{7,6},{8,9},{9,8},{10,11... | collective-permute-start | bytes 393224 | tf_op jit(solution)/shard_map/ppermute | solution.py:670
  7.2 24.8 %collective-permute-start.3 = (f32[2,2,256,256]{3,2,1,0:T(8,128)}, f32[2,2,256,256]{3,2,1,0:T(8,128)S(1)}, u32[]{:S(2)}, u32[]{:S(2)}) collective-permute-start(f32[2,2,256,256]{3,2,1,0:T(8,128)} %constant_dynamic-slice_fusion.3), channel_id=1, source_target_pairs={{0,1},{1,0},{2,3},{3,2},{4,5},{5,4},{6,7},{7,6},{8,9},{9,8},{10,11... | collective-permute-start | bytes 3145736 | tf_op jit(solution)/shard_map/ppermute | solution.py:670
  8.1 6.2 %copy-start.19 = (bf16[512,256]{1,0:T(8,128)(2,1)S(1)}, bf16[512,256]{1,0:T(8,128)(2,1)}, u32[]{:S(2)}) copy-start(bf16[512,256]{1,0:T(8,128)(2,1)} %constant.55.clone.rows_high) | copy-start | bytes 786436
  8.1 6.2 %copy-start.38 = (bf16[256,512]{1,0:T(8,128)(2,1)S(1)}, bf16[256,512]{1,0:T(8,128)(2,1)}, u32[]{:S(2)}) copy-start(bf16[256,512]{1,0:T(8,128)(2,1)} %constant.59.clone.depth_low) | copy-start | bytes 786436
  8.1 6.2 %copy-start.40 = (bf16[256,512]{1,0:T(8,128)(2,1)S(1)}, bf16[256,512]{1,0:T(8,128)(2,1)}, u32[]{:S(2)}) copy-start(bf16[256,512]{1,0:T(8,128)(2,1)} %constant.58.clone.depth_high) | copy-start | bytes 786436
  8.1 6.2 %copy-start.44 = (bf16[16,256]{1,0:T(8,128)(2,1)S(1)}, bf16[16,256]{1,0:T(8,128)(2,1)}, u32[]{:S(2)}) copy-start(bf16[16,256]{1,0:T(8,128)(2,1)} %constant.54.clone.basis_ref) | copy-start | bytes 24580
  9.5 4.8 %copy-start.3 = (f32[3,2,512,256]{3,2,1,0:T(8,128)S(1)}, f32[3,2,512,256]{3,2,1,0:T(8,128)}, u32[]{:S(2)}) copy-start(f32[3,2,512,256]{3,2,1,0:T(8,128)} %velocity_ref.1) | copy-start | bytes 9437188
  11.0 21.1 %collective-permute-start.2 = (f32[3,288,256]{2,1,0:T(8,128)}, f32[3,288,256]{2,1,0:T(8,128)}, u32[]{:S(2)}, u32[]{:S(2)}) collective-permute-start(f32[3,288,256]{2,1,0:T(8,128)} %get-tuple-element.76), channel_id=1, source_target_pairs={{0,30},{1,3},{2,0},{3,5},{4,2},{5,7},{6,4},{7,9},{8,6},{9,11},{10,... | collective-permute-start | bytes 2654216 | tf_op jit(solution)/shard_map/ppermute | solution.py:682
  14.3 17.8 %collective-permute-start.1 = (f32[3,288,256]{2,1,0:T(8,128)}, f32[3,288,256]{2,1,0:T(8,128)}, u32[]{:S(2)}, u32[]{:S(2)}) collective-permute-start(f32[3,288,256]{2,1,0:T(8,128)} %get-tuple-element.77), channel_id=1, source_target_pairs={{0,2},{1,31},{2,4},{3,1},{4,6},{5,3},{6,8},{7,5},{8,10},{9,7},{10,... | collective-permute-start | bytes 2654216 | tf_op jit(solution)/shard_map/ppermute | solution.py:679
  20.4 11.7 %copy-start.37 = (f32[2,280,256]{2,1,0:T(8,128)S(1)}, f32[2,280,256]{2,1,0:T(8,128)}, u32[]{:S(2)}) copy-start(f32[2,280,256]{2,1,0:T(8,128)} %copy-done.36) | copy-start | bytes 1720324
  20.4 15.1 %copy-start = (s32[2,512,256]{2,1,0:T(8,128)S(1)}, s32[2,512,256]{2,1,0:T(8,128)}, u32[]{:S(2)}) copy-start(s32[2,512,256]{2,1,0:T(8,128)} %solid_ref.3) | copy-start | bytes 3145732
  22.1 38.2 %copy-start.20 = (bf16[512,256]{1,0:T(8,128)(2,1)S(1)}, bf16[512,256]{1,0:T(8,128)(2,1)}, u32[]{:S(2)}) copy-start(bf16[512,256]{1,0:T(8,128)(2,1)} %constant.55.clone.rows_high) | copy-start | bytes 786436
  22.1 38.2 %copy-start.39 = (bf16[256,512]{1,0:T(8,128)(2,1)S(1)}, bf16[256,512]{1,0:T(8,128)(2,1)}, u32[]{:S(2)}) copy-start(bf16[256,512]{1,0:T(8,128)(2,1)} %constant.59.clone.depth_low) | copy-start | bytes 786436
  22.1 38.2 %copy-start.41 = (bf16[256,512]{1,0:T(8,128)(2,1)S(1)}, bf16[256,512]{1,0:T(8,128)(2,1)}, u32[]{:S(2)}) copy-start(bf16[256,512]{1,0:T(8,128)(2,1)} %constant.58.clone.depth_high) | copy-start | bytes 786436
  22.1 38.2 %copy-start.43 = (bf16[512,32]{1,0:T(8,128)(2,1)S(1)}, bf16[512,32]{1,0:T(8,128)(2,1)}, u32[]{:S(2)}) copy-start(bf16[512,32]{1,0:T(8,128)(2,1)} %constant.57.clone.spread) | copy-start | bytes 98308
  22.2 41.7 %collective-permute-start.5 = (f32[3,2,256,256]{3,2,1,0:T(8,128)S(1)}, f32[3,2,256,256]{3,2,1,0:T(8,128)S(1)}, u32[]{:S(2)}, u32[]{:S(2)}) collective-permute-start(f32[3,2,256,256]{3,2,1,0:T(8,128)S(1)} %constant_dynamic-slice_fusion.2.own_ref), channel_id=1, source_target_pairs={{0,30},{1,3},{2,0},{3,5},{4,2},{5,7},{6,4},{7,9},{8,6},{9,11},{10,... | collective-permute-start | bytes 4718600 | tf_op jit(solution)/shard_map/ppermute | solution.py:682
  32.0 31.8 %collective-permute-start.6 = (f32[2,2,256,256]{3,2,1,0:T(8,128)S(1)}, f32[2,2,256,256]{3,2,1,0:T(8,128)S(1)}, u32[]{:S(2)}, u32[]{:S(2)}) collective-permute-start(f32[2,2,256,256]{3,2,1,0:T(8,128)S(1)} %collective-permute-done.3.uv_ref.peers), channel_id=1, source_target_pairs={{0,2},{1,31},{2,4},{3,1},{4,6},{5,3},{6,8},{7,5},{8,10},{9,7},{10,... | collective-permute-start | bytes 3145736 | tf_op jit(solution)/shard_map/ppermute | solution.py:679
  32.1 11.1 %collective-permute-start.4 = (f32[2,280,256]{2,1,0:T(8,128)S(1)}, f32[2,280,256]{2,1,0:T(8,128)S(1)}, u32[]{:S(2)}, u32[]{:S(2)}) collective-permute-start(f32[2,280,256]{2,1,0:T(8,128)S(1)} %copy-done.37), channel_id=1, source_target_pairs={{0,1},{1,0},{2,3},{3,2},{4,5},{5,4},{6,7},{7,6},{8,9},{9,8},{10,11... | collective-permute-start | bytes 1720328 | tf_op jit(solution)/shard_map/ppermute | solution.py:670
  35.6 28.3 %collective-permute-start.7 = (s32[2,256,256]{2,1,0:T(8,128)S(1)}, s32[2,256,256]{2,1,0:T(8,128)S(1)}, u32[]{:S(2)}, u32[]{:S(2)}) collective-permute-start(s32[2,256,256]{2,1,0:T(8,128)S(1)} %get-tuple-element.78), channel_id=1, source_target_pairs={{0,1},{1,0},{2,3},{3,2},{4,5},{5,4},{6,7},{7,6},{8,9},{9,8},{10,11... | collective-permute-start | bytes 1572872 | tf_op jit(solution)/shard_map/ppermute | solution.py:670
  43.2 20.7 %copy-start.2 = (f32[3,2,256,256]{3,2,1,0:T(8,128)S(1)}, f32[3,2,256,256]{3,2,1,0:T(8,128)}, u32[]{:S(2)}) copy-start(f32[3,2,256,256]{3,2,1,0:T(8,128)} %copy-done.1) | copy-start | bytes 4718596
  43.2 26.3 %collective-permute-start.10 = (f32[2,256,256]{2,1,0:T(8,128)S(1)}, f32[2,256,256]{2,1,0:T(8,128)S(1)}, u32[]{:S(2)}, u32[]{:S(2)}) collective-permute-start(f32[2,256,256]{2,1,0:T(8,128)S(1)} %slice.54), channel_id=1, source_target_pairs={{0,2},{1,31},{2,4},{3,1},{4,6},{5,3},{6,8},{7,5},{8,10},{9,7},{10,... | collective-permute-start | bytes 1572872 | tf_op jit(solution)/shard_map/ppermute | solution.py:679
  63.9 5.7 %copy-start.35 = (bf16[4,16,64]{2,1,0:T(8,128)(2,1)S(1)}, bf16[4,16,64]{2,1,0:T(8,128)(2,1)}, u32[]{:S(2)}) copy-start(bf16[4,16,64]{2,1,0:T(8,128)(2,1)} %constant.60.clone.basis_ref) | copy-start | bytes 24580
  65.1 11.6 %copy-start.8 = (f32[2,256,256]{2,1,0:T(8,128)}, f32[2,256,256]{2,1,0:T(8,128)S(1)}, u32[]{:S(2)}) copy-start(f32[2,256,256]{2,1,0:T(8,128)S(1)} %get-tuple-element.44.near_u) | copy-start | bytes 1572868
  65.1 11.6 %copy-start.10 = (f32[2,256,256]{2,1,0:T(8,128)}, f32[2,256,256]{2,1,0:T(8,128)S(1)}, u32[]{:S(2)}) copy-start(f32[2,256,256]{2,1,0:T(8,128)S(1)} %get-tuple-element.45.far_u) | copy-start | bytes 1572868
  65.1 11.5 %collective-permute-start.8 = (f32[2,256,256]{2,1,0:T(8,128)S(1)}, f32[2,256,256]{2,1,0:T(8,128)S(1)}, u32[]{:S(2)}, u32[]{:S(2)}) collective-permute-start(f32[2,256,256]{2,1,0:T(8,128)S(1)} %get-tuple-element.45.far_u), channel_id=1, source_target_pairs={{0,2},{1,31},{2,4},{3,1},{4,6},{5,3},{6,8},{7,5},{8,10},{9,7},{10,... | collective-permute-start | bytes 1572872 | tf_op jit(solution)/shard_map/ppermute | solution.py:679
  68.1 5.1 %copy-start.12 = (bf16[256,256]{1,0:T(8,128)(2,1)S(1)}, bf16[256,256]{1,0:T(8,128)(2,1)}, u32[]{:S(2)}) copy-start(bf16[256,256]{1,0:T(8,128)(2,1)} %constant.62.clone.depth_low) | copy-start | bytes 393220
  68.1 5.1 %copy-start.14 = (bf16[256,256]{1,0:T(8,128)(2,1)S(1)}, bf16[256,256]{1,0:T(8,128)(2,1)}, u32[]{:S(2)}) copy-start(bf16[256,256]{1,0:T(8,128)(2,1)} %constant.61.clone.depth_high) | copy-start | bytes 393220
  68.1 8.5 %collective-permute-start.9 = (f32[2,256,256]{2,1,0:T(8,128)S(1)}, f32[2,256,256]{2,1,0:T(8,128)S(1)}, u32[]{:S(2)}, u32[]{:S(2)}) collective-permute-start(f32[2,256,256]{2,1,0:T(8,128)S(1)} %get-tuple-element.44.near_u), channel_id=1, source_target_pairs={{0,30},{1,3},{2,0},{3,5},{4,2},{5,7},{6,4},{7,9},{8,6},{9,11},{10,... | collective-permute-start | bytes 1572872 | tf_op jit(solution)/shard_map/ppermute | solution.py:682
  72.6 4.0 %collective-permute-start.11 = (f32[4,8,256]{2,1,0:T(8,128)S(1)}, f32[4,8,256]{2,1,0:T(8,128)S(1)}, u32[]{:S(2)}, u32[]{:S(2)}) collective-permute-start(f32[4,8,256]{2,1,0:T(8,128)S(1)} %get-tuple-element.51), channel_id=1, source_target_pairs={{0,1},{1,0},{2,3},{3,2},{4,5},{5,4},{6,7},{7,6},{8,9},{9,8},{10,11... | collective-permute-start | bytes 98312 | tf_op jit(solution)/shard_map/ppermute | solution.py:670
  74.2 28.0 %copy-start.17 = (bf16[256,128]{1,0:T(8,128)(2,1)S(1)}, bf16[256,128]{1,0:T(8,128)(2,1)}, u32[]{:S(2)}) copy-start(bf16[256,128]{1,0:T(8,128)(2,1)} %constant.64.clone.depth_pick.mid_rows) | copy-start | bytes 196612
  74.2 28.0 %copy-start.25 = (bf16[144,288]{1,0:T(8,128)(2,1)S(1)}, bf16[144,288]{1,0:T(8,128)(2,1)}, u32[]{:S(2)}) copy-start(bf16[144,288]{1,0:T(8,128)(2,1)} %constant.65.clone.rows_pick) | copy-start | bytes 248836
  77.7 24.5 %collective-permute-start.13 = (f32[2,256,256]{2,1,0:T(8,128)S(1)}, f32[2,256,256]{2,1,0:T(8,128)S(1)}, u32[]{:S(2)}, u32[]{:S(2)}) collective-permute-start(f32[2,256,256]{2,1,0:T(8,128)S(1)} %get-tuple-element.52.near_r), channel_id=1, source_target_pairs={{0,30},{1,3},{2,0},{3,5},{4,2},{5,7},{6,4},{7,9},{8,6},{9,11},{10,... | collective-permute-start | bytes 1572872 | tf_op jit(solution)/shard_map/ppermute | solution.py:682
  82.1 20.1 %collective-permute-start.12 = (f32[2,256,256]{2,1,0:T(8,128)S(1)}, f32[2,256,256]{2,1,0:T(8,128)S(1)}, u32[]{:S(2)}, u32[]{:S(2)}) collective-permute-start(f32[2,256,256]{2,1,0:T(8,128)S(1)} %get-tuple-element.53.far_r), channel_id=1, source_target_pairs={{0,2},{1,31},{2,4},{3,1},{4,6},{5,3},{6,8},{7,5},{8,10},{9,7},{10,... | collective-permute-start | bytes 1572872 | tf_op jit(solution)/shard_map/ppermute | solution.py:679
  83.1 7.1 %collective-permute-start.14 = (f32[4,32,256]{2,1,0:T(8,128)S(1)}, f32[4,32,256]{2,1,0:T(8,128)S(1)}, u32[]{:S(2)}, u32[]{:S(2)}) collective-permute-start(f32[4,32,256]{2,1,0:T(8,128)S(1)} %pad_maximum_fusion.4), channel_id=1, source_target_pairs={{0,1},{1,0},{2,3},{3,2},{4,5},{5,4},{6,7},{7,6},{8,9},{9,8},{10,11... | collective-permute-start | bytes 393224 | tf_op jit(solution)/shard_map/ppermute | solution.py:670
  90.3 7.5 %collective-permute-start.16 = (f32[2,32,256]{2,1,0:T(8,128)S(1)}, f32[2,32,256]{2,1,0:T(8,128)S(1)}, u32[]{:S(2)}, u32[]{:S(2)}) collective-permute-start(f32[2,32,256]{2,1,0:T(8,128)S(1)} %get-tuple-element.84), channel_id=1, source_target_pairs={{0,30},{1,3},{2,0},{3,5},{4,2},{5,7},{6,4},{7,9},{8,6},{9,11},{10,... | collective-permute-start | bytes 196616 | tf_op jit(solution)/shard_map/ppermute | solution.py:682
  95.8 6.4 %collective-permute-start.15 = (f32[2,32,256]{2,1,0:T(8,128)S(1)}, f32[2,32,256]{2,1,0:T(8,128)S(1)}, u32[]{:S(2)}, u32[]{:S(2)}) collective-permute-start(f32[2,32,256]{2,1,0:T(8,128)S(1)} %get-tuple-element.85), channel_id=1, source_target_pairs={{0,2},{1,31},{2,4},{3,1},{4,6},{5,3},{6,8},{7,5},{8,10},{9,7},{10,... | collective-permute-start | bytes 196616 | tf_op jit(solution)/shard_map/ppermute | solution.py:679
  107.7 10.6 %collective-permute-start.17 = (f32[432,256]{1,0:T(8,128)S(1)}, f32[432,256]{1,0:T(8,128)S(1)}, u32[]{:S(2)}, u32[]{:S(2)}) collective-permute-start(f32[432,256]{1,0:T(8,128)S(1)} %get-tuple-element.58), channel_id=1, source_target_pairs={{0,2},{1,31},{2,4},{3,1},{4,6},{5,3},{6,8},{7,5},{8,10},{9,7},{10,... | collective-permute-start | bytes 1327112 | tf_op jit(solution)/shard_map/ppermute | solution.py:679
  107.7 10.5 %collective-permute-start.18 = (f32[432,256]{1,0:T(8,128)S(1)}, f32[432,256]{1,0:T(8,128)S(1)}, u32[]{:S(2)}, u32[]{:S(2)}) collective-permute-start(f32[432,256]{1,0:T(8,128)S(1)} %get-tuple-element.59), channel_id=1, source_target_pairs={{0,30},{1,3},{2,0},{3,5},{4,2},{5,7},{6,4},{7,9},{8,6},{9,11},{10,... | collective-permute-start | bytes 1327112 | tf_op jit(solution)/shard_map/ppermute | solution.py:682
  113.2 5.9 %copy-start.31 = (bf16[128,256]{1,0:T(8,128)(2,1)S(1)}, bf16[128,256]{1,0:T(8,128)(2,1)}, u32[]{:S(2)}) copy-start(bf16[128,256]{1,0:T(8,128)(2,1)} %constant.66.clone.depth_pick) | copy-start | bytes 196612
  113.2 5.9 %copy-start.34 = (bf16[64,144]{1,0:T(8,128)(2,1)S(1)}, bf16[64,144]{1,0:T(8,128)(2,1)}, u32[]{:S(2)}) copy-start(bf16[64,144]{1,0:T(8,128)(2,1)} %constant.67.clone.rows_pick) | copy-start | bytes 55300
  113.2 22.5 %collective-permute-start.21 = (f32[2,2,256,256]{3,2,1,0:T(8,128)}, f32[2,2,256,256]{3,2,1,0:T(8,128)}, u32[]{:S(2)}, u32[]{:S(2)}) collective-permute-start(f32[2,2,256,256]{3,2,1,0:T(8,128)} %pad_maximum_fusion.1), channel_id=1, source_target_pairs={{0,1},{1,0},{2,3},{3,2},{4,5},{5,4},{6,7},{7,6},{8,9},{9,8},{10,11... | collective-permute-start | bytes 3145736 | tf_op jit(solution)/shard_map/ppermute | solution.py:670
  119.8 33.7 %copy-start.33 = (bf16[128,128]{1,0:T(8,128)(2,1)S(1)}, bf16[128,128]{1,0:T(8,128)(2,1)}, u32[]{:S(2)}) copy-start(bf16[128,128]{1,0:T(8,128)(2,1)} %constant.68.clone.mid_depth) | copy-start | bytes 98308
  119.8 6.4 %collective-permute-start.20 = (f32[1,144,128]{2,1,0:T(8,128)S(1)}, f32[1,144,128]{2,1,0:T(8,128)S(1)}, u32[]{:S(2)}, u32[]{:S(2)}) collective-permute-start(f32[1,144,128]{2,1,0:T(8,128)S(1)} %get-tuple-element.82), channel_id=1, source_target_pairs={{0,30},{1,3},{2,0},{3,5},{4,2},{5,7},{6,4},{7,9},{8,6},{9,11},{10,... | collective-permute-start | bytes 221192 | tf_op jit(solution)/shard_map/ppermute | solution.py:682
  124.2 6.5 %collective-permute-start.19 = (f32[1,144,128]{2,1,0:T(8,128)S(1)}, f32[1,144,128]{2,1,0:T(8,128)S(1)}, u32[]{:S(2)}, u32[]{:S(2)}) collective-permute-start(f32[1,144,128]{2,1,0:T(8,128)S(1)} %get-tuple-element.83), channel_id=1, source_target_pairs={{0,2},{1,31},{2,4},{3,1},{4,6},{5,3},{6,8},{7,5},{8,10},{9,7},{10,... | collective-permute-start | bytes 221192 | tf_op jit(solution)/shard_map/ppermute | solution.py:679
  132.2 27.4 %copy-start.9 = (f32[2,256,256]{2,1,0:T(8,128)S(1)}, f32[2,256,256]{2,1,0:T(8,128)}, u32[]{:S(2)}) copy-start(f32[2,256,256]{2,1,0:T(8,128)} %copy-done.8) | copy-start | bytes 1572868
  132.2 27.4 %copy-start.11 = (f32[2,256,256]{2,1,0:T(8,128)S(1)}, f32[2,256,256]{2,1,0:T(8,128)}, u32[]{:S(2)}) copy-start(f32[2,256,256]{2,1,0:T(8,128)} %copy-done.10) | copy-start | bytes 1572868
  132.2 21.4 %all-to-all-start = ((f32[32,32,128]{2,1,0:T(8,128)}), f32[32,32,128]{2,1,0:T(8,128)}, u32[]{:S(2)}, u32[]{:S(2)}) async-start(f32[32,32,128]{2,1,0:T(8,128)} %broadcast_in_dim.3), calls=%async_computation | async-start | bytes 1048576 | tf_op jit(solution)/shard_map/all_to_all | solution.py:851
  137.6 22.0 %collective-permute-start.27 = (f32[2,256,256]{2,1,0:T(8,128)S(1)}, f32[2,256,256]{2,1,0:T(8,128)}, u32[]{:S(2)}, u32[]{:S(2)}) collective-permute-start(f32[2,256,256]{2,1,0:T(8,128)S(1)} %get-tuple-element.71.near_base.near_ref), channel_id=1, source_target_pairs={{0,30},{1,3},{2,0},{3,5},{4,2},{5,7},{6,4},{7,9},{8,6},{9,11},{10,... | collective-permute-start | bytes 1572872 | tf_op jit(solution)/shard_map/ppermute | solution.py:682
  141.9 17.7 %collective-permute-start.26 = (f32[2,256,256]{2,1,0:T(8,128)S(1)}, f32[2,256,256]{2,1,0:T(8,128)}, u32[]{:S(2)}, u32[]{:S(2)}) collective-permute-start(f32[2,256,256]{2,1,0:T(8,128)S(1)} %get-tuple-element.70.far_base.far_ref), channel_id=1, source_target_pairs={{0,2},{1,31},{2,4},{3,1},{4,6},{5,3},{6,8},{7,5},{8,10},{9,7},{10,... | collective-permute-start | bytes 1572872 | tf_op jit(solution)/shard_map/ppermute | solution.py:679
  141.9 5.6 %collective-permute-start.22 = (f32[2,128,128]{2,1,0:T(8,128)S(1)}, f32[2,128,128]{2,1,0:T(8,128)S(1)}, u32[]{:S(2)}, u32[]{:S(2)}) collective-permute-start(f32[2,128,128]{2,1,0:T(8,128)S(1)} %shard_map.258), channel_id=1, source_target_pairs={{0,1},{1,0},{2,3},{3,2},{4,5},{5,4},{6,7},{7,6},{8,9},{9,8},{10,11... | collective-permute-start | bytes 393224 | tf_op jit(solution)/shard_map/ppermute | solution.py:670
  147.5 8.7 %collective-permute-start.24 = (f32[2,2,128,128]{3,2,1,0:T(8,128)S(1)}, f32[2,2,128,128]{3,2,1,0:T(8,128)}, u32[]{:S(2)}, u32[]{:S(2)}) collective-permute-start(f32[2,2,128,128]{3,2,1,0:T(8,128)S(1)} %pad_maximum_fusion.2.own_mid), channel_id=1, source_target_pairs={{0,30},{1,3},{2,0},{3,5},{4,2},{5,7},{6,4},{7,9},{8,6},{9,11},{10,... | collective-permute-start | bytes 786440 | tf_op jit(solution)/shard_map/ppermute | solution.py:682
  150.8 8.8 %collective-permute-start.23 = (f32[2,2,128,128]{3,2,1,0:T(8,128)S(1)}, f32[2,2,128,128]{3,2,1,0:T(8,128)}, u32[]{:S(2)}, u32[]{:S(2)}) collective-permute-start(f32[2,2,128,128]{3,2,1,0:T(8,128)S(1)} %pad_maximum_fusion.2.own_mid), channel_id=1, source_target_pairs={{0,2},{1,31},{2,4},{3,1},{4,6},{5,3},{6,8},{7,5},{8,10},{9,7},{10,... | collective-permute-start | bytes 786440 | tf_op jit(solution)/shard_map/ppermute | solution.py:679
  150.8 11.8 %collective-permute-start.25 = (f32[2,256,256]{2,1,0:T(8,128)S(1)}, f32[2,256,256]{2,1,0:T(8,128)}, u32[]{:S(2)}, u32[]{:S(2)}) collective-permute-start(f32[2,256,256]{2,1,0:T(8,128)S(1)} %get-tuple-element.70.far_base.far_ref), channel_id=1, source_target_pairs={{0,1},{1,0},{2,3},{3,2},{4,5},{5,4},{6,7},{7,6},{8,9},{9,8},{10,11... | collective-permute-start | bytes 1572872 | tf_op jit(solution)/shard_map/ppermute | solution.py:670
  156.1 6.5 %copy-start.5 = (f32[2,256,256]{2,1,0:T(8,128)S(1)}, f32[2,256,256]{2,1,0:T(8,128)}, u32[]{:S(2)}) copy-start(f32[2,256,256]{2,1,0:T(8,128)} %copy-done.4) | copy-start | bytes 1572868
  156.1 6.5 %copy-start.7 = (f32[2,256,256]{2,1,0:T(8,128)S(1)}, f32[2,256,256]{2,1,0:T(8,128)}, u32[]{:S(2)}) copy-start(f32[2,256,256]{2,1,0:T(8,128)} %copy-done.6) | copy-start | bytes 1572868
  156.1 6.5 %copy-start.13 = (bf16[256,256]{1,0:T(8,128)(2,1)S(1)}, bf16[256,256]{1,0:T(8,128)(2,1)}, u32[]{:S(2)}) copy-start(bf16[256,256]{1,0:T(8,128)(2,1)} %constant.62.clone.depth_low) | copy-start | bytes 393220
  156.1 6.5 %copy-start.15 = (bf16[256,256]{1,0:T(8,128)(2,1)S(1)}, bf16[256,256]{1,0:T(8,128)(2,1)}, u32[]{:S(2)}) copy-start(bf16[256,256]{1,0:T(8,128)(2,1)} %constant.61.clone.depth_high) | copy-start | bytes 393220
  156.1 6.5 %copy-start.16 = (bf16[512,256]{1,0:T(8,128)(2,1)S(1)}, bf16[512,256]{1,0:T(8,128)(2,1)}, u32[]{:S(2)}) copy-start(bf16[512,256]{1,0:T(8,128)(2,1)} %constant.74.clone.fine_rows) | copy-start | bytes 786436
  156.2 6.5 %copy-start.21 = (bf16[256,256]{1,0:T(8,128)(2,1)S(1)}, bf16[256,256]{1,0:T(8,128)(2,1)}, u32[]{:S(2)}) copy-start(bf16[256,256]{1,0:T(8,128)(2,1)} %constant.72.clone.diff_low) | copy-start | bytes 393220
  156.2 6.5 %copy-start.22 = (bf16[256,256]{1,0:T(8,128)(2,1)S(1)}, bf16[256,256]{1,0:T(8,128)(2,1)}, u32[]{:S(2)}) copy-start(bf16[256,256]{1,0:T(8,128)(2,1)} %constant.71.clone.diff_high) | copy-start | bytes 393220
  156.2 6.5 %copy-start.23 = (bf16[256,256]{1,0:T(8,128)(2,1)S(1)}, bf16[256,256]{1,0:T(8,128)(2,1)}, u32[]{:S(2)}) copy-start(bf16[256,256]{1,0:T(8,128)(2,1)} %constant.70.clone.sum_low) | copy-start | bytes 393220
  156.2 6.5 %copy-start.24 = (bf16[256,256]{1,0:T(8,128)(2,1)S(1)}, bf16[256,256]{1,0:T(8,128)(2,1)}, u32[]{:S(2)}) copy-start(bf16[256,256]{1,0:T(8,128)(2,1)} %constant.69.clone.sum_high) | copy-start | bytes 393220
  156.2 6.5 %copy-start.30 = (bf16[128,256]{1,0:T(8,128)(2,1)S(1)}, bf16[128,256]{1,0:T(8,128)(2,1)}, u32[]{:S(2)}) copy-start(bf16[128,256]{1,0:T(8,128)(2,1)} %constant.73.clone.fine_depth) | copy-start | bytes 196612
  161.1 12.4 %collective-permute-start.28 = (f32[2,256,256]{2,1,0:T(8,128)S(1)}, f32[2,256,256]{2,1,0:T(8,128)S(1)}, u32[]{:S(2)}, u32[]{:S(2)}) collective-permute-start(f32[2,256,256]{2,1,0:T(8,128)S(1)} %get-tuple-element.74), channel_id=1, source_target_pairs={{0,1},{1,0},{2,3},{3,2},{4,5},{5,4},{6,7},{7,6},{8,9},{9,8},{10,11... | collective-permute-start | bytes 1572872 | tf_op jit(solution)/shard_map/ppermute | solution.py:670
  (12 other events, 22.8 us)

commit v5 on v4

--- a/solution.py
+++ b/solution.py
@@ -590,9 +590,9 @@
     own_mid_rows = pl.ds(pl.multiple_of(side * mid_half, mid_half), mid_half)
     peer_mid_rows = pl.ds(pl.multiple_of((1 - side) * mid_half, mid_half), mid_half)
     for k in range(5):
-        held = (left_mid, own_mid, right_mid)[k // 2]
-        base[k, own_mid_rows] = held[0, k % 2]
-        base[k, peer_mid_rows] = held[1, 1 - k % 2]
+        held = left_mid if k < 2 else own_mid
+        base[k, own_mid_rows] = right_mid[0] if k == 4 else held[0, k % 2]
+        base[k, peer_mid_rows] = right_mid[1] if k == 4 else held[1, 1 - k % 2]
     for k in range(1, 8):
         centre = spread_ref[k // 2]
         total = spread_ref[(k - 1) // 2] + spread_ref[(k + 1) // 2] + cross_sum(centre)
@@ -847,7 +847,7 @@
     )
     peer_mid = swap(mid_base)
     both_mid = jnp.stack([mid_base, peer_mid])
-    left_mid, right_mid = (ahead(both_mid), behind(both_mid))
+    left_mid, right_mid = (ahead(both_mid), behind(jnp.stack([mid_base[0], peer_mid[1]])))
     low_all = lax.all_to_all(
         jnp.broadcast_to(tied(low_source, left_two, right_two), (2 * tunnel_size,) + low_source.shape), both, 0, 0, tiled=True
     )

time: 179 us -> 179 us (level); the launches traced: 176 us -> 179 us
  starting transfers between devices: 77.3 us -> 80 us
  transfers between devices with their start and end apart: 30 -> 30, of which waited for: 14 -> 13; matrix products, arithmetic and copies ran while one was open for 4% -> 5% of each run, Pallas kernels for 16% -> 16%
where the time goes in v5:
time: 179 us
  starting transfers between devices  80 us (45%)
  waiting for transfers between devices  44.7 us (25%)
  Pallas kernels  36.6 us (20%)
  local copies, waits for them, and re-layouts  11.6 us (6%)
  other arithmetic  4.53 us (3%)
    ppermute x9, starting transfers between devices, behind(): return lax.ppermute(value, both, behind_way)  36.7 us
    pallas_call x14, Pallas kernels, kernel_call(): pl.pallas_call(body, out_shape=[jax.ShapeDtypeStruct(s, f32) for s in out...  36.6 us
    ppermute x10, waiting for transfers between devices, swap(): return lax.ppermute(value, 'group', [(0, 1), (1, 0)])  24.8 us
    ppermute x10, starting transfers between devices, ahead(): return lax.ppermute(value, both, ahead_way)  21.2 us
    ppermute x10, starting transfers between devices, swap(): return lax.ppermute(value, 'group', [(0, 1), (1, 0)])  18.7 us
    ppermute x10, waiting for transfers between devices, ahead(): return lax.ppermute(value, both, ahead_way)  16 us
    unnamed x90, local copies, waits for them, and re-layouts  5.3 us
    ppermute x9, waiting for transfers between devices, behind(): return lax.ppermute(value, both, behind_way)  3.9 us
  transfers between devices with their start and end apart: 30, of which 13 were waited for; matrix products, arithmetic and copies ran while one was open for 5% of the time, Pallas kernels for 16%

profile of v5, /device:TPU:0, one launch (start us, length us, event | category | flops | bytes accessed | tf_op | source)
XLA Modules:
  0.0 178.8 jit_solution(1518077091495662598)
XLA Ops:
  0.6 0.9 fusion
  1.5 3.0 %collective-permute-start = (f32[4,32,256]{2,1,0:T(8,128)S(1)}, f32[4,32,256]{2,1,0:T(8,128)S(1)}, u32[]{:S(2)}, u32[]{:S(2)}) collective-permute-start(f32[4,32,256]{2,1,0:T(8,128)S(1)} %pad_maximum_fusion.3), channel_id=1, source_target_pairs={{0,1},{1,0},{2,3},{3,2},{4,5},{5,4},{6,7},{7,6},{8,9},{9,8},{10,11... | collective-permute-start | bytes 393224 | tf_op jit(solution)/shard_map/ppermute | solution.py:670
  4.6 1.6 slice-done
  6.2 1.1 constant_dynamic-slice_fusion.3
  7.2 0.8 collective-permute-done
  8.1 1.4 pad_maximum_fusion.pressure_tall
  9.6 1.4 slice_select_fusion
  11.0 3.3 %collective-permute-start.2 = (f32[3,288,256]{2,1,0:T(8,128)}, f32[3,288,256]{2,1,0:T(8,128)}, u32[]{:S(2)}, u32[]{:S(2)}) collective-permute-start(f32[3,288,256]{2,1,0:T(8,128)} %get-tuple-element.76), channel_id=1, source_target_pairs={{0,30},{1,3},{2,0},{3,5},{4,2},{5,7},{6,4},{7,9},{8,6},{9,11},{10,... | collective-permute-start | bytes 2654216 | tf_op jit(solution)/shard_map/ppermute | solution.py:682
  14.3 4.1 %shard_map.248 = (f32[3,2,256,256]{3,2,1,0:T(8,128)S(1)}, f32[2,280,256]{2,1,0:T(8,128)S(1)}) custom-call(f32[3,2,512,256]{3,2,1,0:T(8,128)S(1)} %copy-done.3, bf16[16,256]{1,0:T(8,128)(2,1)S(1)} %copy-done.44, bf16[512,256]{1,0:T(8,128)(2,1)S(1)} %copy-done.19, bf16[512,256]{1,0:T(8,128)(2,1)S(1)} %copy-done.18, bf16[512,32]{1,0:T(8,128)(2,1)S(1)} %copy-done.42, ...), custom_call_target="tpu_custom_call" | custom-call | flops 3000000000 | bytes 6381568 | tf_op jit(solution)/shard_map/pallas_call | solution.py:301
  18.4 1.1 copy-done.1
  19.6 0.8 copy-done.36
  20.4 1.7 constant_dynamic-slice_fusion.2.own_ref
  22.2 4.5 %collective-permute-start.5 = (f32[3,2,256,256]{3,2,1,0:T(8,128)S(1)}, f32[3,2,256,256]{3,2,1,0:T(8,128)S(1)}, u32[]{:S(2)}, u32[]{:S(2)}) collective-permute-start(f32[3,2,256,256]{3,2,1,0:T(8,128)S(1)} %constant_dynamic-slice_fusion.2.own_ref), channel_id=1, source_target_pairs={{0,30},{1,3},{2,0},{3,5},{4,2},{5,7},{6,4},{7,9},{8,6},{9,11},{10,... | collective-permute-start | bytes 4718600 | tf_op jit(solution)/shard_map/ppermute | solution.py:682
  26.6 5.4 %collective-permute-done.3.uv_ref.peers = f32[2,2,256,256]{3,2,1,0:T(8,128)S(1)} collective-permute-done((f32[2,2,256,256]{3,2,1,0:T(8,128)}, f32[2,2,256,256]{3,2,1,0:T(8,128)S(1)}, u32[]{:S(2)}, u32[]{:S(2)}) %collective-permute-start.3) | collective-permute-done | bytes 1048608 | tf_op jit(solution)/shard_map/ppermute | solution.py:670
  32.1 3.4 %collective-permute-start.4 = (f32[2,280,256]{2,1,0:T(8,128)S(1)}, f32[2,280,256]{2,1,0:T(8,128)S(1)}, u32[]{:S(2)}, u32[]{:S(2)}) collective-permute-start(f32[2,280,256]{2,1,0:T(8,128)S(1)} %copy-done.37), channel_id=1, source_target_pairs={{0,1},{1,0},{2,3},{3,2},{4,5},{5,4},{6,7},{7,6},{8,9},{9,8},{10,11... | collective-permute-start | bytes 1720328 | tf_op jit(solution)/shard_map/ppermute | solution.py:670
  35.5 0.1 constant_dynamic-slice_fusion
  35.6 0.1 collective-permute-start.7
  35.7 7.5 %collective-permute-done.4.w_ref.peer_w = f32[2,280,256]{2,1,0:T(8,128)S(1)} collective-permute-done((f32[2,280,256]{2,1,0:T(8,128)S(1)}, f32[2,280,256]{2,1,0:T(8,128)S(1)}, u32[]{:S(2)}, u32[]{:S(2)}) %collective-permute-start.4) | collective-permute-done | bytes 573472 | tf_op jit(solution)/shard_map/ppermute | solution.py:670
  43.2 17.1 %collective-permute-start.10 = (f32[2,256,256]{2,1,0:T(8,128)S(1)}, f32[2,256,256]{2,1,0:T(8,128)S(1)}, u32[]{:S(2)}, u32[]{:S(2)}) collective-permute-start(f32[2,256,256]{2,1,0:T(8,128)S(1)} %slice.62), channel_id=1, source_target_pairs={{0,2},{1,31},{2,4},{3,1},{4,6},{5,3},{6,8},{7,5},{8,10},{9,7},{10,... | collective-permute-start | bytes 1572872 | tf_op jit(solution)/shard_map/ppermute | solution.py:679
  60.4 3.5 %shard_map.249.raw_peer = f32[3,2,256,256]{3,2,1,0:T(8,128)S(1)} custom-call(f32[2,2,256,256]{3,2,1,0:T(8,128)S(1)} %collective-permute-done.3.uv_ref.peers, f32[2,280,256]{2,1,0:T(8,128)S(1)} %collective-permute-done.4.w_ref.peer_w, bf16[512,256]{1,0:T(8,128)(2,1)S(1)} %copy-done.20, bf16[512,256]{1,0:T(8,128)(2,1)S(1)} %copy-done.18, ...), custom_call_target="tpu_custom_call" | custom-call | flops 3000000000 | bytes 4276224 | tf_op jit(solution)/shard_map/pallas_call | solution.py:301
  63.9 1.1 shard_map.250
  65.1 3.1 %collective-permute-start.8 = (f32[2,256,256]{2,1,0:T(8,128)S(1)}, f32[2,256,256]{2,1,0:T(8,128)S(1)}, u32[]{:S(2)}, u32[]{:S(2)}) collective-permute-start(f32[2,256,256]{2,1,0:T(8,128)S(1)} %get-tuple-element.45.far_u), channel_id=1, source_target_pairs={{0,2},{1,31},{2,4},{3,1},{4,6},{5,3},{6,8},{7,5},{8,10},{9,7},{10,... | collective-permute-start | bytes 1572872 | tf_op jit(solution)/shard_map/ppermute | solution.py:679
  68.1 1.4 collective-permute-start.9
  69.6 3.0 %shard_map.251 = (f32[2,256,256]{2,1,0:T(8,128)S(1)}, f32[2,256,256]{2,1,0:T(8,128)S(1)}, f32[2,256,256]{2,1,0:T(8,128)S(1)}, f32[2,256,256]{2,1,0:T(8,128)S(1)}, f32[4,8,256]{2,1,0:T(8,128)S(1)}) custom-call(f32[3,2,256,256]{3,2,1,0:T(8,128)S(1)} %copy-done.2, f32[3,2,256,256]{3,2,1,0:T(8,128)S(1)} %shard_map.249.raw_peer, ...), custom_call_target="tpu_custom_call" | custom-call | flops 100000000 | bytes 12673024 | tf_op jit(solution)/shard_map/pallas_call | solution.py:301
  72.6 0.6 collective-permute-start.11
  73.2 1.0 shard_map.252.cross_ref
  74.2 2.4 %collective-permute-done.11.sum_ref = f32[4,8,256]{2,1,0:T(8,128)S(1)} collective-permute-done((f32[4,8,256]{2,1,0:T(8,128)S(1)}, f32[4,8,256]{2,1,0:T(8,128)S(1)}, u32[]{:S(2)}, u32[]{:S(2)}) %collective-permute-start.11) | collective-permute-done | bytes 32800 | tf_op jit(solution)/shard_map/ppermute | solution.py:670
  76.6 1.1 shard_map.253
  77.7 4.4 %collective-permute-start.13 = (f32[2,256,256]{2,1,0:T(8,128)S(1)}, f32[2,256,256]{2,1,0:T(8,128)S(1)}, u32[]{:S(2)}, u32[]{:S(2)}) collective-permute-start(f32[2,256,256]{2,1,0:T(8,128)S(1)} %get-tuple-element.52.near_r), channel_id=1, source_target_pairs={{0,30},{1,3},{2,0},{3,5},{4,2},{5,7},{6,4},{7,9},{8,6},{9,11},{10,... | collective-permute-start | bytes 1572872 | tf_op jit(solution)/shard_map/ppermute | solution.py:682
  82.1 1.0 collective-permute-start.12
  83.1 4.0 %collective-permute-start.14 = (f32[4,32,256]{2,1,0:T(8,128)S(1)}, f32[4,32,256]{2,1,0:T(8,128)S(1)}, u32[]{:S(2)}, u32[]{:S(2)}) collective-permute-start(f32[4,32,256]{2,1,0:T(8,128)S(1)} %pad_maximum_fusion.4), channel_id=1, source_target_pairs={{0,1},{1,0},{2,3},{3,2},{4,5},{5,4},{6,7},{7,6},{8,9},{9,8},{10,11... | collective-permute-start | bytes 393224 | tf_op jit(solution)/shard_map/ppermute | solution.py:670
  87.1 3.1 %collective-permute-done.14.edge_ref = f32[4,32,256]{2,1,0:T(8,128)S(1)} collective-permute-done((f32[4,32,256]{2,1,0:T(8,128)S(1)}, f32[4,32,256]{2,1,0:T(8,128)S(1)}, u32[]{:S(2)}, u32[]{:S(2)}) %collective-permute-start.14) | collective-permute-done | bytes 131104 | tf_op jit(solution)/shard_map/ppermute | solution.py:670
  90.3 5.6 %collective-permute-start.16 = (f32[2,32,256]{2,1,0:T(8,128)S(1)}, f32[2,32,256]{2,1,0:T(8,128)S(1)}, u32[]{:S(2)}, u32[]{:S(2)}) collective-permute-start(f32[2,32,256]{2,1,0:T(8,128)S(1)} %get-tuple-element.84), channel_id=1, source_target_pairs={{0,30},{1,3},{2,0},{3,5},{4,2},{5,7},{6,4},{7,9},{8,6},{9,11},{10,... | collective-permute-start | bytes 196616 | tf_op jit(solution)/shard_map/ppermute | solution.py:682
  95.9 1.9 %collective-permute-done.16.right_edge = f32[2,32,256]{2,1,0:T(8,128)S(1)} collective-permute-done((f32[2,32,256]{2,1,0:T(8,128)S(1)}, f32[2,32,256]{2,1,0:T(8,128)S(1)}, u32[]{:S(2)}, u32[]{:S(2)}) %collective-permute-start.16) | collective-permute-done | bytes 65568 | tf_op jit(solution)/shard_map/ppermute | solution.py:682
  97.8 4.5 %collective-permute-done.15.left_edge = f32[2,32,256]{2,1,0:T(8,128)S(1)} collective-permute-done((f32[2,32,256]{2,1,0:T(8,128)S(1)}, f32[2,32,256]{2,1,0:T(8,128)S(1)}, u32[]{:S(2)}, u32[]{:S(2)}) %collective-permute-start.15) | collective-permute-done | bytes 65568 | tf_op jit(solution)/shard_map/ppermute | solution.py:679
  102.3 5.4 %shard_map.254 = (f32[4,288,256]{2,1,0:T(8,128)S(1)}, f32[2,144,128]{2,1,0:T(8,128)S(1)}, f32[432,256]{1,0:T(8,128)S(1)}, f32[432,256]{1,0:T(8,128)S(1)}) custom-call(f32[4,288,256]{2,1,0:T(8,128)S(1)} %pad_maximum_fusion.pressure_tall, f32[3,288,256]{2,1,0:T(8,128)} %collective-permute-done.1.pressure_left, ...), custom_call_target="tpu_custom_call" | custom-call | flops 100000000 | bytes 7668736 | tf_op jit(solution)/shard_map/pallas_call | solution.py:301
  107.7 4.4 %collective-permute-start.18 = (f32[432,256]{1,0:T(8,128)S(1)}, f32[432,256]{1,0:T(8,128)S(1)}, u32[]{:S(2)}, u32[]{:S(2)}) collective-permute-start(f32[432,256]{1,0:T(8,128)S(1)} %get-tuple-element.59), channel_id=1, source_target_pairs={{0,30},{1,3},{2,0},{3,5},{4,2},{5,7},{6,4},{7,9},{8,6},{9,11},{10,... | collective-permute-start | bytes 1327112 | tf_op jit(solution)/shard_map/ppermute | solution.py:682
  112.2 1.0 pad_maximum_fusion.1
  113.2 5.0 %collective-permute-done.17.left_ref = f32[432,256]{1,0:T(8,128)S(1)} collective-permute-done((f32[432,256]{1,0:T(8,128)S(1)}, f32[432,256]{1,0:T(8,128)S(1)}, u32[]{:S(2)}, u32[]{:S(2)}) %collective-permute-start.17) | collective-permute-done | bytes 442400 | tf_op jit(solution)/shard_map/ppermute | solution.py:679
  118.3 0.8 shard_map.255
  119.1 0.7 shard_map.256
  119.8 4.4 %collective-permute-start.20 = (f32[1,144,128]{2,1,0:T(8,128)S(1)}, f32[1,144,128]{2,1,0:T(8,128)S(1)}, u32[]{:S(2)}, u32[]{:S(2)}) collective-permute-start(f32[1,144,128]{2,1,0:T(8,128)S(1)} %get-tuple-element.82), channel_id=1, source_target_pairs={{0,30},{1,3},{2,0},{3,5},{4,2},{5,7},{6,4},{7,9},{8,6},{9,11},{10,... | collective-permute-start | bytes 221192 | tf_op jit(solution)/shard_map/ppermute | solution.py:682
  124.2 2.0 %collective-permute-done.20.right_ref = f32[1,144,128]{2,1,0:T(8,128)S(1)} collective-permute-done((f32[1,144,128]{2,1,0:T(8,128)S(1)}, f32[1,144,128]{2,1,0:T(8,128)S(1)}, u32[]{:S(2)}, u32[]{:S(2)}) %collective-permute-start.20) | collective-permute-done | bytes 73760 | tf_op jit(solution)/shard_map/ppermute | solution.py:682
  126.2 0.6 copy-done.26
  126.8 3.9 %collective-permute-done.19.left_ref = f32[1,144,128]{2,1,0:T(8,128)S(1)} collective-permute-done((f32[1,144,128]{2,1,0:T(8,128)S(1)}, f32[1,144,128]{2,1,0:T(8,128)S(1)}, u32[]{:S(2)}, u32[]{:S(2)}) %collective-permute-start.19) | collective-permute-done | bytes 73760 | tf_op jit(solution)/shard_map/ppermute | solution.py:679
  130.7 0.6 copy-done.28
  131.3 0.9 broadcast_in_dim.3
  132.2 3.3 %all-to-all-start = ((f32[32,32,128]{2,1,0:T(8,128)}), f32[32,32,128]{2,1,0:T(8,128)}, u32[]{:S(2)}, u32[]{:S(2)}) async-start(f32[32,32,128]{2,1,0:T(8,128)} %broadcast_in_dim.3), calls=%async_computation | async-start | bytes 1048576 | tf_op jit(solution)/shard_map/all_to_all | solution.py:851
  135.6 1.0 copy-done.27
  136.5 0.9 copy-done.29
  137.4 0.1 shard_map.258
  137.6 4.3 %collective-permute-start.27 = (f32[2,256,256]{2,1,0:T(8,128)S(1)}, f32[2,256,256]{2,1,0:T(8,128)}, u32[]{:S(2)}, u32[]{:S(2)}) collective-permute-start(f32[2,256,256]{2,1,0:T(8,128)S(1)} %get-tuple-element.71.near_base.near_ref), channel_id=1, source_target_pairs={{0,30},{1,3},{2,0},{3,5},{4,2},{5,7},{6,4},{7,9},{8,6},{9,11},{10,... | collective-permute-start | bytes 1572872 | tf_op jit(solution)/shard_map/ppermute | solution.py:682
  141.8 1.8 %collective-permute-start.22 = (f32[2,128,128]{2,1,0:T(8,128)S(1)}, f32[2,128,128]{2,1,0:T(8,128)S(1)}, u32[]{:S(2)}, u32[]{:S(2)}) collective-permute-start(f32[2,128,128]{2,1,0:T(8,128)S(1)} %shard_map.258), channel_id=1, source_target_pairs={{0,1},{1,0},{2,3},{3,2},{4,5},{5,4},{6,7},{7,6},{8,9},{9,8},{10,11... | collective-permute-start | bytes 393224 | tf_op jit(solution)/shard_map/ppermute | solution.py:670
  143.6 3.8 %collective-permute-done.22 = f32[2,128,128]{2,1,0:T(8,128)S(1)} collective-permute-done((f32[2,128,128]{2,1,0:T(8,128)S(1)}, f32[2,128,128]{2,1,0:T(8,128)S(1)}, u32[]{:S(2)}, u32[]{:S(2)}) %collective-permute-start.22) | collective-permute-done | bytes 131104 | tf_op jit(solution)/shard_map/ppermute | solution.py:670
  147.5 0.7 pad_maximum_fusion.5
  148.2 4.4 %collective-permute-start.24 = (f32[2,128,128]{2,1,0:T(8,128)}, f32[2,128,128]{2,1,0:T(8,128)}, u32[]{:S(2)}, u32[]{:S(2)}) collective-permute-start(f32[2,128,128]{2,1,0:T(8,128)} %pad_maximum_fusion.5), channel_id=1, source_target_pairs={{0,30},{1,3},{2,0},{3,5},{4,2},{5,7},{6,4},{7,9},{8,6},{9,11},{10,... | collective-permute-start | bytes 393224 | tf_op jit(solution)/shard_map/ppermute | solution.py:682
  152.6 0.2 collective-permute-start.25
  152.8 2.5 %shard_map.257.spread_ref = f32[5,256,128]{2,1,0:T(8,128)S(1)} custom-call(f32[32,32,128]{2,1,0:T(8,128)} %all-to-all-done.all_ref, bf16[128,128]{1,0:T(8,128)(2,1)S(1)} %copy-done.33, bf16[256,128]{1,0:T(8,128)(2,1)S(1)} %copy-done.17), custom_call_target="tpu_custom_call" | custom-call | flops 10000000 | bytes 1277952 | tf_op jit(solution)/shard_map/pallas_call | solution.py:301
  155.5 2.6 %collective-permute-done.23.left_mid = f32[2,2,128,128]{3,2,1,0:T(8,128)} collective-permute-done((f32[2,2,128,128]{3,2,1,0:T(8,128)S(1)}, f32[2,2,128,128]{3,2,1,0:T(8,128)}, u32[]{:S(2)}, u32[]{:S(2)}) %collective-permute-start.23) | collective-permute-done | bytes 262176 | tf_op jit(solution)/shard_map/ppermute | solution.py:679
  158.1 1.4 shard_map.260
  159.5 5.6 %collective-permute-start.28 = (f32[2,256,256]{2,1,0:T(8,128)S(1)}, f32[2,256,256]{2,1,0:T(8,128)S(1)}, u32[]{:S(2)}, u32[]{:S(2)}) collective-permute-start(f32[2,256,256]{2,1,0:T(8,128)S(1)} %get-tuple-element.74), channel_id=1, source_target_pairs={{0,1},{1,0},{2,3},{3,2},{4,5},{5,4},{6,7},{7,6},{8,9},{9,8},{10,11... | collective-permute-start | bytes 1572872 | tf_op jit(solution)/shard_map/ppermute | solution.py:670
  165.2 9.7 %shard_map.259 = (f32[3,2,512,256]{3,2,1,0:T(8,128)}, f32[4,256,256]{2,1,0:T(8,128)}) custom-call(f32[5,256,128]{2,1,0:T(8,128)S(1)} %shard_map.257.spread_ref, f32[2,2,128,128]{3,2,1,0:T(8,128)S(1)} %pad_maximum_fusion.2.own_mid, f32[2,2,128,128]{3,2,1,0:T(8,128)} %collective-permute-done.23.left_mid, f32[2,128,128]{2,1,0:T(8,128)} %collective-permute-done.24.right_mid, ...), custom_call_target="tpu_custom_call" | custom-call | flops 1000000000 | bytes 11337728 | tf_op jit(solution)/shard_map/pallas_call | solution.py:301
  174.9 1.8 %collective-permute-done.28.peer_u = f32[2,256,256]{2,1,0:T(8,128)S(1)} collective-permute-done((f32[2,256,256]{2,1,0:T(8,128)S(1)}, f32[2,256,256]{2,1,0:T(8,128)S(1)}, u32[]{:S(2)}, u32[]{:S(2)}) %collective-permute-start.28) | collective-permute-done | bytes 524320 | tf_op jit(solution)/shard_map/ppermute | solution.py:670
  176.7 2.1 %shard_map.261 = f32[3,2,512,256]{3,2,1,0:T(8,128)} custom-call(f32[3,2,512,256]{3,2,1,0:T(8,128)} %get-tuple-element.69.gradient_ref, f32[2,256,256]{2,1,0:T(8,128)S(1)} %get-tuple-element.73.own_u, f32[2,256,256]{2,1,0:T(8,128)S(1)} %collective-permute-done.28.peer_u, s32[2,512,256]{2,1,0:T(8,128)S(1)} %copy-done), custom_call_target="tpu_custom_call", output_to_operand_aliasing={{}: (0, {})} | custom-call | flops 10000000 | bytes 8388608 | tf_op jit(solution)/shard_map/pallas_call | solution.py:301
  (120 shorter events, 0.6 us)
Async XLA Ops:
  1.5 6.5 %collective-permute-start = (f32[4,32,256]{2,1,0:T(8,128)S(1)}, f32[4,32,256]{2,1,0:T(8,128)S(1)}, u32[]{:S(2)}, u32[]{:S(2)}) collective-permute-start(f32[4,32,256]{2,1,0:T(8,128)S(1)} %pad_maximum_fusion.3), channel_id=1, source_target_pairs={{0,1},{1,0},{2,3},{3,2},{4,5},{5,4},{6,7},{7,6},{8,9},{9,8},{10,11... | collective-permute-start | bytes 393224 | tf_op jit(solution)/shard_map/ppermute | solution.py:670
  7.2 24.8 %collective-permute-start.3 = (f32[2,2,256,256]{3,2,1,0:T(8,128)}, f32[2,2,256,256]{3,2,1,0:T(8,128)S(1)}, u32[]{:S(2)}, u32[]{:S(2)}) collective-permute-start(f32[2,2,256,256]{3,2,1,0:T(8,128)} %constant_dynamic-slice_fusion.3), channel_id=1, source_target_pairs={{0,1},{1,0},{2,3},{3,2},{4,5},{5,4},{6,7},{7,6},{8,9},{9,8},{10,11... | collective-permute-start | bytes 3145736 | tf_op jit(solution)/shard_map/ppermute | solution.py:670
  8.1 6.2 %copy-start.19 = (bf16[512,256]{1,0:T(8,128)(2,1)S(1)}, bf16[512,256]{1,0:T(8,128)(2,1)}, u32[]{:S(2)}) copy-start(bf16[512,256]{1,0:T(8,128)(2,1)} %constant.55.clone.rows_high) | copy-start | bytes 786436
  8.1 6.2 %copy-start.38 = (bf16[256,512]{1,0:T(8,128)(2,1)S(1)}, bf16[256,512]{1,0:T(8,128)(2,1)}, u32[]{:S(2)}) copy-start(bf16[256,512]{1,0:T(8,128)(2,1)} %constant.59.clone.depth_low) | copy-start | bytes 786436
  8.1 6.2 %copy-start.40 = (bf16[256,512]{1,0:T(8,128)(2,1)S(1)}, bf16[256,512]{1,0:T(8,128)(2,1)}, u32[]{:S(2)}) copy-start(bf16[256,512]{1,0:T(8,128)(2,1)} %constant.58.clone.depth_high) | copy-start | bytes 786436
  8.1 6.2 %copy-start.44 = (bf16[16,256]{1,0:T(8,128)(2,1)S(1)}, bf16[16,256]{1,0:T(8,128)(2,1)}, u32[]{:S(2)}) copy-start(bf16[16,256]{1,0:T(8,128)(2,1)} %constant.54.clone.basis_ref) | copy-start | bytes 24580
  9.5 4.8 %copy-start.3 = (f32[3,2,512,256]{3,2,1,0:T(8,128)S(1)}, f32[3,2,512,256]{3,2,1,0:T(8,128)}, u32[]{:S(2)}) copy-start(f32[3,2,512,256]{3,2,1,0:T(8,128)} %velocity_ref.1) | copy-start | bytes 9437188
  11.0 21.1 %collective-permute-start.2 = (f32[3,288,256]{2,1,0:T(8,128)}, f32[3,288,256]{2,1,0:T(8,128)}, u32[]{:S(2)}, u32[]{:S(2)}) collective-permute-start(f32[3,288,256]{2,1,0:T(8,128)} %get-tuple-element.76), channel_id=1, source_target_pairs={{0,30},{1,3},{2,0},{3,5},{4,2},{5,7},{6,4},{7,9},{8,6},{9,11},{10,... | collective-permute-start | bytes 2654216 | tf_op jit(solution)/shard_map/ppermute | solution.py:682
  14.3 17.8 %collective-permute-start.1 = (f32[3,288,256]{2,1,0:T(8,128)}, f32[3,288,256]{2,1,0:T(8,128)}, u32[]{:S(2)}, u32[]{:S(2)}) collective-permute-start(f32[3,288,256]{2,1,0:T(8,128)} %get-tuple-element.77), channel_id=1, source_target_pairs={{0,2},{1,31},{2,4},{3,1},{4,6},{5,3},{6,8},{7,5},{8,10},{9,7},{10,... | collective-permute-start | bytes 2654216 | tf_op jit(solution)/shard_map/ppermute | solution.py:679
  20.4 11.7 %copy-start.37 = (f32[2,280,256]{2,1,0:T(8,128)S(1)}, f32[2,280,256]{2,1,0:T(8,128)}, u32[]{:S(2)}) copy-start(f32[2,280,256]{2,1,0:T(8,128)} %copy-done.36) | copy-start | bytes 1720324
  20.4 15.1 %copy-start = (s32[2,512,256]{2,1,0:T(8,128)S(1)}, s32[2,512,256]{2,1,0:T(8,128)}, u32[]{:S(2)}) copy-start(s32[2,512,256]{2,1,0:T(8,128)} %solid_ref.3) | copy-start | bytes 3145732
  22.1 38.2 %copy-start.20 = (bf16[512,256]{1,0:T(8,128)(2,1)S(1)}, bf16[512,256]{1,0:T(8,128)(2,1)}, u32[]{:S(2)}) copy-start(bf16[512,256]{1,0:T(8,128)(2,1)} %constant.55.clone.rows_high) | copy-start | bytes 786436
  22.1 38.2 %copy-start.39 = (bf16[256,512]{1,0:T(8,128)(2,1)S(1)}, bf16[256,512]{1,0:T(8,128)(2,1)}, u32[]{:S(2)}) copy-start(bf16[256,512]{1,0:T(8,128)(2,1)} %constant.59.clone.depth_low) | copy-start | bytes 786436
  22.1 38.2 %copy-start.41 = (bf16[256,512]{1,0:T(8,128)(2,1)S(1)}, bf16[256,512]{1,0:T(8,128)(2,1)}, u32[]{:S(2)}) copy-start(bf16[256,512]{1,0:T(8,128)(2,1)} %constant.58.clone.depth_high) | copy-start | bytes 786436
  22.1 38.2 %copy-start.43 = (bf16[512,32]{1,0:T(8,128)(2,1)S(1)}, bf16[512,32]{1,0:T(8,128)(2,1)}, u32[]{:S(2)}) copy-start(bf16[512,32]{1,0:T(8,128)(2,1)} %constant.57.clone.spread) | copy-start | bytes 98308
  22.2 41.7 %collective-permute-start.5 = (f32[3,2,256,256]{3,2,1,0:T(8,128)S(1)}, f32[3,2,256,256]{3,2,1,0:T(8,128)S(1)}, u32[]{:S(2)}, u32[]{:S(2)}) collective-permute-start(f32[3,2,256,256]{3,2,1,0:T(8,128)S(1)} %constant_dynamic-slice_fusion.2.own_ref), channel_id=1, source_target_pairs={{0,30},{1,3},{2,0},{3,5},{4,2},{5,7},{6,4},{7,9},{8,6},{9,11},{10,... | collective-permute-start | bytes 4718600 | tf_op jit(solution)/shard_map/ppermute | solution.py:682
  32.0 31.8 %collective-permute-start.6 = (f32[2,2,256,256]{3,2,1,0:T(8,128)S(1)}, f32[2,2,256,256]{3,2,1,0:T(8,128)S(1)}, u32[]{:S(2)}, u32[]{:S(2)}) collective-permute-start(f32[2,2,256,256]{3,2,1,0:T(8,128)S(1)} %collective-permute-done.3.uv_ref.peers), channel_id=1, source_target_pairs={{0,2},{1,31},{2,4},{3,1},{4,6},{5,3},{6,8},{7,5},{8,10},{9,7},{10,... | collective-permute-start | bytes 3145736 | tf_op jit(solution)/shard_map/ppermute | solution.py:679
  32.1 11.1 %collective-permute-start.4 = (f32[2,280,256]{2,1,0:T(8,128)S(1)}, f32[2,280,256]{2,1,0:T(8,128)S(1)}, u32[]{:S(2)}, u32[]{:S(2)}) collective-permute-start(f32[2,280,256]{2,1,0:T(8,128)S(1)} %copy-done.37), channel_id=1, source_target_pairs={{0,1},{1,0},{2,3},{3,2},{4,5},{5,4},{6,7},{7,6},{8,9},{9,8},{10,11... | collective-permute-start | bytes 1720328 | tf_op jit(solution)/shard_map/ppermute | solution.py:670
  35.6 28.3 %collective-permute-start.7 = (s32[2,256,256]{2,1,0:T(8,128)S(1)}, s32[2,256,256]{2,1,0:T(8,128)S(1)}, u32[]{:S(2)}, u32[]{:S(2)}) collective-permute-start(s32[2,256,256]{2,1,0:T(8,128)S(1)} %get-tuple-element.78), channel_id=1, source_target_pairs={{0,1},{1,0},{2,3},{3,2},{4,5},{5,4},{6,7},{7,6},{8,9},{9,8},{10,11... | collective-permute-start | bytes 1572872 | tf_op jit(solution)/shard_map/ppermute | solution.py:670
  43.2 20.7 %copy-start.2 = (f32[3,2,256,256]{3,2,1,0:T(8,128)S(1)}, f32[3,2,256,256]{3,2,1,0:T(8,128)}, u32[]{:S(2)}) copy-start(f32[3,2,256,256]{3,2,1,0:T(8,128)} %copy-done.1) | copy-start | bytes 4718596
  43.2 26.3 %collective-permute-start.10 = (f32[2,256,256]{2,1,0:T(8,128)S(1)}, f32[2,256,256]{2,1,0:T(8,128)S(1)}, u32[]{:S(2)}, u32[]{:S(2)}) collective-permute-start(f32[2,256,256]{2,1,0:T(8,128)S(1)} %slice.62), channel_id=1, source_target_pairs={{0,2},{1,31},{2,4},{3,1},{4,6},{5,3},{6,8},{7,5},{8,10},{9,7},{10,... | collective-permute-start | bytes 1572872 | tf_op jit(solution)/shard_map/ppermute | solution.py:679
  63.9 5.7 %copy-start.35 = (bf16[4,16,64]{2,1,0:T(8,128)(2,1)S(1)}, bf16[4,16,64]{2,1,0:T(8,128)(2,1)}, u32[]{:S(2)}) copy-start(bf16[4,16,64]{2,1,0:T(8,128)(2,1)} %constant.60.clone.basis_ref) | copy-start | bytes 24580
  65.1 11.6 %copy-start.8 = (f32[2,256,256]{2,1,0:T(8,128)}, f32[2,256,256]{2,1,0:T(8,128)S(1)}, u32[]{:S(2)}) copy-start(f32[2,256,256]{2,1,0:T(8,128)S(1)} %get-tuple-element.44.near_u) | copy-start | bytes 1572868
  65.1 11.6 %copy-start.10 = (f32[2,256,256]{2,1,0:T(8,128)}, f32[2,256,256]{2,1,0:T(8,128)S(1)}, u32[]{:S(2)}) copy-start(f32[2,256,256]{2,1,0:T(8,128)S(1)} %get-tuple-element.45.far_u) | copy-start | bytes 1572868
  65.1 11.5 %collective-permute-start.8 = (f32[2,256,256]{2,1,0:T(8,128)S(1)}, f32[2,256,256]{2,1,0:T(8,128)S(1)}, u32[]{:S(2)}, u32[]{:S(2)}) collective-permute-start(f32[2,256,256]{2,1,0:T(8,128)S(1)} %get-tuple-element.45.far_u), channel_id=1, source_target_pairs={{0,2},{1,31},{2,4},{3,1},{4,6},{5,3},{6,8},{7,5},{8,10},{9,7},{10,... | collective-permute-start | bytes 1572872 | tf_op jit(solution)/shard_map/ppermute | solution.py:679
  68.1 5.1 %copy-start.12 = (bf16[256,256]{1,0:T(8,128)(2,1)S(1)}, bf16[256,256]{1,0:T(8,128)(2,1)}, u32[]{:S(2)}) copy-start(bf16[256,256]{1,0:T(8,128)(2,1)} %constant.62.clone.depth_low) | copy-start | bytes 393220
  68.1 5.1 %copy-start.14 = (bf16[256,256]{1,0:T(8,128)(2,1)S(1)}, bf16[256,256]{1,0:T(8,128)(2,1)}, u32[]{:S(2)}) copy-start(bf16[256,256]{1,0:T(8,128)(2,1)} %constant.61.clone.depth_high) | copy-start | bytes 393220
  68.1 8.5 %collective-permute-start.9 = (f32[2,256,256]{2,1,0:T(8,128)S(1)}, f32[2,256,256]{2,1,0:T(8,128)S(1)}, u32[]{:S(2)}, u32[]{:S(2)}) collective-permute-start(f32[2,256,256]{2,1,0:T(8,128)S(1)} %get-tuple-element.44.near_u), channel_id=1, source_target_pairs={{0,30},{1,3},{2,0},{3,5},{4,2},{5,7},{6,4},{7,9},{8,6},{9,11},{10,... | collective-permute-start | bytes 1572872 | tf_op jit(solution)/shard_map/ppermute | solution.py:682
  72.6 4.0 %collective-permute-start.11 = (f32[4,8,256]{2,1,0:T(8,128)S(1)}, f32[4,8,256]{2,1,0:T(8,128)S(1)}, u32[]{:S(2)}, u32[]{:S(2)}) collective-permute-start(f32[4,8,256]{2,1,0:T(8,128)S(1)} %get-tuple-element.51), channel_id=1, source_target_pairs={{0,1},{1,0},{2,3},{3,2},{4,5},{5,4},{6,7},{7,6},{8,9},{9,8},{10,11... | collective-permute-start | bytes 98312 | tf_op jit(solution)/shard_map/ppermute | solution.py:670
  74.2 28.0 %copy-start.17 = (bf16[256,128]{1,0:T(8,128)(2,1)S(1)}, bf16[256,128]{1,0:T(8,128)(2,1)}, u32[]{:S(2)}) copy-start(bf16[256,128]{1,0:T(8,128)(2,1)} %constant.64.clone.depth_pick.mid_rows) | copy-start | bytes 196612
  74.2 28.0 %copy-start.25 = (bf16[144,288]{1,0:T(8,128)(2,1)S(1)}, bf16[144,288]{1,0:T(8,128)(2,1)}, u32[]{:S(2)}) copy-start(bf16[144,288]{1,0:T(8,128)(2,1)} %constant.65.clone.rows_pick) | copy-start | bytes 248836
  77.7 24.5 %collective-permute-start.13 = (f32[2,256,256]{2,1,0:T(8,128)S(1)}, f32[2,256,256]{2,1,0:T(8,128)S(1)}, u32[]{:S(2)}, u32[]{:S(2)}) collective-permute-start(f32[2,256,256]{2,1,0:T(8,128)S(1)} %get-tuple-element.52.near_r), channel_id=1, source_target_pairs={{0,30},{1,3},{2,0},{3,5},{4,2},{5,7},{6,4},{7,9},{8,6},{9,11},{10,... | collective-permute-start | bytes 1572872 | tf_op jit(solution)/shard_map/ppermute | solution.py:682
  82.1 20.1 %collective-permute-start.12 = (f32[2,256,256]{2,1,0:T(8,128)S(1)}, f32[2,256,256]{2,1,0:T(8,128)S(1)}, u32[]{:S(2)}, u32[]{:S(2)}) collective-permute-start(f32[2,256,256]{2,1,0:T(8,128)S(1)} %get-tuple-element.53.far_r), channel_id=1, source_target_pairs={{0,2},{1,31},{2,4},{3,1},{4,6},{5,3},{6,8},{7,5},{8,10},{9,7},{10,... | collective-permute-start | bytes 1572872 | tf_op jit(solution)/shard_map/ppermute | solution.py:679
  83.1 7.1 %collective-permute-start.14 = (f32[4,32,256]{2,1,0:T(8,128)S(1)}, f32[4,32,256]{2,1,0:T(8,128)S(1)}, u32[]{:S(2)}, u32[]{:S(2)}) collective-permute-start(f32[4,32,256]{2,1,0:T(8,128)S(1)} %pad_maximum_fusion.4), channel_id=1, source_target_pairs={{0,1},{1,0},{2,3},{3,2},{4,5},{5,4},{6,7},{7,6},{8,9},{9,8},{10,11... | collective-permute-start | bytes 393224 | tf_op jit(solution)/shard_map/ppermute | solution.py:670
  90.3 7.5 %collective-permute-start.16 = (f32[2,32,256]{2,1,0:T(8,128)S(1)}, f32[2,32,256]{2,1,0:T(8,128)S(1)}, u32[]{:S(2)}, u32[]{:S(2)}) collective-permute-start(f32[2,32,256]{2,1,0:T(8,128)S(1)} %get-tuple-element.84), channel_id=1, source_target_pairs={{0,30},{1,3},{2,0},{3,5},{4,2},{5,7},{6,4},{7,9},{8,6},{9,11},{10,... | collective-permute-start | bytes 196616 | tf_op jit(solution)/shard_map/ppermute | solution.py:682
  95.8 6.4 %collective-permute-start.15 = (f32[2,32,256]{2,1,0:T(8,128)S(1)}, f32[2,32,256]{2,1,0:T(8,128)S(1)}, u32[]{:S(2)}, u32[]{:S(2)}) collective-permute-start(f32[2,32,256]{2,1,0:T(8,128)S(1)} %get-tuple-element.85), channel_id=1, source_target_pairs={{0,2},{1,31},{2,4},{3,1},{4,6},{5,3},{6,8},{7,5},{8,10},{9,7},{10,... | collective-permute-start | bytes 196616 | tf_op jit(solution)/shard_map/ppermute | solution.py:679
  107.7 10.6 %collective-permute-start.17 = (f32[432,256]{1,0:T(8,128)S(1)}, f32[432,256]{1,0:T(8,128)S(1)}, u32[]{:S(2)}, u32[]{:S(2)}) collective-permute-start(f32[432,256]{1,0:T(8,128)S(1)} %get-tuple-element.58), channel_id=1, source_target_pairs={{0,2},{1,31},{2,4},{3,1},{4,6},{5,3},{6,8},{7,5},{8,10},{9,7},{10,... | collective-permute-start | bytes 1327112 | tf_op jit(solution)/shard_map/ppermute | solution.py:679
  107.7 10.5 %collective-permute-start.18 = (f32[432,256]{1,0:T(8,128)S(1)}, f32[432,256]{1,0:T(8,128)S(1)}, u32[]{:S(2)}, u32[]{:S(2)}) collective-permute-start(f32[432,256]{1,0:T(8,128)S(1)} %get-tuple-element.59), channel_id=1, source_target_pairs={{0,30},{1,3},{2,0},{3,5},{4,2},{5,7},{6,4},{7,9},{8,6},{9,11},{10,... | collective-permute-start | bytes 1327112 | tf_op jit(solution)/shard_map/ppermute | solution.py:682
  113.2 5.9 %copy-start.31 = (bf16[128,256]{1,0:T(8,128)(2,1)S(1)}, bf16[128,256]{1,0:T(8,128)(2,1)}, u32[]{:S(2)}) copy-start(bf16[128,256]{1,0:T(8,128)(2,1)} %constant.66.clone.depth_pick) | copy-start | bytes 196612
  113.2 5.9 %copy-start.34 = (bf16[64,144]{1,0:T(8,128)(2,1)S(1)}, bf16[64,144]{1,0:T(8,128)(2,1)}, u32[]{:S(2)}) copy-start(bf16[64,144]{1,0:T(8,128)(2,1)} %constant.67.clone.rows_pick) | copy-start | bytes 55300
  113.2 22.3 %collective-permute-start.21 = (f32[2,2,256,256]{3,2,1,0:T(8,128)}, f32[2,2,256,256]{3,2,1,0:T(8,128)}, u32[]{:S(2)}, u32[]{:S(2)}) collective-permute-start(f32[2,2,256,256]{3,2,1,0:T(8,128)} %pad_maximum_fusion.1), channel_id=1, source_target_pairs={{0,1},{1,0},{2,3},{3,2},{4,5},{5,4},{6,7},{7,6},{8,9},{9,8},{10,11... | collective-permute-start | bytes 3145736 | tf_op jit(solution)/shard_map/ppermute | solution.py:670
  119.8 6.4 %collective-permute-start.20 = (f32[1,144,128]{2,1,0:T(8,128)S(1)}, f32[1,144,128]{2,1,0:T(8,128)S(1)}, u32[]{:S(2)}, u32[]{:S(2)}) collective-permute-start(f32[1,144,128]{2,1,0:T(8,128)S(1)} %get-tuple-element.82), channel_id=1, source_target_pairs={{0,30},{1,3},{2,0},{3,5},{4,2},{5,7},{6,4},{7,9},{8,6},{9,11},{10,... | collective-permute-start | bytes 221192 | tf_op jit(solution)/shard_map/ppermute | solution.py:682
  124.2 6.5 %collective-permute-start.19 = (f32[1,144,128]{2,1,0:T(8,128)S(1)}, f32[1,144,128]{2,1,0:T(8,128)S(1)}, u32[]{:S(2)}, u32[]{:S(2)}) collective-permute-start(f32[1,144,128]{2,1,0:T(8,128)S(1)} %get-tuple-element.83), channel_id=1, source_target_pairs={{0,2},{1,31},{2,4},{3,1},{4,6},{5,3},{6,8},{7,5},{8,10},{9,7},{10,... | collective-permute-start | bytes 221192 | tf_op jit(solution)/shard_map/ppermute | solution.py:679
  131.3 21.5 %copy-start.33 = (bf16[128,128]{1,0:T(8,128)(2,1)S(1)}, bf16[128,128]{1,0:T(8,128)(2,1)}, u32[]{:S(2)}) copy-start(bf16[128,128]{1,0:T(8,128)(2,1)} %constant.68.clone.mid_depth) | copy-start | bytes 98308
  132.2 20.6 %all-to-all-start = ((f32[32,32,128]{2,1,0:T(8,128)}), f32[32,32,128]{2,1,0:T(8,128)}, u32[]{:S(2)}, u32[]{:S(2)}) async-start(f32[32,32,128]{2,1,0:T(8,128)} %broadcast_in_dim.3), calls=%async_computation | async-start | bytes 1048576 | tf_op jit(solution)/shard_map/all_to_all | solution.py:851
  135.5 22.5 %copy-start.9 = (f32[2,256,256]{2,1,0:T(8,128)S(1)}, f32[2,256,256]{2,1,0:T(8,128)}, u32[]{:S(2)}) copy-start(f32[2,256,256]{2,1,0:T(8,128)} %copy-done.8) | copy-start | bytes 1572868
  135.5 22.5 %copy-start.11 = (f32[2,256,256]{2,1,0:T(8,128)S(1)}, f32[2,256,256]{2,1,0:T(8,128)}, u32[]{:S(2)}) copy-start(f32[2,256,256]{2,1,0:T(8,128)} %copy-done.10) | copy-start | bytes 1572868
  137.6 20.5 %collective-permute-start.27 = (f32[2,256,256]{2,1,0:T(8,128)S(1)}, f32[2,256,256]{2,1,0:T(8,128)}, u32[]{:S(2)}, u32[]{:S(2)}) collective-permute-start(f32[2,256,256]{2,1,0:T(8,128)S(1)} %get-tuple-element.71.near_base.near_ref), channel_id=1, source_target_pairs={{0,30},{1,3},{2,0},{3,5},{4,2},{5,7},{6,4},{7,9},{8,6},{9,11},{10,... | collective-permute-start | bytes 1572872 | tf_op jit(solution)/shard_map/ppermute | solution.py:682
  141.8 16.2 %collective-permute-start.26 = (f32[2,256,256]{2,1,0:T(8,128)S(1)}, f32[2,256,256]{2,1,0:T(8,128)}, u32[]{:S(2)}, u32[]{:S(2)}) collective-permute-start(f32[2,256,256]{2,1,0:T(8,128)S(1)} %get-tuple-element.70.far_base.far_ref), channel_id=1, source_target_pairs={{0,2},{1,31},{2,4},{3,1},{4,6},{5,3},{6,8},{7,5},{8,10},{9,7},{10,... | collective-permute-start | bytes 1572872 | tf_op jit(solution)/shard_map/ppermute | solution.py:679
  141.8 5.6 %collective-permute-start.22 = (f32[2,128,128]{2,1,0:T(8,128)S(1)}, f32[2,128,128]{2,1,0:T(8,128)S(1)}, u32[]{:S(2)}, u32[]{:S(2)}) collective-permute-start(f32[2,128,128]{2,1,0:T(8,128)S(1)} %shard_map.258), channel_id=1, source_target_pairs={{0,1},{1,0},{2,3},{3,2},{4,5},{5,4},{6,7},{7,6},{8,9},{9,8},{10,11... | collective-permute-start | bytes 393224 | tf_op jit(solution)/shard_map/ppermute | solution.py:670
  147.4 10.6 %collective-permute-start.23 = (f32[2,2,128,128]{3,2,1,0:T(8,128)S(1)}, f32[2,2,128,128]{3,2,1,0:T(8,128)}, u32[]{:S(2)}, u32[]{:S(2)}) collective-permute-start(f32[2,2,128,128]{3,2,1,0:T(8,128)S(1)} %pad_maximum_fusion.2.own_mid), channel_id=1, source_target_pairs={{0,2},{1,31},{2,4},{3,1},{4,6},{5,3},{6,8},{7,5},{8,10},{9,7},{10,... | collective-permute-start | bytes 786440 | tf_op jit(solution)/shard_map/ppermute | solution.py:679
  148.2 7.3 %collective-permute-start.24 = (f32[2,128,128]{2,1,0:T(8,128)}, f32[2,128,128]{2,1,0:T(8,128)}, u32[]{:S(2)}, u32[]{:S(2)}) collective-permute-start(f32[2,128,128]{2,1,0:T(8,128)} %pad_maximum_fusion.5), channel_id=1, source_target_pairs={{0,30},{1,3},{2,0},{3,5},{4,2},{5,7},{6,4},{7,9},{8,6},{9,11},{10,... | collective-permute-start | bytes 393224 | tf_op jit(solution)/shard_map/ppermute | solution.py:682
  152.6 12.5 %collective-permute-start.25 = (f32[2,256,256]{2,1,0:T(8,128)S(1)}, f32[2,256,256]{2,1,0:T(8,128)}, u32[]{:S(2)}, u32[]{:S(2)}) collective-permute-start(f32[2,256,256]{2,1,0:T(8,128)S(1)} %get-tuple-element.70.far_base.far_ref), channel_id=1, source_target_pairs={{0,1},{1,0},{2,3},{3,2},{4,5},{5,4},{6,7},{7,6},{8,9},{9,8},{10,11... | collective-permute-start | bytes 1572872 | tf_op jit(solution)/shard_map/ppermute | solution.py:670
  155.4 9.7 %copy-start.5 = (f32[2,256,256]{2,1,0:T(8,128)S(1)}, f32[2,256,256]{2,1,0:T(8,128)}, u32[]{:S(2)}) copy-start(f32[2,256,256]{2,1,0:T(8,128)} %copy-done.4) | copy-start | bytes 1572868
  155.4 9.7 %copy-start.7 = (f32[2,256,256]{2,1,0:T(8,128)S(1)}, f32[2,256,256]{2,1,0:T(8,128)}, u32[]{:S(2)}) copy-start(f32[2,256,256]{2,1,0:T(8,128)} %copy-done.6) | copy-start | bytes 1572868
  155.4 9.7 %copy-start.13 = (bf16[256,256]{1,0:T(8,128)(2,1)S(1)}, bf16[256,256]{1,0:T(8,128)(2,1)}, u32[]{:S(2)}) copy-start(bf16[256,256]{1,0:T(8,128)(2,1)} %constant.62.clone.depth_low) | copy-start | bytes 393220
  155.4 9.7 %copy-start.15 = (bf16[256,256]{1,0:T(8,128)(2,1)S(1)}, bf16[256,256]{1,0:T(8,128)(2,1)}, u32[]{:S(2)}) copy-start(bf16[256,256]{1,0:T(8,128)(2,1)} %constant.61.clone.depth_high) | copy-start | bytes 393220
  155.4 9.7 %copy-start.16 = (bf16[512,256]{1,0:T(8,128)(2,1)S(1)}, bf16[512,256]{1,0:T(8,128)(2,1)}, u32[]{:S(2)}) copy-start(bf16[512,256]{1,0:T(8,128)(2,1)} %constant.74.clone.fine_rows) | copy-start | bytes 786436
  155.4 9.7 %copy-start.21 = (bf16[256,256]{1,0:T(8,128)(2,1)S(1)}, bf16[256,256]{1,0:T(8,128)(2,1)}, u32[]{:S(2)}) copy-start(bf16[256,256]{1,0:T(8,128)(2,1)} %constant.72.clone.diff_low) | copy-start | bytes 393220
  155.4 9.7 %copy-start.22 = (bf16[256,256]{1,0:T(8,128)(2,1)S(1)}, bf16[256,256]{1,0:T(8,128)(2,1)}, u32[]{:S(2)}) copy-start(bf16[256,256]{1,0:T(8,128)(2,1)} %constant.71.clone.diff_high) | copy-start | bytes 393220
  155.4 9.7 %copy-start.23 = (bf16[256,256]{1,0:T(8,128)(2,1)S(1)}, bf16[256,256]{1,0:T(8,128)(2,1)}, u32[]{:S(2)}) copy-start(bf16[256,256]{1,0:T(8,128)(2,1)} %constant.70.clone.sum_low) | copy-start | bytes 393220
  155.5 9.7 %copy-start.24 = (bf16[256,256]{1,0:T(8,128)(2,1)S(1)}, bf16[256,256]{1,0:T(8,128)(2,1)}, u32[]{:S(2)}) copy-start(bf16[256,256]{1,0:T(8,128)(2,1)} %constant.69.clone.sum_high) | copy-start | bytes 393220
  155.5 9.7 %copy-start.30 = (bf16[128,256]{1,0:T(8,128)(2,1)S(1)}, bf16[128,256]{1,0:T(8,128)(2,1)}, u32[]{:S(2)}) copy-start(bf16[128,256]{1,0:T(8,128)(2,1)} %constant.73.clone.fine_depth) | copy-start | bytes 196612
  159.5 17.2 %collective-permute-start.28 = (f32[2,256,256]{2,1,0:T(8,128)S(1)}, f32[2,256,256]{2,1,0:T(8,128)S(1)}, u32[]{:S(2)}, u32[]{:S(2)}) collective-permute-start(f32[2,256,256]{2,1,0:T(8,128)S(1)} %get-tuple-element.74), channel_id=1, source_target_pairs={{0,1},{1,0},{2,3},{3,2},{4,5},{5,4},{6,7},{7,6},{8,9},{9,8},{10,11... | collective-permute-start | bytes 1572872 | tf_op jit(solution)/shard_map/ppermute | solution.py:670
  (12 other events, 22.9 us)
